TPU v7x, 128 devices: a whole 4x4x4 slice. The times are simulated.
128 devices in a mesh: section: 4 (over y), tensor: 32 (over z, x, core).
Axes of the slice: x: 4, y: 4, z: 4, core: 2. Of those that a mesh axis runs over, the one named last changes fastest.
Arguments:
- token_ids: int32 [4, 128], replicated, may hold values from 0 to 64127
- embedding: bfloat16 [64128, 8192], P('section', 'tensor'), may hold values from -6 to 6
- norm_gain: float32 [4, 8192], P('section'), may hold values from 0.1 to 1.9
- query_weight: bfloat16 [4, 8192, 8192], P('section', None, 'tensor'), may hold values from -0.0625 to 0.0625
- keyval_weight: bfloat16 [4, 8192, 2048], P('section', None, 'tensor'), may hold values from -0.0625 to 0.0625
- output_weight: bfloat16 [4, 8192, 8192], P('section', 'tensor'), may hold values from -0.0625 to 0.0625
- prefix_cache: bfloat16 [4, 128, 128, 2, 1024], P('section', 'tensor')
- prefix_lengths: int32 [128], P('tensor'), may hold values from 16 to 128, as said below
Outputs:
- answers: float32 [4, 128, 8192], P('section', 'tensor')
Inputs may be any that keep to these rules, and one draw needn't show every extreme that they name: `prefix_lengths`: some row has exactly 128 live positions.
All inputs are finite; a program needn't handle non-finite values.
Results may differ from a plain program's by a relative error of at most 0.039.
Values may be sent and summed in bfloat16 or wider, within the bound.
No kernel may reach another device: no remote copies, remote signals or barrier semaphores. Data moves between devices by JAX's collectives and lax.ppermute only.
A program may use at most 128 MiB of HBM per device.

v0:
```python
import jax
import jax.numpy as jnp
from jax import lax
from jax.sharding import PartitionSpec as P

HEADS = 64
KVH = 8
HD = 128


NORM_EPSILON = 1e-05
ROPE_BASE = 500000.0


def passed_along(block, axis, distance):
    devices = range(lax.axis_size(axis))
    route = [(i - distance, i) for i in devices if i - distance in devices]
    return lax.ppermute(block, axis, route)


def rope_tables(positions, head_dim):
    half_dim = head_dim // 2
    frequency = ROPE_BASE ** (-(jnp.arange(half_dim, dtype=jnp.float32) * 2.0 / head_dim))
    angles = positions.astype(jnp.float32)[:, None] * frequency[None, :]
    cosine = jnp.concatenate([jnp.cos(angles), jnp.cos(angles)], axis=-1)
    sine_table = jnp.concatenate([jnp.sin(angles), jnp.sin(angles)], axis=-1)
    return (cosine, sine_table)


def rotate(vectors, cosine, sine_table):
    half_dim = vectors.shape[-1] // 2
    swapped = jnp.concatenate([-vectors[..., half_dim:], vectors[..., :half_dim]], axis=-1)
    return vectors * cosine[:, None, :] + swapped * sine_table[:, None, :]


def normalize(values, gain_vec):
    scaling = lax.rsqrt(jnp.mean(values * values, axis=-1, keepdims=True) + NORM_EPSILON)
    return (values * scaling * gain_vec).astype(jnp.bfloat16)


def attend(queries, prefix, fresh_rows, live_len, step_index):
    row_count, kv_heads, group_size, head_dim = queries.shape
    step_total = fresh_rows.shape[0]
    past_keys = prefix[:, :, 0, :].reshape(row_count, -1, kv_heads, head_dim)
    past_vals = prefix[:, :, 1, :].reshape(row_count, -1, kv_heads, head_dim)
    new_keys = fresh_rows[:, :, 0, :].reshape(step_total, row_count, kv_heads, head_dim)
    new_vals = fresh_rows[:, :, 1, :].reshape(step_total, row_count, kv_heads, head_dim)
    score_scale = head_dim ** (-0.5)
    past_score = (
        jnp.einsum("rkgd,rlkd->rkgl", queries, past_keys, preferred_element_type=jnp.float32)
        * score_scale
    )
    new_score = (
        jnp.einsum("rkgd,srkd->rkgs", queries, new_keys, preferred_element_type=jnp.float32)
        * score_scale
    )
    past_mask = jnp.arange(past_keys.shape[1])[None, None, None, :] < live_len[:, None, None, None]
    new_mask = jnp.arange(step_total)[None, None, None, :] <= step_index
    past_score = jnp.where(past_mask, past_score, -1e30)
    new_score = jnp.where(new_mask, new_score, -1e30)
    top_score = jnp.maximum(jnp.max(past_score, axis=-1), jnp.max(new_score, axis=-1))[..., None]
    past_weight = jnp.exp(past_score - top_score)
    new_weight = jnp.exp(new_score - top_score)
    weight_total = jnp.sum(past_weight, axis=-1, keepdims=True) + jnp.sum(
        new_weight, axis=-1, keepdims=True
    )
    past_prob = (past_weight / weight_total).astype(jnp.bfloat16)
    new_prob = (new_weight / weight_total).astype(jnp.bfloat16)
    attended = jnp.einsum(
        "rkgl,rlkd->rkgd", past_prob, past_vals, preferred_element_type=jnp.float32
    )
    attended = attended + jnp.einsum(
        "rkgs,srkd->rkgd", new_prob, new_vals, preferred_element_type=jnp.float32
    )
    return attended.astype(jnp.bfloat16).reshape(row_count, kv_heads * group_size * head_dim)


def body(
    token_ids,
    embedding,
    norm_gain,
    query_weight,
    keyval_weight,
    output_weight,
    prefix_cache,
    prefix_lengths,
):
    n_tensor = lax.axis_size("tensor")
    section_pos = lax.axis_index("section")
    tensor_pos = lax.axis_index("tensor")
    last_section = lax.axis_size("section") - 1
    step_count = token_ids.shape[0]
    vocab_part = embedding.shape[0]
    own_rows = prefix_lengths.shape[0]
    model_width = embedding.shape[1] * n_tensor
    kv_width = KVH * HD
    group_size = HEADS // KVH
    local_ids = token_ids - section_pos * vocab_part
    inside = (local_ids >= 0) & (local_ids < vocab_part)
    picked = jnp.take(embedding, jnp.clip(local_ids, 0, vocab_part - 1), axis=0)
    partial_embed = jnp.where(inside[:, :, None], picked.astype(jnp.float32), 0.0)
    columns = lax.psum(partial_embed.astype(jnp.bfloat16), "section")
    own_embed = lax.all_to_all(columns, "tensor", split_axis=1, concat_axis=2, tiled=True)
    block_count = 1
    block_rows = own_rows // block_count
    item_count = step_count * block_count
    tick_count = item_count + last_section
    gain_vec = norm_gain[0]
    query_mat = query_weight[0]
    keyval_mat = keyval_weight[0]
    output_mat = output_weight[0]
    cache_rows = prefix_cache[0]
    carried = jnp.zeros((block_rows, model_width), jnp.float32)
    fresh_kv = jnp.zeros((step_count, own_rows, 2, kv_width), jnp.bfloat16)
    finals = jnp.zeros((step_count, own_rows, model_width), jnp.float32)

    def advance(tick_index, carry_state):
        incoming, fresh_kv, finals = carry_state
        item_index = tick_index - section_pos
        is_valid = (item_index >= 0) & (item_index < item_count)
        item_index = jnp.clip(item_index, 0, item_count - 1)
        step_index = item_index // block_count
        row_start = item_index % block_count * block_rows
        step_embed = lax.dynamic_index_in_dim(own_embed, step_index, 0, keepdims=False)
        first_input = step_embed.astype(jnp.float32)
        hidden_in = jnp.where(section_pos == 0, first_input, incoming)
        normed = lax.all_gather(normalize(hidden_in, gain_vec), "tensor", axis=0, tiled=True)
        queries = jnp.dot(normed, query_mat, preferred_element_type=jnp.float32)
        keyvals = jnp.dot(normed, keyval_mat, preferred_element_type=jnp.float32)
        queries, keyvals = (
            lax.all_to_all(queries, "tensor", split_axis=0, concat_axis=1, tiled=True),
            lax.all_to_all(keyvals, "tensor", split_axis=0, concat_axis=1, tiled=True),
        )
        cosine, sine_table = rope_tables(prefix_lengths + step_index, HD)
        turned_q = rotate(queries.reshape(block_rows, HEADS, HD), cosine, sine_table).astype(
            jnp.bfloat16
        )
        turned_k = rotate(
            keyvals[:, :kv_width].reshape(block_rows, KVH, HD), cosine, sine_table
        ).astype(jnp.bfloat16)
        value_cols = keyvals[:, kv_width:].astype(jnp.bfloat16)
        entry_kv = jnp.stack([turned_k.reshape(block_rows, kv_width), value_cols], axis=1)
        current = lax.dynamic_slice(
            fresh_kv, (step_index, row_start, 0, 0), (1, block_rows, 2, kv_width)
        )
        fresh_kv = lax.dynamic_update_slice(
            fresh_kv, jnp.where(is_valid, entry_kv[None], current), (step_index, row_start, 0, 0)
        )
        mixed_out = attend(
            turned_q.reshape(block_rows, KVH, group_size, HD),
            cache_rows,
            fresh_kv,
            prefix_lengths,
            step_index,
        )
        head_cols = lax.all_to_all(mixed_out, "tensor", split_axis=1, concat_axis=0, tiled=True)
        partial_value = (
            jnp.dot(head_cols, output_mat, preferred_element_type=jnp.float32)
            .astype(jnp.bfloat16)
            .astype(jnp.float32)
        )
        summed_all = lax.psum(partial_value.astype(jnp.bfloat16), "tensor").astype(jnp.float32)
        summed = lax.dynamic_slice_in_dim(summed_all, tensor_pos * block_rows, block_rows, 0)
        hidden_out = hidden_in + summed
        write_final = is_valid & (section_pos == last_section)
        current_final = lax.dynamic_slice(
            finals, (step_index, row_start, 0), (1, block_rows, model_width)
        )
        finals = lax.dynamic_update_slice(
            finals,
            jnp.where(write_final, hidden_out[None], current_final),
            (step_index, row_start, 0),
        )
        outgoing = passed_along(hidden_out, "section", 1)
        return (outgoing, fresh_kv, finals)

    spent, fresh_kv, finals = lax.fori_loop(0, tick_count, advance, (carried, fresh_kv, finals))
    answers = lax.psum_scatter(finals, "section", scatter_dimension=0, tiled=True)
    return answers


def solution(mesh):
    in_specs = (
        P(),
        P("section", "tensor"),
        P("section", None),
        P("section", None, "tensor"),
        P("section", None, "tensor"),
        P("section", "tensor", None),
        P("section", "tensor", None, None, None),
        P("tensor"),
    )
    out_specs = P("section", "tensor", None)
    return jax.shard_map(body, mesh=mesh, in_specs=in_specs, out_specs=out_specs, check_vma=False)
```

profile of v0, /device:TPU:0, one launch (start us, length us, event | category | flops | bytes accessed | tf_op | source)
XLA Modules:
  0.0 1589.0 jit_solution(3336385134684504714)
XLA Ops:
  8.2 5.9 gather_fusion
  15.2 44.3 %all-reduce.5.cloned.1.call-done = bf16[4,128,256]{2,0,1:T(4,128)(2,1)} async-done(((bf16[4,128,256]{2,0,1:T(4,128)(2,1)}), bf16[4,128,256]{2,0,1:T(4,128)(2,1)}) %all-reduce.5.cloned.1.call-update) | async-done | bytes 262160 | tf_op jit(solution)/shard_map/psum | solution.py:102
  59.5 7.2 all-to-all-start.3
  76.9 1456.6 %while.19 = (s32[]{:T(128)}, f32[4,8192]{1,0:T(4,128)S(1)}, bf16[4,4,2,1024]{3,1,2,0:T(4,128)(2,1)S(1)}, f32[4,4,8192]{2,1,0:T(4,128)}, pred[]{:T(512)}, /*index...) while((s32[]{:T(128)}, f32[4,8192]{1,0:T(4,128)S(1)}, ...), condition=%wide.region_8.9_spmd, body=%wide.region_1.8_spmd.sunk | while | flops 1228397952 | bytes 74761704 | solution.py:177
  81.3 41.5 %all-gather.5.cloned.1.call-done = bf16[32,4,8192]{2,1,0:T(4,128)(2,1)} async-done(((bf16[1,4,8192]{2,1,0:T(4,128)(2,1)}), bf16[32,4,8192]{2,1,0:T(4,128)(2,1)}) %all-gather.5.cloned.1.call-update) | async-done | bytes 2097168 | tf_op jit(solution)/shard_map/while/body/eval_jaxpr/all_gather | solution.py:127
  147.3 5.3 all-to-all-done
  155.0 11.0 all_to_all.139
  170.3 105.2 %all-reduce.9.cloned.1.call-done = bf16[128,8192]{1,0:T(8,128)(2,1)} async-done(((bf16[128,8192]{1,0:T(8,128)(2,1)}), bf16[128,8192]{1,0:T(8,128)(2,1)}) %all-reduce.9.cloned.1.call-update) | async-done | bytes 2097168 | tf_op jit(solution)/shard_map/while/body/eval_jaxpr/psum | solution.py:162
  287.8 43.3 %all-gather.5.cloned.1.call-done = bf16[32,4,8192]{2,1,0:T(4,128)(2,1)} async-done(((bf16[1,4,8192]{2,1,0:T(4,128)(2,1)}), bf16[32,4,8192]{2,1,0:T(4,128)(2,1)}) %all-gather.5.cloned.1.call-update) | async-done | bytes 2097168 | tf_op jit(solution)/shard_map/while/body/eval_jaxpr/all_gather | solution.py:127
  355.7 5.3 all-to-all-done
  363.3 11.0 all_to_all.139
  378.6 105.2 %all-reduce.9.cloned.1.call-done = bf16[128,8192]{1,0:T(8,128)(2,1)} async-done(((bf16[128,8192]{1,0:T(8,128)(2,1)}), bf16[128,8192]{1,0:T(8,128)(2,1)}) %all-reduce.9.cloned.1.call-update) | async-done | bytes 2097168 | tf_op jit(solution)/shard_map/while/body/eval_jaxpr/psum | solution.py:162
  496.1 43.3 %all-gather.5.cloned.1.call-done = bf16[32,4,8192]{2,1,0:T(4,128)(2,1)} async-done(((bf16[1,4,8192]{2,1,0:T(4,128)(2,1)}), bf16[32,4,8192]{2,1,0:T(4,128)(2,1)}) %all-gather.5.cloned.1.call-update) | async-done | bytes 2097168 | tf_op jit(solution)/shard_map/while/body/eval_jaxpr/all_gather | solution.py:127
  564.0 5.3 all-to-all-done
  571.6 11.0 all_to_all.139
  586.9 105.2 %all-reduce.9.cloned.1.call-done = bf16[128,8192]{1,0:T(8,128)(2,1)} async-done(((bf16[128,8192]{1,0:T(8,128)(2,1)}), bf16[128,8192]{1,0:T(8,128)(2,1)}) %all-reduce.9.cloned.1.call-update) | async-done | bytes 2097168 | tf_op jit(solution)/shard_map/while/body/eval_jaxpr/psum | solution.py:162
  704.4 43.7 %all-gather.5.cloned.1.call-done = bf16[32,4,8192]{2,1,0:T(4,128)(2,1)} async-done(((bf16[1,4,8192]{2,1,0:T(4,128)(2,1)}), bf16[32,4,8192]{2,1,0:T(4,128)(2,1)}) %all-gather.5.cloned.1.call-update) | async-done | bytes 2097168 | tf_op jit(solution)/shard_map/while/body/eval_jaxpr/all_gather | solution.py:127
  772.6 5.3 all-to-all-done
  780.2 11.0 all_to_all.139
  795.5 105.2 %all-reduce.9.cloned.1.call-done = bf16[128,8192]{1,0:T(8,128)(2,1)} async-done(((bf16[128,8192]{1,0:T(8,128)(2,1)}), bf16[128,8192]{1,0:T(8,128)(2,1)}) %all-reduce.9.cloned.1.call-update) | async-done | bytes 2097168 | tf_op jit(solution)/shard_map/while/body/eval_jaxpr/psum | solution.py:162
  913.0 43.4 %all-gather.5.cloned.1.call-done = bf16[32,4,8192]{2,1,0:T(4,128)(2,1)} async-done(((bf16[1,4,8192]{2,1,0:T(4,128)(2,1)}), bf16[32,4,8192]{2,1,0:T(4,128)(2,1)}) %all-gather.5.cloned.1.call-update) | async-done | bytes 2097168 | tf_op jit(solution)/shard_map/while/body/eval_jaxpr/all_gather | solution.py:127
  980.9 5.3 all-to-all-done
  988.5 11.0 all_to_all.139
  1003.8 105.2 %all-reduce.9.cloned.1.call-done = bf16[128,8192]{1,0:T(8,128)(2,1)} async-done(((bf16[128,8192]{1,0:T(8,128)(2,1)}), bf16[128,8192]{1,0:T(8,128)(2,1)}) %all-reduce.9.cloned.1.call-update) | async-done | bytes 2097168 | tf_op jit(solution)/shard_map/while/body/eval_jaxpr/psum | solution.py:162
  1121.3 43.3 %all-gather.5.cloned.1.call-done = bf16[32,4,8192]{2,1,0:T(4,128)(2,1)} async-done(((bf16[1,4,8192]{2,1,0:T(4,128)(2,1)}), bf16[32,4,8192]{2,1,0:T(4,128)(2,1)}) %all-gather.5.cloned.1.call-update) | async-done | bytes 2097168 | tf_op jit(solution)/shard_map/while/body/eval_jaxpr/all_gather | solution.py:127
  1196.8 11.0 all_to_all.139
  1212.1 105.2 %all-reduce.9.cloned.1.call-done = bf16[128,8192]{1,0:T(8,128)(2,1)} async-done(((bf16[128,8192]{1,0:T(8,128)(2,1)}), bf16[128,8192]{1,0:T(8,128)(2,1)}) %all-reduce.9.cloned.1.call-update) | async-done | bytes 2097168 | tf_op jit(solution)/shard_map/while/body/eval_jaxpr/psum | solution.py:162
  1329.6 43.3 %all-gather.5.cloned.1.call-done = bf16[32,4,8192]{2,1,0:T(4,128)(2,1)} async-done(((bf16[1,4,8192]{2,1,0:T(4,128)(2,1)}), bf16[32,4,8192]{2,1,0:T(4,128)(2,1)}) %all-gather.5.cloned.1.call-update) | async-done | bytes 2097168 | tf_op jit(solution)/shard_map/while/body/eval_jaxpr/all_gather | solution.py:127
  1397.5 5.3 all-to-all-done
  1405.1 11.0 all_to_all.139
  1420.4 105.3 %all-reduce.9.cloned.1.call-done = bf16[128,8192]{1,0:T(8,128)(2,1)} async-done(((bf16[128,8192]{1,0:T(8,128)(2,1)}), bf16[128,8192]{1,0:T(8,128)(2,1)}) %all-reduce.9.cloned.1.call-update) | async-done | bytes 2097168 | tf_op jit(solution)/shard_map/while/body/eval_jaxpr/psum | solution.py:162
  1535.3 44.9 %all-reduce.7.cloned.1.call-done = f32[4,4,8192]{2,1,0:T(4,128)} async-done(((f32[4,4,8192]{2,1,0:T(4,128)}), f32[4,4,8192]{2,1,0:T(4,128)}) %all-reduce.7.cloned.1.call-update) | async-done | bytes 524304
  (587 shorter events, 323.7 us)
Async XLA Ops:
  6.5 53.0 %all-reduce.5.cloned.1.call-start = ((), (), s32[]{:S(2)}) async-start(), calls=%async_computation.4 | async-start | bytes 524288 | tf_op jit(solution)/shard_map/psum | solution.py:102
  59.5 16.1 %all-to-all-start.3 = ((bf16[4,128,256]{2,0,1:T(4,128)(2,1)}), bf16[4,128,256]{2,0,1:T(4,128)(2,1)S(1)}, u32[]{:S(2)}, u32[]{:S(2)}) async-start(bf16[4,128,256]{2,0,1:T(4,128)(2,1)} %all-reduce.5.cloned.1.call-done), calls=%async_computation.3 | async-start | bytes 524288 | tf_op jit(solution)/shard_map/all_to_all | solution.py:103
  76.9 45.9 %all-gather.5.cloned.1.call-start = ((), (), s32[]{:S(2)}) async-start(), calls=%async_computation.6 | async-start | bytes 2162688 | tf_op jit(solution)/shard_map/while/body/eval_jaxpr/all_gather | solution.py:127
  128.3 12.6 all-to-all-start.1
  141.0 11.7 all-to-all-start
  144.9 130.6 %all-reduce.9.cloned.1.call-start = ((), (), s32[]{:S(2)}) async-start(), calls=%async_computation.7 | async-start | bytes 4194304 | tf_op jit(solution)/shard_map/while/body/eval_jaxpr/psum | solution.py:162
  283.4 47.8 %all-gather.5.cloned.1.call-start = ((), (), s32[]{:S(2)}) async-start(), calls=%async_computation.6 | async-start | bytes 2162688 | tf_op jit(solution)/shard_map/while/body/eval_jaxpr/all_gather | solution.py:127
  336.7 12.6 all-to-all-start.1
  349.3 11.7 all-to-all-start
  353.2 130.6 %all-reduce.9.cloned.1.call-start = ((), (), s32[]{:S(2)}) async-start(), calls=%async_computation.7 | async-start | bytes 4194304 | tf_op jit(solution)/shard_map/while/body/eval_jaxpr/psum | solution.py:162
  485.5 6.1 collective-permute-start
  491.7 47.8 %all-gather.5.cloned.1.call-start = ((), (), s32[]{:S(2)}) async-start(), calls=%async_computation.6 | async-start | bytes 2162688 | tf_op jit(solution)/shard_map/while/body/eval_jaxpr/all_gather | solution.py:127
  545.0 12.6 all-to-all-start.1
  557.6 11.7 all-to-all-start
  561.5 130.6 %all-reduce.9.cloned.1.call-start = ((), (), s32[]{:S(2)}) async-start(), calls=%async_computation.7 | async-start | bytes 4194304 | tf_op jit(solution)/shard_map/while/body/eval_jaxpr/psum | solution.py:162
  700.0 48.1 %all-gather.5.cloned.1.call-start = ((), (), s32[]{:S(2)}) async-start(), calls=%async_computation.6 | async-start | bytes 2162688 | tf_op jit(solution)/shard_map/while/body/eval_jaxpr/all_gather | solution.py:127
  753.6 12.6 all-to-all-start.1
  766.2 11.7 all-to-all-start
  770.1 130.6 %all-reduce.9.cloned.1.call-start = ((), (), s32[]{:S(2)}) async-start(), calls=%async_computation.7 | async-start | bytes 4194304 | tf_op jit(solution)/shard_map/while/body/eval_jaxpr/psum | solution.py:162
  908.6 47.8 %all-gather.5.cloned.1.call-start = ((), (), s32[]{:S(2)}) async-start(), calls=%async_computation.6 | async-start | bytes 2162688 | tf_op jit(solution)/shard_map/while/body/eval_jaxpr/all_gather | solution.py:127
  961.9 12.6 all-to-all-start.1
  974.5 11.7 all-to-all-start
  978.4 130.6 %all-reduce.9.cloned.1.call-start = ((), (), s32[]{:S(2)}) async-start(), calls=%async_computation.7 | async-start | bytes 4194304 | tf_op jit(solution)/shard_map/while/body/eval_jaxpr/psum | solution.py:162
  1116.9 47.8 %all-gather.5.cloned.1.call-start = ((), (), s32[]{:S(2)}) async-start(), calls=%async_computation.6 | async-start | bytes 2162688 | tf_op jit(solution)/shard_map/while/body/eval_jaxpr/all_gather | solution.py:127
  1170.2 12.6 all-to-all-start.1
  1182.8 11.7 all-to-all-start
  1186.7 130.6 %all-reduce.9.cloned.1.call-start = ((), (), s32[]{:S(2)}) async-start(), calls=%async_computation.7 | async-start | bytes 4194304 | tf_op jit(solution)/shard_map/while/body/eval_jaxpr/psum | solution.py:162
  1325.2 47.8 %all-gather.5.cloned.1.call-start = ((), (), s32[]{:S(2)}) async-start(), calls=%async_computation.6 | async-start | bytes 2162688 | tf_op jit(solution)/shard_map/while/body/eval_jaxpr/all_gather | solution.py:127
  1378.5 12.6 all-to-all-start.1
  1391.2 11.7 all-to-all-start
  1395.0 130.6 %all-reduce.9.cloned.1.call-start = ((), (), s32[]{:S(2)}) async-start(), calls=%async_computation.7 | async-start | bytes 4194304 | tf_op jit(solution)/shard_map/while/body/eval_jaxpr/psum | solution.py:162
  1533.5 46.7 %all-reduce.7.cloned.1.call-start = ((), (), s32[]{:S(2)}) async-start(), calls=%async_computation.5 | async-start | bytes 1048576
  (86 other events, 3070.7 us)
Sparse Core Ops, SparseCore 0:
  15.4 44.1 all-reduce.4
  80.3 42.4 all-gather.4
  170.4 105.0 all-reduce.8
  286.4 44.6 all-gather.4
  378.7 105.0 all-reduce.8
  494.7 44.6 all-gather.4
  587.0 105.0 all-reduce.8
  703.3 44.6 all-gather.4
  795.6 105.0 all-reduce.8
  911.6 44.6 all-gather.4
  1003.9 105.0 all-reduce.8
  1119.9 44.6 all-gather.4
  1212.2 105.0 all-reduce.8
  1328.2 44.6 all-gather.4
  1420.5 105.0 all-reduce.8
  1536.5 43.7 all-reduce.6
where the time goes:
time: 1590 us
  waiting for transfers between devices  1210 us (76%)
  starting transfers between devices  95.2 us (6%)
  matrix products  77.1 us (5%)
  blocking collectives  76.7 us (5%)
  local copies, waits for them, and re-layouts  60.2 us (4%)
  other arithmetic  50.7 us (3%)
    psum x7, waiting for transfers between devices, advance(): lax.psum(partial_value.astype(jnp.bfloat16), 'tensor').astype(jnp.float32)  737 us
    all_gather x7, waiting for transfers between devices, advance(): lax.all_gather(normalize(hidden_in, gain_vec), 'tensor', axis=0, tiled=True)  302 us
    all_to_all x7, blocking collectives, advance(): lax.all_to_all(mixed_out, 'tensor', split_axis=1, concat_axis=0, tiled=True)  76.7 us
    unnamed x3, waiting for transfers between devices  45.4 us
    psum x1, waiting for transfers between devices, body(): columns = lax.psum(partial_embed.astype(jnp.bfloat16), 'section')  44.3 us
    all_to_all x7, waiting for transfers between devices, advance(): lax.all_to_all(queries, 'tensor', split_axis=0, concat_axis=1, tiled=True)  37.2 us
    all_to_all x7, starting transfers between devices, advance(): lax.all_to_all(keyvals, 'tensor', split_axis=0, concat_axis=1, tiled=True)  36.6 us
  transfers between devices with their start and end apart: 38, of which 38 were waited for; matrix products, arithmetic and copies ran while one was open for 4% of the time, Pallas kernels for 0%

commit v1 on v0

v1 whole, which is shorter than its diff:
```python
import jax
import jax.numpy as jnp
from jax import lax
from jax.sharding import PartitionSpec as P

HD = 128
NORM_EPSILON = 1e-05
ROPE_BASE = 500000.0
SECTIONS = 4
CHIPS = 16
CORES = 2
STEPS = 4
HEADS_PER_CHIP = 4
BF16 = jnp.bfloat16
F32 = jnp.float32
PLANE = [[2 * p + c for p in range(CHIPS)] for c in range(CORES)]


def section_send(block, distance):
    if distance == 0:
        return block
    route = [(i, (i + distance) % SECTIONS) for i in range(SECTIONS)]
    return lax.ppermute(block, "section", route)


def core_swap(block):
    return lax.ppermute(block, "tensor", [(i, i ^ 1) for i in range(CHIPS * CORES)])


def chip_send(block, target):
    route = [(2 * p + c, 2 * target(p) + c) for p in range(CHIPS) for c in range(CORES)]
    return lax.ppermute(block, "tensor", route)


def plane_exchange(blocks):
    return lax.all_to_all(
        blocks, "tensor", split_axis=0, concat_axis=0, tiled=True, axis_index_groups=PLANE
    )


def section_exchange(blocks):
    return lax.all_to_all(blocks, "section", split_axis=0, concat_axis=0, tiled=True)


def embed(token_ids, embedding, section_pos):
    vocab_part = embedding.shape[0]
    local_ids = token_ids.T.reshape(-1) - section_pos * vocab_part
    inside = (local_ids >= 0) & (local_ids < vocab_part)
    picked = jnp.take(embedding, jnp.clip(local_ids, 0, vocab_part - 1), axis=0)
    picked = jnp.where(inside[:, None], picked, jnp.zeros_like(picked))
    by_row = lax.all_to_all(
        picked.reshape(CHIPS * CORES, 16, -1), "tensor", split_axis=0, concat_axis=0, tiled=True
    )
    by_quarter = section_exchange(by_row).reshape(SECTIONS, 8, 16, -1)
    columns = jnp.sum(by_quarter.astype(F32), axis=0)
    return columns.transpose(1, 0, 2).reshape(16, -1)


def row_order(section_pos):
    place = jnp.arange(256)[:, None]
    source = jnp.arange(256)[None, :]
    turn, chip, step = place // 64, place // 4 % CHIPS, place % 4
    wanted = chip * 16 + (section_pos + turn) % SECTIONS * 4 + step
    forward = (wanted == source).astype(BF16)
    turn, chip, step = source // 64, source // 4 % CHIPS, source % 4
    held = chip * 16 + (section_pos - turn) % SECTIONS * 4 + step
    backward = (held == place).astype(BF16)
    return forward, backward


def project(rows, order, inverse_gain, weights):
    wq_mine, wq_other, keys_t, values_t = weights
    rows = jnp.dot(order, rows, preferred_element_type=F32).astype(BF16)
    plain = rows.astype(F32) * inverse_gain
    squares = jnp.sum(plain * plain, axis=-1, keepdims=True)
    transposed = (((1,), (1,)), ((), ()))
    parts = [
        jnp.dot(rows, wq_mine, preferred_element_type=F32),
        jnp.dot(rows, wq_other, preferred_element_type=F32),
        lax.dot_general(rows, keys_t, transposed, preferred_element_type=F32),
        lax.dot_general(rows, values_t, transposed, preferred_element_type=F32),
        jnp.broadcast_to(squares, (256, HD)),
    ]
    return jnp.concatenate(parts, axis=1)


def turn(vectors, cosine, sine):
    half = HD // 2
    swapped = jnp.concatenate([-vectors[..., half:], vectors[..., :half]], axis=-1)
    return vectors * cosine + swapped * sine


def attend(parts, cosine, sine, cache, lengths):
    total = (parts[0] + parts[1]) + (parts[2] + parts[3])
    width = HEADS_PER_CHIP * HD
    squares = total[:, width + 2 * HD : width + 2 * HD + 1]
    scaling = lax.rsqrt(squares / 8192.0 + NORM_EPSILON)
    total = total * scaling
    heads = [total[:, i * HD : (i + 1) * HD] for i in range(HEADS_PER_CHIP)]
    queries = jnp.concatenate([turn(h, cosine, sine) for h in heads], axis=0).astype(BF16)
    new_keys = turn(total[:, width : width + HD], cosine, sine).astype(BF16)
    new_values = total[:, width + HD : width + 2 * HD].astype(BF16)
    keys = cache[:, 0].reshape(-1, HD)
    values = cache[:, 1].reshape(-1, HD)
    transposed = (((1,), (1,)), ((), ()))
    scale = HD**-0.5
    past = lax.dot_general(queries, keys, transposed, preferred_element_type=F32) * scale
    new = lax.dot_general(queries, new_keys, transposed, preferred_element_type=F32) * scale
    row = jnp.arange(256)[:, None] % 64
    column = jnp.arange(past.shape[1])[None, :]
    live = lengths[:, None].repeat(HD, 1).reshape(1, -1)
    past_live = (row // 4 == column // 128) & (column % 128 < live)
    column = jnp.arange(64)[None, :]
    new_live = (row // 4 == column // 4) & (column % 4 <= row % 4)
    past = jnp.where(past_live, past, -1e30)
    new = jnp.where(new_live, new, -1e30)
    top = jnp.maximum(jnp.max(past, -1, keepdims=True), jnp.max(new, -1, keepdims=True))
    past = jnp.exp(past - top)
    new = jnp.exp(new - top)
    weight = jnp.sum(past, -1, keepdims=True) + jnp.sum(new, -1, keepdims=True)
    past = (past / weight).astype(BF16)
    new = (new / weight).astype(BF16)
    mixed = jnp.dot(past, values, preferred_element_type=F32)
    mixed = mixed + jnp.dot(new, new_values, preferred_element_type=F32)
    mixed = mixed.astype(BF16)
    return jnp.concatenate([mixed[i * 64 : (i + 1) * 64] for i in range(HEADS_PER_CHIP)], axis=1)


def body(
    token_ids,
    embedding,
    norm_gain,
    query_weight,
    keyval_weight,
    output_weight,
    prefix_cache,
    prefix_lengths,
):
    section_pos = lax.axis_index("section")
    tensor_pos = lax.axis_index("tensor")
    core, chip = tensor_pos % CORES, tensor_pos // CORES
    quarter = query_weight.shape[1] // SECTIONS

    def share(weight, axis, distance):
        start = (section_pos + distance) % SECTIONS * quarter
        return section_send(lax.dynamic_slice_in_dim(weight, start, quarter, axis), distance)

    kv_mat = keyval_weight[0].T
    wq_mine = [share(query_weight[0], 0, d) for d in range(SECTIONS)]
    kv_mine = jnp.stack([share(kv_mat, 1, d) for d in range(SECTIONS)])
    wo_mine = [share(output_weight[0], 1, d) for d in range(SECTIONS)]
    wq_other = jnp.stack([core_swap(w) for w in wq_mine])
    wo_other = jnp.stack([core_swap(w) for w in wo_mine])
    wq_mine = jnp.stack(wq_mine)
    wo_mine = jnp.stack(wo_mine)
    first = chip_send(kv_mine, lambda p: 2 * p if p < 8 else 2 * (p - 8) + 1)
    second = chip_send(kv_mine, lambda p: 2 * p + 1 if p < 8 else 2 * (p - 8))
    even = chip % 2 == 0
    heads_t = []
    for half in (jnp.where(even, first, second), jnp.where(even, second, first)):
        other = core_swap(half)
        low = jnp.where(core == 0, half, other)
        high = jnp.where(core == 0, other, half)
        heads_t.append(jnp.concatenate([low, high], axis=1))
    keys_t, values_t = heads_t

    gains = section_exchange(norm_gain[0].reshape(SECTIONS, quarter))
    hidden = embed(token_ids, embedding, section_pos)

    lengths = lax.all_gather(prefix_lengths, "tensor", axis=0, axis_index_groups=PLANE)
    lengths = lax.dynamic_index_in_dim(lengths, section_pos, 1, keepdims=False)
    cache = section_exchange(prefix_cache[0])
    cache = cache.reshape(SECTIONS, 128, 2, 8, HD).transpose(3, 0, 2, 1, 4)
    cache = plane_exchange(jnp.repeat(cache, 2, axis=0))

    frequency = ROPE_BASE ** (-(jnp.arange(HD // 2, dtype=F32) * 2.0 / HD))
    positions = (lengths[:, None] + jnp.arange(STEPS)[None, :]).reshape(-1).astype(F32)
    angles = positions[:, None] * frequency[None, :]
    cosine = jnp.concatenate([jnp.cos(angles)] * 2, axis=-1)
    sine = jnp.concatenate([jnp.sin(angles)] * 2, axis=-1)
    forward, backward = row_order(section_pos)

    for layer in range(SECTIONS):
        slot = (section_pos - layer) % SECTIONS
        pick = lambda stacked: lax.dynamic_index_in_dim(stacked, slot, 0, keepdims=False)
        gain = gains[layer][None, :]
        scaled = (hidden * gain).astype(BF16)
        rows = plane_exchange(jnp.broadcast_to(scaled[None], (CHIPS, 16, quarter)))
        weights = [pick(w) for w in (wq_mine, wq_other, keys_t, values_t)]
        partial = project(rows.reshape(256, quarter), forward, 1.0 / gain, weights)
        parts = [section_send(partial[64 * d : 64 * (d + 1)], d) for d in range(SECTIONS)]
        mixed = attend(parts, cosine, sine, cache[:, layer], lengths)
        gathered = jnp.concatenate([section_send(mixed, d) for d in range(SECTIONS)], axis=0)
        gathered = jnp.dot(backward, gathered, preferred_element_type=F32).astype(BF16)
        out_mat = jnp.concatenate([pick(wo_mine), pick(wo_other)], axis=0)
        terms = jnp.dot(gathered, out_mat, preferred_element_type=F32).astype(BF16)
        terms = plane_exchange(terms.reshape(CHIPS, 16, quarter))
        hidden = hidden + jnp.sum(terms.astype(F32), axis=0)

    finals = section_exchange(hidden.reshape(4, STEPS, quarter).transpose(1, 0, 2))
    return finals.transpose(1, 0, 2).reshape(1, 4, SECTIONS * quarter)


def solution(mesh):
    in_specs = (
        P(),
        P("section", "tensor"),
        P("section", None),
        P("section", None, "tensor"),
        P("section", None, "tensor"),
        P("section", "tensor", None),
        P("section", "tensor", None, None, None),
        P("tensor"),
    )
    out_specs = P("section", "tensor", None)
    return jax.shard_map(body, mesh=mesh, in_specs=in_specs, out_specs=out_specs, check_vma=False)
```

time: 1590 us -> 538 us (0.34)
  waiting for transfers between devices: 1210 us -> 196 us
  matrix products: 77.1 us -> 44.5 us
  starting transfers between devices: 95.2 us -> 123 us
  other arithmetic: 50.7 us -> 28.2 us
    psum x8 -> x0, waiting for transfers between devices: 781 us -> none  [the longest x7 737 us: advance(): lax.psum(partial_value.astype(jnp.bfloat16), 'tensor').astype(jnp.float32)]
    all_gather x7 -> x0, waiting for transfers between devices: 302 us -> none  [advance(): lax.all_gather(normalize(hidden_in, gain_vec), 'tensor', axis=0, tiled=True)]
    ppermute x7 -> x45, waiting for transfers between devices: 19.2 us -> 105 us  [the longest x33 105 us: section_send(): return lax.ppermute(block, 'section', route)]
    ppermute x7 -> x45, starting transfers between devices: 23.7 us -> 77.5 us  [the longest x33 64.5 us: section_send(): return lax.ppermute(block, 'section', route)]
    unnamed x3 -> x0, waiting for transfers between devices: 45.4 us -> none
    dot_general x49 -> x40, matrix products: 77.1 us -> 44.5 us  [the longest x4 12.3 us: body(): terms = jnp.dot(gathered, out_mat, preferred_element_type=F32).astype(BF16)]
    all_to_all x15 -> x10, starting transfers between devices: 70.9 us -> 45.2 us  [the longest x6 26.9 us: plane_exchange(): lax.all_to_all(blocks, 'tensor', split_axis=0, concat_axis=0, tiled=True,...]
    all_to_all x15 -> x10, waiting for transfers between devices: 65.6 us -> 90.2 us  [the longest x6 68.6 us: plane_exchange(): lax.all_to_all(blocks, 'tensor', split_axis=0, concat_axis=0, tiled=True,...]
  transfers between devices with their start and end apart: 38 -> 55, of which waited for: 38 -> 30; matrix products, arithmetic and copies ran while one was open for 4% -> 12% of each run, Pallas kernels for 0% -> 0%
where the time goes in v1:
time: 538 us; the launch traced here: 527 us
  waiting for transfers between devices  196 us (36%)
  starting transfers between devices  123 us (23%)
  blocking collectives  80.6 us (15%)
  local copies, waits for them, and re-layouts  53.1 us (10%)
  matrix products  44.5 us (8%)
  other arithmetic  28.2 us (5%)
    ppermute x33, waiting for transfers between devices, section_send(): return lax.ppermute(block, 'section', route)  105 us
    all_to_all x6, waiting for transfers between devices, plane_exchange(): lax.all_to_all(blocks, 'tensor', split_axis=0, concat_axis=0, tiled=True,...  68.6 us
    ppermute x33, starting transfers between devices, section_send(): return lax.ppermute(block, 'section', route)  64.5 us
    all_to_all x3, blocking collectives, plane_exchange(): lax.all_to_all(blocks, 'tensor', split_axis=0, concat_axis=0, tiled=True,...  54.4 us
    all_to_all x6, starting transfers between devices, plane_exchange(): lax.all_to_all(blocks, 'tensor', split_axis=0, concat_axis=0, tiled=True,...  26.9 us
    unnamed x1, blocking collectives  17.8 us
    all_to_all x3, waiting for transfers between devices, section_exchange(): lax.all_to_all(blocks, 'section', split_axis=0, concat_axis=0, tiled=True)  17.6 us
    all_to_all x3, starting transfers between devices, section_exchange(): lax.all_to_all(blocks, 'section', split_axis=0, concat_axis=0, tiled=True)  13.7 us
  transfers between devices with their start and end apart: 55, of which 30 were waited for; matrix products, arithmetic and copies ran while one was open for 12% of the time, Pallas kernels for 0%

profile of v1, /device:TPU:0, one launch (start us, length us, event | category | flops | bytes accessed | tf_op | source)
XLA Modules:
  0.0 527.2 jit_solution(1688956902040601119)
XLA Ops:
  0.0 4.5 all-to-all-start.2
  21.4 17.8 %all-reduce.1 = s32[16,4]{1,0:T(8,128)S(1)} all-reduce(s32[16,4]{1,0:T(8,128)S(1)} %reshape.792), channel_id=2, replica_groups={{0,2,4,6,8,10,12,14,16,18,20,22,24,26,28,30},{1,3,5,7,9,11,13,15,17,19,..., use_global_device_ids=true, to_apply=%add | all-reduce | flops 64 | bytes 512
  39.6 5.9 %gather_fusion = bf16[512,256]{1,0:T(8,128)(2,1)S(1)} fusion(bf16[16032,256]{1,0:T(8,128)(2,1)} %param.9, s32[1024]{0:T(1024)S(1)} %pad_clamp_fusion), kind=kCustom, calls=%fused_computation | custom fusion | bytes 526336 | tf_op jit(solution)/shard_map/jit(_take)/gather | solution.py:49
  47.3 4.6 all-to-all-start
  64.6 7.1 %all-to-all-done.1 = bf16[32,16,256]{2,1,0:T(8,128)(2,1)S(1)} async-done(((bf16[32,16,256]{2,1,0:T(8,128)(2,1)}), bf16[32,16,256]{2,1,0:T(8,128)(2,1)S(1)}, u32[]{:S(2)}, u32[]{:S(2)}) %all-to-all-start.1) | async-done | bytes 262176 | tf_op jit(solution)/shard_map/all_to_all | solution.py:42
  75.4 5.0 all-to-all-start.3
  87.8 9.4 %collective-permute-start.10 = (bf16[4,64,2048]{2,1,0:T(8,128)(2,1)}, bf16[4,64,2048]{2,1,0:T(8,128)(2,1)}, u32[]{:S(2)}, u32[]{:S(2)}) collective-permute-start(bf16[4,64,2048]{2,1,0:T(8,128)(2,1)} %pad_maximum_fusion.4), channel_id=1, source_target_pairs={{0,0},{1,1},{2,4},{3,5},{4,8},{5,9},{6,12},{7,13},{8,16},{9,17},{1... | collective-permute-start | bytes 3145736 | tf_op jit(solution)/shard_map/ppermute | solution.py:32
  97.2 22.9 %collective-permute-done.22 = bf16[256,2048]{1,0:T(8,128)(2,1)} collective-permute-done((bf16[256,2048]{1,0:T(8,128)(2,1)S(1)}, bf16[256,2048]{1,0:T(8,128)(2,1)}, u32[]{:S(2)}, u32[]{:S(2)}) %collective-permute-start.22) | collective-permute-done | bytes 1048608 | tf_op jit(solution)/shard_map/ppermute | solution.py:23
  124.6 5.3 %all-to-all-start.4 = ((bf16[4,128,2,1024]{3,2,1,0:T(2,128)(2,1)}), bf16[4,128,2,1024]{3,2,1,0:T(2,128)(2,1)S(1)}, u32[]{:S(2)}, u32[]{:S(2)}) async-start(bf16[4,128,2,1024]{3,2,1,0:T(2,128)(2,1)} %bitcast.201), calls=%async_computation.4 | async-start | bytes 4194304 | tf_op jit(solution)/shard_map/all_to_all | solution.py:42
  129.9 4.4 dynamic-slice_bitcast_fusion.3
  134.8 8.9 %collective-permute-done.2 = bf16[2048,256]{1,0:T(8,128)(2,1)} collective-permute-done((bf16[2048,256]{1,0:T(8,128)(2,1)}, bf16[2048,256]{1,0:T(8,128)(2,1)}, u32[]{:S(2)}, u32[]{:S(2)}) %collective-permute-start.2) | collective-permute-done | bytes 1048608 | tf_op jit(solution)/shard_map/ppermute | solution.py:23
  153.8 10.5 %all-to-all-done.4 = bf16[4,128,2,1024]{3,2,1,0:T(2,128)(2,1)S(1)} async-done(((bf16[4,128,2,1024]{3,2,1,0:T(2,128)(2,1)}), bf16[4,128,2,1024]{3,2,1,0:T(2,128)(2,1)S(1)}, u32[]{:S(2)}, u32[]{:S(2)}) %all-to-all-start.4) | async-done | bytes 2097184 | tf_op jit(solution)/shard_map/all_to_all | solution.py:42
  172.1 4.7 all-to-all-start.5
  195.6 7.0 %collective-permute-done.14 = f32[64,896]{0,1:T(8,128)S(1)} collective-permute-done((f32[64,896]{0,1:T(8,128)S(1)}, f32[64,896]{0,1:T(8,128)S(1)}, u32[]{:S(2)}, u32[]{:S(2)}) %collective-permute-start.14) | collective-permute-done | bytes 229408 | tf_op jit(solution)/shard_map/ppermute | solution.py:23
  202.6 11.0 %collective-permute-done.15 = f32[64,896]{0,1:T(8,128)S(1)} collective-permute-done((f32[64,896]{0,1:T(8,128)S(1)}, f32[64,896]{0,1:T(8,128)S(1)}, u32[]{:S(2)}, u32[]{:S(2)}) %collective-permute-start.15) | collective-permute-done | bytes 229408 | tf_op jit(solution)/shard_map/ppermute | solution.py:23
  214.8 10.5 %all-to-all-done.5 = bf16[16,4,2,128,128]{4,3,2,1,0:T(8,128)(2,1)} async-done(((bf16[16,4,2,128,128]{4,3,2,1,0:T(8,128)(2,1)}), bf16[16,4,2,128,128]{4,3,2,1,0:T(8,128)(2,1)}, u32[]{:S(2)}, u32[]{:S(2)}) %all-to-all-start.5) | async-done | bytes 4194336 | tf_op jit(solution)/shard_map/all_to_all | solution.py:36
  233.8 13.3 %collective-permute-start.17 = (bf16[64,512]{1,0:T(8,128)(2,1)S(1)}, bf16[64,512]{1,0:T(8,128)(2,1)S(1)}, u32[]{:S(2)}, u32[]{:S(2)}) collective-permute-start(bf16[64,512]{1,0:T(8,128)(2,1)S(1)} %pad_maximum_fusion.8), channel_id=1, source_target_pairs={{0,32},{32,64},{64,96},{96,0},{1,33},{33,65},{65,97},{97,1},{2,34}... | collective-permute-start | bytes 196616 | tf_op jit(solution)/shard_map/ppermute | solution.py:23
  259.2 17.2 %all_to_all.74 = bf16[16,16,2048]{2,1,0:T(8,128)(2,1)S(1)} all-to-all(bf16[16,16,2048]{2,1,0:T(8,128)(2,1)} %bitcast.206), channel_id=1, replica_groups={{0,2,4,6,8,10,12,14,16,18,20,22,24,26,28,30},{1,3,5,7,9,11,13,15,17,19,..., dimensions={0} | all-to-all | bytes 2097152 | tf_op jit(solution)/shard_map/all_to_all | solution.py:36
  278.3 4.3 all-to-all-start.7
  282.7 13.3 %all-to-all-done.7 = bf16[16,16,2048]{2,1,0:T(8,128)(2,1)} async-done(((bf16[16,16,2048]{2,1,0:T(8,128)(2,1)}), bf16[16,16,2048]{2,1,0:T(8,128)(2,1)}, u32[]{:S(2)}, u32[]{:S(2)}) %all-to-all-start.7) | async-done | bytes 1048608 | tf_op jit(solution)/shard_map/all_to_all | solution.py:36
  307.6 13.1 %collective-permute-done.27 = f32[64,896]{0,1:T(8,128)S(1)} collective-permute-done((f32[64,896]{0,1:T(8,128)S(1)}, f32[64,896]{0,1:T(8,128)S(1)}, u32[]{:S(2)}, u32[]{:S(2)}) %collective-permute-start.27) | collective-permute-done | bytes 229408 | tf_op jit(solution)/shard_map/ppermute | solution.py:23
  336.2 18.3 %all_to_all.75 = bf16[16,16,2048]{2,1,0:T(8,128)(2,1)S(1)} all-to-all(bf16[16,16,2048]{2,1,0:T(8,128)(2,1)} %bitcast.207), channel_id=1, replica_groups={{0,2,4,6,8,10,12,14,16,18,20,22,24,26,28,30},{1,3,5,7,9,11,13,15,17,19,..., dimensions={0} | all-to-all | bytes 2097152 | tf_op jit(solution)/shard_map/all_to_all | solution.py:36
  356.5 4.5 all-to-all-start.9
  361.0 14.2 %all-to-all-done.9 = bf16[16,16,2048]{2,1,0:T(8,128)(2,1)} async-done(((bf16[16,16,2048]{2,1,0:T(8,128)(2,1)}), bf16[16,16,2048]{2,1,0:T(8,128)(2,1)}, u32[]{:S(2)}, u32[]{:S(2)}) %all-to-all-start.9) | async-done | bytes 1048608 | tf_op jit(solution)/shard_map/all_to_all | solution.py:36
  388.3 8.1 %collective-permute-done.33 = f32[64,896]{0,1:T(8,128)S(1)} collective-permute-done((f32[64,896]{0,1:T(8,128)S(1)}, f32[64,896]{0,1:T(8,128)S(1)}, u32[]{:S(2)}, u32[]{:S(2)}) %collective-permute-start.33) | collective-permute-done | bytes 229408 | tf_op jit(solution)/shard_map/ppermute | solution.py:23
  396.4 4.9 collective-permute-done.34
  417.2 19.0 %all_to_all.76 = bf16[16,16,2048]{2,1,0:T(8,128)(2,1)S(1)} all-to-all(bf16[16,16,2048]{2,1,0:T(8,128)(2,1)} %bitcast.208), channel_id=1, replica_groups={{0,2,4,6,8,10,12,14,16,18,20,22,24,26,28,30},{1,3,5,7,9,11,13,15,17,19,..., dimensions={0} | all-to-all | bytes 2097152 | tf_op jit(solution)/shard_map/all_to_all | solution.py:36
  438.1 4.3 all-to-all-start.11
  442.5 14.5 %all-to-all-done.11 = bf16[16,16,2048]{2,1,0:T(8,128)(2,1)} async-done(((bf16[16,16,2048]{2,1,0:T(8,128)(2,1)}), bf16[16,16,2048]{2,1,0:T(8,128)(2,1)}, u32[]{:S(2)}, u32[]{:S(2)}) %all-to-all-start.11) | async-done | bytes 1048608 | tf_op jit(solution)/shard_map/all_to_all | solution.py:36
  468.8 14.5 %collective-permute-done.39 = f32[64,896]{0,1:T(8,128)S(1)} collective-permute-done((f32[64,896]{0,1:T(8,128)S(1)}, f32[64,896]{0,1:T(8,128)S(1)}, u32[]{:S(2)}, u32[]{:S(2)}) %collective-permute-start.39) | collective-permute-done | bytes 229408 | tf_op jit(solution)/shard_map/ppermute | solution.py:23
  501.4 16.0 %all-to-all-done.12 = bf16[16,16,2048]{2,1,0:T(8,128)(2,1)S(1)} async-done(((bf16[16,16,2048]{2,1,0:T(8,128)(2,1)}), bf16[16,16,2048]{2,1,0:T(8,128)(2,1)S(1)}, u32[]{:S(2)}, u32[]{:S(2)}) %all-to-all-start.12) | async-done | bytes 1048608 | tf_op jit(solution)/shard_map/all_to_all | solution.py:36
  517.7 8.4 %all_to_all.77 = f32[4,4,2048]{2,1,0:T(4,128)S(1)} all-to-all(f32[4,4,2048]{2,1,0:T(4,128)S(1)} %copy.24), channel_id=1, replica_groups=mesh['section'=4,'tensor'=32] {'section'}, dimensions={0} | all-to-all | bytes 262144 | tf_op jit(solution)/shard_map/all_to_all | solution.py:42
  (397 shorter events, 197.1 us)
Async XLA Ops:
  0.0 47.2 %all-to-all-start.2 = ((f32[4,1,2048]{2,1,0:T(1,128)}), f32[4,1,2048]{2,1,0:T(1,128)S(1)}, u32[]{:S(2)}, u32[]{:S(2)}) async-start(f32[4,1,2048]{2,1,0:T(1,128)} %bitcast.233), calls=%async_computation.2 | async-start | bytes 65536 | tf_op jit(solution)/shard_map/all_to_all | solution.py:42
  6.7 65.7 %collective-permute-start.7 = (bf16[64,2048]{1,0:T(8,128)(2,1)}, bf16[64,2048]{1,0:T(8,128)(2,1)}, u32[]{:S(2)}, u32[]{:S(2)}) collective-permute-start(bf16[64,2048]{1,0:T(8,128)(2,1)} %get-tuple-element.44), channel_id=1, source_target_pairs={{0,32},{32,64},{64,96},{96,0},{1,33},{33,65},{65,97},{97,1},{2,34}... | collective-permute-start | bytes 786440 | tf_op jit(solution)/shard_map/ppermute | solution.py:23
  8.8 71.8 %collective-permute-start.8 = (bf16[64,2048]{1,0:T(8,128)(2,1)}, bf16[64,2048]{1,0:T(8,128)(2,1)}, u32[]{:S(2)}, u32[]{:S(2)}) collective-permute-start(bf16[64,2048]{1,0:T(8,128)(2,1)} %get-tuple-element.46), channel_id=1, source_target_pairs={{0,64},{32,96},{64,0},{96,32},{1,65},{33,97},{65,1},{97,33},{2,66}... | collective-permute-start | bytes 786440 | tf_op jit(solution)/shard_map/ppermute | solution.py:23
  11.4 71.2 %collective-permute-start.9 = (bf16[64,2048]{1,0:T(8,128)(2,1)}, bf16[64,2048]{1,0:T(8,128)(2,1)}, u32[]{:S(2)}, u32[]{:S(2)}) collective-permute-start(bf16[64,2048]{1,0:T(8,128)(2,1)} %get-tuple-element.45), channel_id=1, source_target_pairs={{0,96},{32,0},{64,32},{96,64},{1,97},{33,1},{65,33},{97,65},{2,98}... | collective-permute-start | bytes 786440 | tf_op jit(solution)/shard_map/ppermute | solution.py:23
  16.5 67.0 %collective-permute-start.20 = (bf16[256,2048]{1,0:T(8,128)(2,1)S(1)}, bf16[256,2048]{1,0:T(8,128)(2,1)}, u32[]{:S(2)}, u32[]{:S(2)}) collective-permute-start(bf16[256,2048]{1,0:T(8,128)(2,1)S(1)} %get-tuple-element.26), channel_id=1, source_target_pairs={{0,32},{32,64},{64,96},{96,0},{1,33},{33,65},{65,97},{97,1},{2,34}... | collective-permute-start | bytes 3145736 | tf_op jit(solution)/shard_map/ppermute | solution.py:23
  17.0 70.7 %collective-permute-start.21 = (bf16[256,2048]{1,0:T(8,128)(2,1)S(1)}, bf16[256,2048]{1,0:T(8,128)(2,1)}, u32[]{:S(2)}, u32[]{:S(2)}) collective-permute-start(bf16[256,2048]{1,0:T(8,128)(2,1)S(1)} %get-tuple-element.28), channel_id=1, source_target_pairs={{0,64},{32,96},{64,0},{96,32},{1,65},{33,97},{65,1},{97,33},{2,66}... | collective-permute-start | bytes 3145736 | tf_op jit(solution)/shard_map/ppermute | solution.py:23
  72.4 47.7 %collective-permute-start.22 = (bf16[256,2048]{1,0:T(8,128)(2,1)S(1)}, bf16[256,2048]{1,0:T(8,128)(2,1)}, u32[]{:S(2)}, u32[]{:S(2)}) collective-permute-start(bf16[256,2048]{1,0:T(8,128)(2,1)S(1)} %get-tuple-element.27), channel_id=1, source_target_pairs={{0,96},{32,0},{64,32},{96,64},{1,97},{33,1},{65,33},{97,65},{2,98}... | collective-permute-start | bytes 3145736 | tf_op jit(solution)/shard_map/ppermute | solution.py:23
  75.4 49.2 %all-to-all-start.3 = ((bf16[16,16,2048]{2,1,0:T(8,128)(2,1)}), bf16[16,16,2048]{2,1,0:T(8,128)(2,1)}, u32[]{:S(2)}, u32[]{:S(2)}) async-start(bf16[16,16,2048]{2,1,0:T(8,128)(2,1)} %broadcast_in_dim.59), calls=%async_computation.3 | async-start | bytes 2097152 | tf_op jit(solution)/shard_map/all_to_all | solution.py:36
  80.6 53.7 %collective-permute-start = (bf16[2048,256]{1,0:T(8,128)(2,1)}, bf16[2048,256]{1,0:T(8,128)(2,1)}, u32[]{:S(2)}, u32[]{:S(2)}) collective-permute-start(bf16[2048,256]{1,0:T(8,128)(2,1)} %get-tuple-element.22), channel_id=1, source_target_pairs={{0,32},{32,64},{64,96},{96,0},{1,33},{33,65},{65,97},{97,1},{2,34}... | collective-permute-start | bytes 3145736 | tf_op jit(solution)/shard_map/ppermute | solution.py:23
  82.7 51.6 %collective-permute-start.1 = (bf16[2048,256]{1,0:T(8,128)(2,1)}, bf16[2048,256]{1,0:T(8,128)(2,1)}, u32[]{:S(2)}, u32[]{:S(2)}) collective-permute-start(bf16[2048,256]{1,0:T(8,128)(2,1)} %get-tuple-element.24), channel_id=1, source_target_pairs={{0,64},{32,96},{64,0},{96,32},{1,65},{33,97},{65,1},{97,33},{2,66}... | collective-permute-start | bytes 3145736 | tf_op jit(solution)/shard_map/ppermute | solution.py:23
  83.5 60.2 %collective-permute-start.2 = (bf16[2048,256]{1,0:T(8,128)(2,1)}, bf16[2048,256]{1,0:T(8,128)(2,1)}, u32[]{:S(2)}, u32[]{:S(2)}) collective-permute-start(bf16[2048,256]{1,0:T(8,128)(2,1)} %get-tuple-element.23), channel_id=1, source_target_pairs={{0,96},{32,0},{64,32},{96,64},{1,97},{33,1},{65,33},{97,65},{2,98}... | collective-permute-start | bytes 3145736 | tf_op jit(solution)/shard_map/ppermute | solution.py:23
  87.8 58.4 %collective-permute-start.10 = (bf16[4,64,2048]{2,1,0:T(8,128)(2,1)}, bf16[4,64,2048]{2,1,0:T(8,128)(2,1)}, u32[]{:S(2)}, u32[]{:S(2)}) collective-permute-start(bf16[4,64,2048]{2,1,0:T(8,128)(2,1)} %pad_maximum_fusion.4), channel_id=1, source_target_pairs={{0,0},{1,1},{2,4},{3,5},{4,8},{5,9},{6,12},{7,13},{8,16},{9,17},{1... | collective-permute-start | bytes 3145736 | tf_op jit(solution)/shard_map/ppermute | solution.py:32
  120.1 26.6 %collective-permute-start.11 = (bf16[4,64,2048]{2,1,0:T(8,128)(2,1)}, bf16[4,64,2048]{2,1,0:T(8,128)(2,1)S(1)}, u32[]{:S(2)}, u32[]{:S(2)}) collective-permute-start(bf16[4,64,2048]{2,1,0:T(8,128)(2,1)} %pad_maximum_fusion.4), channel_id=1, source_target_pairs={{0,2},{1,3},{2,6},{3,7},{4,10},{5,11},{6,14},{7,15},{8,18},{9,19},... | collective-permute-start | bytes 3145736 | tf_op jit(solution)/shard_map/ppermute | solution.py:32
  124.6 39.6 %all-to-all-start.4 = ((bf16[4,128,2,1024]{3,2,1,0:T(2,128)(2,1)}), bf16[4,128,2,1024]{3,2,1,0:T(2,128)(2,1)S(1)}, u32[]{:S(2)}, u32[]{:S(2)}) async-start(bf16[4,128,2,1024]{3,2,1,0:T(2,128)(2,1)} %bitcast.201), calls=%async_computation.4 | async-start | bytes 4194304 | tf_op jit(solution)/shard_map/all_to_all | solution.py:42
  134.3 42.5 %collective-permute-start.3 = (bf16[2048,256]{1,0:T(8,128)(2,1)}, bf16[2048,256]{1,0:T(8,128)(2,1)}, u32[]{:S(2)}, u32[]{:S(2)}) collective-permute-start(bf16[2048,256]{1,0:T(8,128)(2,1)} %bitcast.18), channel_id=1, source_target_pairs={{0,1},{1,0},{2,3},{3,2},{4,5},{5,4},{6,7},{7,6},{8,9},{9,8},{10,11... | collective-permute-start | bytes 3145736 | tf_op jit(solution)/shard_map/ppermute | solution.py:27
  134.3 42.6 %collective-permute-start.4 = (bf16[2048,256]{1,0:T(8,128)(2,1)}, bf16[2048,256]{1,0:T(8,128)(2,1)}, u32[]{:S(2)}, u32[]{:S(2)}) collective-permute-start(bf16[2048,256]{1,0:T(8,128)(2,1)} %collective-permute-done), channel_id=1, source_target_pairs={{0,1},{1,0},{2,3},{3,2},{4,5},{5,4},{6,7},{7,6},{8,9},{9,8},{10,11... | collective-permute-start | bytes 3145736 | tf_op jit(solution)/shard_map/ppermute | solution.py:27
  143.7 33.7 %collective-permute-start.5 = (bf16[2048,256]{1,0:T(8,128)(2,1)}, bf16[2048,256]{1,0:T(8,128)(2,1)}, u32[]{:S(2)}, u32[]{:S(2)}) collective-permute-start(bf16[2048,256]{1,0:T(8,128)(2,1)} %collective-permute-done.1), channel_id=1, source_target_pairs={{0,1},{1,0},{2,3},{3,2},{4,5},{5,4},{6,7},{7,6},{8,9},{9,8},{10,11... | collective-permute-start | bytes 3145736 | tf_op jit(solution)/shard_map/ppermute | solution.py:27
  146.1 31.3 %collective-permute-start.6 = (bf16[2048,256]{1,0:T(8,128)(2,1)}, bf16[2048,256]{1,0:T(8,128)(2,1)}, u32[]{:S(2)}, u32[]{:S(2)}) collective-permute-start(bf16[2048,256]{1,0:T(8,128)(2,1)} %collective-permute-done.2), channel_id=1, source_target_pairs={{0,1},{1,0},{2,3},{3,2},{4,5},{5,4},{6,7},{7,6},{8,9},{9,8},{10,11... | collective-permute-start | bytes 3145736 | tf_op jit(solution)/shard_map/ppermute | solution.py:27
  150.2 30.8 %collective-permute-start.12 = (bf16[4,64,2048]{2,1,0:T(8,128)(2,1)}, bf16[4,64,2048]{2,1,0:T(8,128)(2,1)}, u32[]{:S(2)}, u32[]{:S(2)}) collective-permute-start(bf16[4,64,2048]{2,1,0:T(8,128)(2,1)} %get-tuple-element.32), channel_id=1, source_target_pairs={{0,1},{1,0},{2,3},{3,2},{4,5},{5,4},{6,7},{7,6},{8,9},{9,8},{10,11... | collective-permute-start | bytes 3145736 | tf_op jit(solution)/shard_map/ppermute | solution.py:27
  172.1 53.3 %all-to-all-start.5 = ((bf16[16,4,2,128,128]{4,3,2,1,0:T(8,128)(2,1)}), bf16[16,4,2,128,128]{4,3,2,1,0:T(8,128)(2,1)}, u32[]{:S(2)}, u32[]{:S(2)}) async-start(bf16[16,4,2,128,128]{4,3,2,1,0:T(8,128)(2,1)} %bitcast.199), calls=%async_computation.5 | async-start | bytes 8388608 | tf_op jit(solution)/shard_map/all_to_all | solution.py:36
  189.4 24.2 %collective-permute-start.15 = (f32[64,896]{0,1:T(8,128)S(1)}, f32[64,896]{0,1:T(8,128)S(1)}, u32[]{:S(2)}, u32[]{:S(2)}) collective-permute-start(f32[64,896]{0,1:T(8,128)S(1)} %get-tuple-element.57), channel_id=1, source_target_pairs={{0,64},{32,96},{64,0},{96,32},{1,65},{33,97},{65,1},{97,33},{2,66}... | collective-permute-start | bytes 688136 | tf_op jit(solution)/shard_map/ppermute | solution.py:23
  193.3 20.3 %collective-permute-start.16 = (f32[64,896]{0,1:T(8,128)S(1)}, f32[64,896]{0,1:T(8,128)S(1)}, u32[]{:S(2)}, u32[]{:S(2)}) collective-permute-start(f32[64,896]{0,1:T(8,128)S(1)} %get-tuple-element.56), channel_id=1, source_target_pairs={{0,96},{32,0},{64,32},{96,64},{1,97},{33,1},{65,33},{97,65},{2,98}... | collective-permute-start | bytes 688136 | tf_op jit(solution)/shard_map/ppermute | solution.py:23
  233.8 19.3 %collective-permute-start.17 = (bf16[64,512]{1,0:T(8,128)(2,1)S(1)}, bf16[64,512]{1,0:T(8,128)(2,1)S(1)}, u32[]{:S(2)}, u32[]{:S(2)}) collective-permute-start(bf16[64,512]{1,0:T(8,128)(2,1)S(1)} %pad_maximum_fusion.8), channel_id=1, source_target_pairs={{0,32},{32,64},{64,96},{96,0},{1,33},{33,65},{65,97},{97,1},{2,34}... | collective-permute-start | bytes 196616 | tf_op jit(solution)/shard_map/ppermute | solution.py:23
  278.3 17.7 %all-to-all-start.7 = ((bf16[16,16,2048]{2,1,0:T(8,128)(2,1)}), bf16[16,16,2048]{2,1,0:T(8,128)(2,1)}, u32[]{:S(2)}, u32[]{:S(2)}) async-start(bf16[16,16,2048]{2,1,0:T(8,128)(2,1)} %broadcast_in_dim.64), calls=%async_computation.7 | async-start | bytes 2097152 | tf_op jit(solution)/shard_map/all_to_all | solution.py:36
  303.5 17.3 %collective-permute-start.27 = (f32[64,896]{0,1:T(8,128)S(1)}, f32[64,896]{0,1:T(8,128)S(1)}, u32[]{:S(2)}, u32[]{:S(2)}) collective-permute-start(f32[64,896]{0,1:T(8,128)S(1)} %get-tuple-element.55), channel_id=1, source_target_pairs={{0,32},{32,64},{64,96},{96,0},{1,33},{33,65},{65,97},{97,1},{2,34}... | collective-permute-start | bytes 688136 | tf_op jit(solution)/shard_map/ppermute | solution.py:23
  356.5 18.8 %all-to-all-start.9 = ((bf16[16,16,2048]{2,1,0:T(8,128)(2,1)}), bf16[16,16,2048]{2,1,0:T(8,128)(2,1)}, u32[]{:S(2)}, u32[]{:S(2)}) async-start(bf16[16,16,2048]{2,1,0:T(8,128)(2,1)} %broadcast_in_dim.66), calls=%async_computation.9 | async-start | bytes 2097152 | tf_op jit(solution)/shard_map/all_to_all | solution.py:36
  383.3 17.9 %collective-permute-start.34 = (f32[64,896]{0,1:T(8,128)S(1)}, f32[64,896]{0,1:T(8,128)S(1)}, u32[]{:S(2)}, u32[]{:S(2)}) collective-permute-start(f32[64,896]{0,1:T(8,128)S(1)} %get-tuple-element.51), channel_id=1, source_target_pairs={{0,64},{32,96},{64,0},{96,32},{1,65},{33,97},{65,1},{97,33},{2,66}... | collective-permute-start | bytes 688136 | tf_op jit(solution)/shard_map/ppermute | solution.py:23
  438.1 18.8 %all-to-all-start.11 = ((bf16[16,16,2048]{2,1,0:T(8,128)(2,1)}), bf16[16,16,2048]{2,1,0:T(8,128)(2,1)}, u32[]{:S(2)}, u32[]{:S(2)}) async-start(bf16[16,16,2048]{2,1,0:T(8,128)(2,1)} %broadcast_in_dim.68), calls=%async_computation.11 | async-start | bytes 2097152 | tf_op jit(solution)/shard_map/all_to_all | solution.py:36
  464.4 18.9 %collective-permute-start.39 = (f32[64,896]{0,1:T(8,128)S(1)}, f32[64,896]{0,1:T(8,128)S(1)}, u32[]{:S(2)}, u32[]{:S(2)}) collective-permute-start(f32[64,896]{0,1:T(8,128)S(1)} %get-tuple-element.49), channel_id=1, source_target_pairs={{0,32},{32,64},{64,96},{96,0},{1,33},{33,65},{65,97},{97,1},{2,34}... | collective-permute-start | bytes 688136 | tf_op jit(solution)/shard_map/ppermute | solution.py:23
  464.5 18.9 %collective-permute-start.40 = (f32[64,896]{0,1:T(8,128)S(1)}, f32[64,896]{0,1:T(8,128)S(1)}, u32[]{:S(2)}, u32[]{:S(2)}) collective-permute-start(f32[64,896]{0,1:T(8,128)S(1)} %get-tuple-element.48), channel_id=1, source_target_pairs={{0,64},{32,96},{64,0},{96,32},{1,65},{33,97},{65,1},{97,33},{2,66}... | collective-permute-start | bytes 688136 | tf_op jit(solution)/shard_map/ppermute | solution.py:23
  466.4 17.6 %collective-permute-start.41 = (f32[64,896]{0,1:T(8,128)S(1)}, f32[64,896]{0,1:T(8,128)S(1)}, u32[]{:S(2)}, u32[]{:S(2)}) collective-permute-start(f32[64,896]{0,1:T(8,128)S(1)} %get-tuple-element.47), channel_id=1, source_target_pairs={{0,96},{32,0},{64,32},{96,64},{1,97},{33,1},{65,33},{97,65},{2,98}... | collective-permute-start | bytes 688136 | tf_op jit(solution)/shard_map/ppermute | solution.py:23
  497.1 20.3 %all-to-all-start.12 = ((bf16[16,16,2048]{2,1,0:T(8,128)(2,1)}), bf16[16,16,2048]{2,1,0:T(8,128)(2,1)S(1)}, u32[]{:S(2)}, u32[]{:S(2)}) async-start(bf16[16,16,2048]{2,1,0:T(8,128)(2,1)} %bitcast.97), calls=%async_computation.12 | async-start | bytes 2097152 | tf_op jit(solution)/shard_map/all_to_all | solution.py:36
  (94 other events, 1609.9 us)

commit v2 on v1

v2 whole, which is shorter than its diff:
```python
import jax
import jax.numpy as jnp
from jax import lax
from jax.experimental import pallas as pl
from jax.experimental.pallas import tpu as pltpu
from jax.sharding import PartitionSpec as P

HD = 128
NORM_EPSILON = 1e-05
ROPE_BASE = 500000.0
SECTIONS = 4
CHIPS = 16
CORES = 2
STEPS = 4
HEADS_PER_CHIP = 4
BF16 = jnp.bfloat16
F32 = jnp.float32
PLANE = [[2 * p + c for p in range(CHIPS)] for c in range(CORES)]


def section_send(block, distance):
    if distance == 0:
        return block
    route = [(i, (i + distance) % SECTIONS) for i in range(SECTIONS)]
    return lax.ppermute(block, "section", route)


def core_swap(block):
    return lax.ppermute(block, "tensor", [(i, i ^ 1) for i in range(CHIPS * CORES)])


def chip_send(block, target):
    route = [(2 * p + c, 2 * target(p) + c) for p in range(CHIPS) for c in range(CORES)]
    return lax.ppermute(block, "tensor", route)


def plane_exchange(blocks):
    return lax.all_to_all(
        blocks, "tensor", split_axis=0, concat_axis=0, tiled=True, axis_index_groups=PLANE
    )


def section_exchange(blocks):
    return lax.all_to_all(blocks, "section", split_axis=0, concat_axis=0, tiled=True)


def in_three(values):
    high = lax.reduce_precision(values, 8, 7)
    middle = lax.reduce_precision(values - high, 8, 7)
    return [part.astype(BF16) for part in (high, middle, values - high - middle)]


def embed(token_ids, embedding, prefix_lengths, norm_gain, section_pos, core):
    vocab_part, width = embedding.shape
    local_ids = token_ids.T.reshape(-1) - section_pos * vocab_part
    inside = (local_ids >= 0) & (local_ids < vocab_part)
    picked = jnp.take(embedding, jnp.clip(local_ids, 0, vocab_part - 1), axis=0)
    picked = jnp.where(inside[:, None], picked, jnp.zeros_like(picked))
    picked = picked.reshape(CHIPS * CORES, 16, width)
    extra = jnp.pad(prefix_lengths.astype(BF16)[None, :], ((0, 7), (0, width - 4)))
    extra = jnp.broadcast_to(extra[None], (CHIPS * CORES, 8, width))
    by_row = lax.all_to_all(
        jnp.concatenate([picked, extra], axis=1), "tensor", split_axis=0, concat_axis=0, tiled=True
    )
    lengths = by_row[:, 16, :4].reshape(CHIPS, CORES, 4)
    lengths = lax.dynamic_index_in_dim(lengths, core, 1, keepdims=False)
    lengths = lax.dynamic_index_in_dim(lengths, section_pos, 1, keepdims=False)
    gains = jnp.stack(in_three(norm_gain.reshape(CHIPS * CORES, width)), axis=1)
    gains = jnp.pad(gains, ((0, 0), (0, 5), (0, 0)))
    by_quarter = section_exchange(jnp.concatenate([by_row[:, :16], gains], axis=1))
    by_quarter = by_quarter.reshape(SECTIONS, 8, 24, width).astype(F32)
    columns = jnp.sum(by_quarter[:, :, :16], axis=0).transpose(1, 0, 2).reshape(16, -1)
    gains = (by_quarter[:, :, 16] + by_quarter[:, :, 17]) + by_quarter[:, :, 18]
    return columns, gains.reshape(SECTIONS, 1, -1), lengths.astype(jnp.int32)


def row_orders(section_pos):
    place = jnp.arange(256)[:, None]
    source = jnp.arange(256)[None, :]
    wanted = place // 4 % CHIPS * 16 + place // 64 * 4 + place % 4
    forward = (wanted == source).astype(BF16)
    held = source // 4 % CHIPS * 16 + (section_pos - source // 64) % SECTIONS * 4 + source % 4
    backward = (held == place).astype(BF16)
    return forward, backward


TRANSPOSED = (((1,), (1,)), ((), ()))
WIDTH = HEADS_PER_CHIP * HD
SENT = WIDTH + 3 * HD


def project_kernel(rows, order, gain, wq_mine, wq_other, keys_t, values_t, out, total):
    step = pl.program_id(0)

    @pl.when(step == 0)
    def _():
        total[...] = jnp.zeros_like(total)

    block = rows[...].reshape(256, rows.shape[2])
    block = jnp.dot(order[...], block, preferred_element_type=F32).astype(BF16)
    plain = block.astype(F32) / gain[...]
    half = WIDTH // 2
    total[:, :half] += jnp.dot(block, wq_mine[...], preferred_element_type=F32)
    total[:, half:WIDTH] += jnp.dot(block, wq_other[...], preferred_element_type=F32)
    for start, weight in ((WIDTH, keys_t), (WIDTH + HD, values_t)):
        total[:, start : start + HD] += lax.dot_general(
            block, weight[...], TRANSPOSED, preferred_element_type=F32
        )
    total[:, WIDTH + 2 * HD :] += jnp.sum(plain * plain, axis=1, keepdims=True)

    @pl.when(step == pl.num_programs(0) - 1)
    def _():
        squares = total[:, WIDTH + 2 * HD :]
        high = squares.astype(BF16).astype(F32)
        middle = (squares - high).astype(BF16).astype(F32)
        low = squares - high - middle
        lane = lax.broadcasted_iota(jnp.int32, squares.shape, 1)
        parts = jnp.where(lane == 0, high, jnp.where(lane == 1, middle, low))
        parts = jnp.where(lane < 3, parts, 0.0)
        for j in range(SECTIONS):
            own = slice(64 * j, 64 * (j + 1))
            out[j, :, : WIDTH + 2 * HD] = total[own, : WIDTH + 2 * HD].astype(BF16)
            out[j, :, WIDTH + 2 * HD :] = parts[own].astype(BF16)


def project(rows, order, gain, layer, wq_mine, wq_other, keys_t, values_t):
    quarter = rows.shape[2]
    chunk = quarter // 4
    flops = 2 * 256 * quarter * (256 + WIDTH + 2 * HD)
    return pl.pallas_call(
        project_kernel,
        grid=(quarter // chunk,),
        in_specs=[
            pl.BlockSpec((CHIPS, 16, chunk), lambda k: (0, 0, k)),
            pl.BlockSpec((256, 256), lambda k: (0, 0)),
            pl.BlockSpec((None, 1, chunk), lambda k: (layer, 0, k)),
            pl.BlockSpec((None, chunk, 256), lambda k: (layer, k, 0)),
            pl.BlockSpec((None, chunk, 256), lambda k: (layer, k, 0)),
            pl.BlockSpec((None, HD, chunk), lambda k: (layer, 0, k)),
            pl.BlockSpec((None, HD, chunk), lambda k: (layer, 0, k)),
        ],
        out_specs=pl.BlockSpec((SECTIONS, 64, SENT), lambda k: (0, 0, 0)),
        out_shape=jax.ShapeDtypeStruct((SECTIONS, 64, SENT), BF16),
        scratch_shapes=[pltpu.VMEM((256, SENT), F32)],
        compiler_params=pltpu.CompilerParams(vmem_limit_bytes=32 * 2**20),
        cost_estimate=pl.CostEstimate(flops=flops, bytes_accessed=5 * 2**20, transcendentals=0),
        name="project",
    )(rows, order, gain, wq_mine, wq_other, keys_t, values_t)


def attend_kernel(parts, cosine, sine, bias, cache, out):
    total = parts[0].astype(F32)
    for i in range(1, SECTIONS):
        total = total + parts[i].astype(F32)
    squares = jnp.sum(total[:, WIDTH + 2 * HD :], axis=1, keepdims=True)
    scaling = lax.rsqrt(squares / 8192.0 + NORM_EPSILON)
    turned_cos = cosine[...] * scaling
    turned_sin = sine[...] * scaling

    def turn(vectors):
        half = HD // 2
        swapped = jnp.concatenate([-vectors[:, half:], vectors[:, :half]], axis=1)
        return (vectors * turned_cos + swapped * turned_sin).astype(BF16)

    queries = [turn(total[:, HD * h : HD * (h + 1)]) for h in range(HEADS_PER_CHIP)]
    new_keys = turn(total[:, WIDTH : WIDTH + HD])
    new_values = (total[:, WIDTH + HD : WIDTH + 2 * HD] * scaling).astype(BF16)
    row = lax.broadcasted_iota(jnp.int32, (64, 16), 0) % 16
    column = lax.broadcasted_iota(jnp.int32, (64, 16), 1)
    new_live = (row // 4 == column // 4) & (column % 4 <= row % 4)
    scale = HD**-0.5
    for g in range(4):
        own = slice(16 * g, 16 * (g + 1))
        query = jnp.concatenate([q[own] for q in queries], axis=0)
        keys = cache[4 * g : 4 * (g + 1), 0].reshape(4 * 128, HD)
        values = cache[4 * g : 4 * (g + 1), 1].reshape(4 * 128, HD)
        past = lax.dot_general(query, keys, TRANSPOSED, preferred_element_type=F32) * scale
        new = lax.dot_general(query, new_keys[own], TRANSPOSED, preferred_element_type=F32) * scale
        past = past + jnp.concatenate([bias[own]] * HEADS_PER_CHIP, axis=0)
        new = jnp.where(new_live, new, -1e30)
        top = jnp.maximum(
            jnp.max(past, axis=1, keepdims=True), jnp.max(new, axis=1, keepdims=True)
        )
        past = jnp.exp(past - top)
        new = jnp.exp(new - top)
        weight = jnp.sum(past, axis=1, keepdims=True) + jnp.sum(new, axis=1, keepdims=True)
        past = (past / weight).astype(BF16)
        new = (new / weight).astype(BF16)
        mixed = jnp.dot(past, values, preferred_element_type=F32)
        mixed = mixed + jnp.dot(new, new_values[own], preferred_element_type=F32)
        mixed = mixed.astype(BF16)
        for h in range(HEADS_PER_CHIP):
            out[own, HD * h : HD * (h + 1)] = mixed[16 * h : 16 * (h + 1)]


def attend(parts, cosine, sine, bias, cache, layer):
    whole = lambda *shape: pl.BlockSpec(shape, lambda i: (0,) * len(shape))
    return pl.pallas_call(
        attend_kernel,
        grid=(1,),
        in_specs=[
            whole(SECTIONS, 64, SENT),
            whole(64, HD),
            whole(64, HD),
            whole(64, 512),
            pl.BlockSpec((CHIPS, None, 2, 128, HD), lambda i: (0, layer, 0, 0, 0)),
        ],
        out_specs=whole(64, WIDTH),
        out_shape=jax.ShapeDtypeStruct((64, WIDTH), BF16),
        compiler_params=pltpu.CompilerParams(vmem_limit_bytes=32 * 2**20),
        cost_estimate=pl.CostEstimate(
            flops=2**28, bytes_accessed=2 * 2**20, transcendentals=2**17
        ),
        name="attend",
    )(parts, cosine, sine, bias, cache)


def output_kernel(first, second, third, fourth, order, wo_mine, wo_other, out, ordered):
    @pl.when(pl.program_id(0) == 0)
    def _():
        mixed = jnp.concatenate([first[...], second[...], third[...], fourth[...]], axis=0)
        ordered[...] = jnp.dot(order[...], mixed, preferred_element_type=F32).astype(BF16)

    half = WIDTH // 2
    terms = jnp.dot(ordered[:, :half], wo_mine[...], preferred_element_type=F32)
    terms = terms + jnp.dot(ordered[:, half:], wo_other[...], preferred_element_type=F32)
    out[...] = terms.astype(BF16).reshape(out.shape)


def output_terms(gathered, order, wo_mine, wo_other, layer):
    quarter = wo_mine.shape[2]
    chunk = quarter // 4
    return pl.pallas_call(
        output_kernel,
        grid=(quarter // chunk,),
        in_specs=[pl.BlockSpec((64, WIDTH), lambda n: (0, 0))] * SECTIONS
        + [
            pl.BlockSpec((256, 256), lambda n: (0, 0)),
            pl.BlockSpec((None, 256, chunk), lambda n: (layer, 0, n)),
            pl.BlockSpec((None, 256, chunk), lambda n: (layer, 0, n)),
        ],
        out_specs=pl.BlockSpec((CHIPS, 16, chunk), lambda n: (0, 0, n)),
        out_shape=jax.ShapeDtypeStruct((CHIPS, 16, quarter), BF16),
        scratch_shapes=[pltpu.VMEM((256, WIDTH), BF16)],
        compiler_params=pltpu.CompilerParams(vmem_limit_bytes=32 * 2**20),
        cost_estimate=pl.CostEstimate(
            flops=2 * 256 * WIDTH * quarter, bytes_accessed=4 * 2**20, transcendentals=0
        ),
        name="output_terms",
    )(*gathered, order, wo_mine, wo_other)


def body(
    token_ids,
    embedding,
    norm_gain,
    query_weight,
    keyval_weight,
    output_weight,
    prefix_cache,
    prefix_lengths,
):
    section_pos = lax.axis_index("section")
    tensor_pos = lax.axis_index("tensor")
    core, chip = tensor_pos % CORES, tensor_pos // CORES
    quarter = query_weight.shape[1] // SECTIONS

    kv_mine = section_exchange(keyval_weight[0].T.reshape(64, SECTIONS, quarter).transpose(1, 0, 2))
    wq_mine = section_exchange(query_weight[0].reshape(SECTIONS, quarter, 256))
    hidden, gains, lengths = embed(
        token_ids, embedding, prefix_lengths, norm_gain, section_pos, core
    )
    cache = section_exchange(prefix_cache[0])
    wo_mine = section_exchange(output_weight[0].reshape(256, SECTIONS, quarter).transpose(1, 0, 2))
    wq_other = core_swap(wq_mine)
    wo_other = core_swap(wo_mine)

    first = chip_send(kv_mine, lambda p: 2 * p if p < 8 else 2 * (p - 8) + 1)
    second = chip_send(kv_mine, lambda p: 2 * p + 1 if p < 8 else 2 * (p - 8))
    even = chip % 2 == 0
    heads_t = []
    for half in (jnp.where(even, first, second), jnp.where(even, second, first)):
        other = core_swap(half)
        low = jnp.where(core == 0, half, other)
        high = jnp.where(core == 0, other, half)
        heads_t.append(jnp.concatenate([low, high], axis=1))
    keys_t, values_t = heads_t

    cache = cache.reshape(SECTIONS, 128, 2, 8, HD).transpose(3, 0, 2, 1, 4)
    cache = plane_exchange(jnp.repeat(cache, 2, axis=0))

    frequency = ROPE_BASE ** (-(jnp.arange(HD // 2, dtype=F32) * 2.0 / HD))
    positions = (lengths[:, None] + jnp.arange(STEPS)[None, :]).reshape(-1).astype(F32)
    angles = positions[:, None] * frequency[None, :]
    cosine = jnp.concatenate([jnp.cos(angles)] * 2, axis=-1)
    sine = jnp.concatenate([jnp.sin(angles)] * 2, axis=-1)
    row, column = jnp.arange(64)[:, None], jnp.arange(512)[None, :]
    live = jnp.repeat(lengths, STEPS)[:, None]
    live = (row % 16 // 4 == column // 128) & (column % 128 < live)
    bias = jnp.where(live, 0.0, -1e30).astype(F32)
    forward, backward = row_orders(section_pos)

    for layer in range(SECTIONS):
        scaled = (hidden * gains[layer]).astype(BF16)
        rows = plane_exchange(jnp.broadcast_to(scaled[None], (CHIPS, 16, quarter)))
        partial = project(rows, forward, gains, layer, wq_mine, wq_other, keys_t, values_t)
        mixed = attend(section_exchange(partial), cosine, sine, bias, cache, layer)
        gathered = [section_send(mixed, d) for d in range(SECTIONS)]
        terms = plane_exchange(output_terms(gathered, backward, wo_mine, wo_other, layer))
        hidden = hidden + jnp.sum(terms.astype(F32), axis=0)

    finals = section_exchange(hidden.reshape(4, STEPS, quarter).transpose(1, 0, 2))
    return finals.transpose(1, 0, 2).reshape(1, 4, SECTIONS * quarter)


def solution(mesh):
    in_specs = (
        P(),
        P("section", "tensor"),
        P("section", None),
        P("section", None, "tensor"),
        P("section", None, "tensor"),
        P("section", "tensor", None),
        P("section", "tensor", None, None, None),
        P("tensor"),
    )
    out_specs = P("section", "tensor", None)
    return jax.shard_map(body, mesh=mesh, in_specs=in_specs, out_specs=out_specs, check_vma=False)
```

time: 538 us -> 516 us (0.959); the launches traced: 527 us -> 513 us
  blocking collectives: 80.6 us -> 181 us
  starting transfers between devices: 123 us -> 60.6 us
  matrix products: 44.5 us -> 0 us
  Pallas kernels: 0 us -> 42.2 us
  local copies, waits for them, and re-layouts: 53.1 us -> 33.6 us
  other arithmetic: 28.2 us -> 11.7 us
  waiting for transfers between devices: 196 us -> 183 us
    ppermute x33 -> x12, waiting for transfers between devices: 105 us -> 21.3 us  [section_send(): return lax.ppermute(block, 'section', route)]
    all_to_all x3 -> x5, waiting for transfers between devices: 17.6 us -> 101 us  [section_exchange(): lax.all_to_all(blocks, 'section', split_axis=0, concat_axis=0, tiled=True)]
    all_to_all x3 -> x7, blocking collectives: 54.4 us -> 123 us  [plane_exchange(): lax.all_to_all(blocks, 'tensor', split_axis=0, concat_axis=0, tiled=True,...]
    ppermute x33 -> x12, starting transfers between devices: 64.5 us -> 11.7 us  [section_send(): return lax.ppermute(block, 'section', route)]
    all_to_all x1 -> x5, blocking collectives: 8.36 us -> 58.1 us  [section_exchange(): lax.all_to_all(blocks, 'section', split_axis=0, concat_axis=0, tiled=True)]
    dot_general x40 -> x0, matrix products: 44.5 us -> none  [the longest x4 12.3 us: body(): terms = jnp.dot(gathered, out_mat, preferred_element_type=F32).astype(BF16)]
    pallas_call x0 -> x12, Pallas kernels: none -> 42.2 us  [the longest x4 16.3 us: project(): pl.pallas_call(project_kernel, grid=(quarter // chunk,), in_specs=[pl.Blo...]
    all_to_all x6 -> x2, waiting for transfers between devices: 68.6 us -> 45.5 us  [plane_exchange(): lax.all_to_all(blocks, 'tensor', split_axis=0, concat_axis=0, tiled=True,...]
  transfers between devices with their start and end apart: 55 -> 26, of which waited for: 30 -> 22; matrix products, arithmetic and copies ran while one was open for 12% -> 6% of each run, Pallas kernels for 0% -> 1%
where the time goes in v2:
time: 516 us; the launch traced here: 513 us
  waiting for transfers between devices  183 us (35%)
  blocking collectives  181 us (35%)
  starting transfers between devices  60.6 us (12%)
  Pallas kernels  42.2 us (8%)
  local copies, waits for them, and re-layouts  33.6 us (7%)
  other arithmetic  11.7 us (2%)
    all_to_all x7, blocking collectives, plane_exchange(): lax.all_to_all(blocks, 'tensor', split_axis=0, concat_axis=0, tiled=True,...  123 us
    all_to_all x5, waiting for transfers between devices, section_exchange(): lax.all_to_all(blocks, 'section', split_axis=0, concat_axis=0, tiled=True)  101 us
    all_to_all x5, blocking collectives, section_exchange(): lax.all_to_all(blocks, 'section', split_axis=0, concat_axis=0, tiled=True)  58.1 us
    all_to_all x2, waiting for transfers between devices, plane_exchange(): lax.all_to_all(blocks, 'tensor', split_axis=0, concat_axis=0, tiled=True,...  45.5 us
    ppermute x12, waiting for transfers between devices, section_send(): return lax.ppermute(block, 'section', route)  21.3 us
    all_to_all x5, starting transfers between devices, section_exchange(): lax.all_to_all(blocks, 'section', split_axis=0, concat_axis=0, tiled=True)  21.3 us
    pallas_call x4, Pallas kernels, project(): pl.pallas_call(project_kernel, grid=(quarter // chunk,), in_specs=[pl.Blo...  16.3 us
    pallas_call x4, Pallas kernels, output_terms(): pl.pallas_call(output_kernel, grid=(quarter // chunk,), in_specs=[pl.Bloc...  14.3 us
  transfers between devices with their start and end apart: 26, of which 22 were waited for; matrix products, arithmetic and copies ran while one was open for 6% of the time, Pallas kernels for 1%

profile of v2, /device:TPU:0, one launch (start us, length us, event | category | flops | bytes accessed | tf_op | source)
XLA Modules:
  0.0 512.9 jit_solution(803338339787358524)
XLA Ops:
  2.7 5.9 %gather_fusion = bf16[512,256]{1,0:T(8,128)(2,1)S(1)} fusion(bf16[16032,256]{1,0:T(8,128)(2,1)} %param.9, s32[1024]{0:T(1024)S(1)} %pad_clamp_fusion), kind=kCustom, calls=%fused_computation | custom fusion | bytes 526336 | tf_op jit(solution)/shard_map/jit(_take)/gather | solution.py:57
  9.7 8.2 %all-to-all-start = ((bf16[32,24,256]{2,1,0:T(8,128)(2,1)}), bf16[32,24,256]{2,1,0:T(8,128)(2,1)S(1)}, u32[]{:S(2)}, u32[]{:S(2)}) async-start(bf16[32,24,256]{2,1,0:T(8,128)(2,1)} %pad_maximum_fusion.2), calls=%async_computation | async-start | bytes 786432 | tf_op jit(solution)/shard_map/all_to_all | solution.py:62
  18.0 10.2 %all-to-all-done = bf16[32,24,256]{2,1,0:T(8,128)(2,1)S(1)} async-done(((bf16[32,24,256]{2,1,0:T(8,128)(2,1)}), bf16[32,24,256]{2,1,0:T(8,128)(2,1)S(1)}, u32[]{:S(2)}, u32[]{:S(2)}) %all-to-all-start) | async-done | bytes 393248 | tf_op jit(solution)/shard_map/all_to_all | solution.py:62
  29.1 4.5 all-to-all-start.1
  33.7 8.3 %all-to-all-done.1 = bf16[32,24,256]{2,1,0:T(8,128)(2,1)S(1)} async-done(((bf16[32,24,256]{2,1,0:T(8,128)(2,1)}), bf16[32,24,256]{2,1,0:T(8,128)(2,1)S(1)}, u32[]{:S(2)}, u32[]{:S(2)}) %all-to-all-start.1) | async-done | bytes 393248 | tf_op jit(solution)/shard_map/all_to_all | solution.py:44
  42.0 17.4 %all_to_all.100 = bf16[4,64,2048]{2,1,0:T(8,128)(2,1)} all-to-all(bf16[4,64,2048]{2,1,0:T(8,128)(2,1)S(1)} %bitcast.54), channel_id=1, replica_groups=mesh['section'=4,'tensor'=32] {'section'}, dimensions={0} | all-to-all | bytes 2097152 | tf_op jit(solution)/shard_map/all_to_all | solution.py:44
  64.8 22.7 %all-to-all-done.6 = bf16[4,128,2,1024]{3,2,1,0:T(2,128)(2,1)S(1)} async-done(((bf16[4,128,2,1024]{3,2,1,0:T(2,128)(2,1)}), bf16[4,128,2,1024]{3,2,1,0:T(2,128)(2,1)S(1)}, u32[]{:S(2)}, u32[]{:S(2)}) %all-to-all-start.6) | async-done | bytes 2097184 | tf_op jit(solution)/shard_map/all_to_all | solution.py:44
  87.6 20.7 %all_to_all.101.rows = bf16[16,16,2048]{2,1,0:T(8,128)(2,1)S(1)} all-to-all(bf16[16,16,2048]{2,1,0:T(8,128)(2,1)S(1)} %broadcast_in_dim.48), channel_id=1, replica_groups={{0,2,4,6,8,10,12,14,16,18,20,22,24,26,28,30},{1,3,5,7,9,11,13,15,17,19,..., dimensions={0} | all-to-all | bytes 2097152 | tf_op jit(solution)/shard_map/all_to_all | solution.py:38
  108.3 4.9 all-to-all-start.3
  113.2 6.4 %copy.69 = bf16[1,256,8192]{1,2,0:T(8,128)(2,1)} copy(bf16[1,256,8192]{2,1,0:T(8,128)(2,1)} %param.13) | data formatting | bytes 8388608 | tf_op args[5]
  119.6 6.3 %copy.70 = bf16[256,4,2048]{2,0,1:T(8,128)(2,1)} copy(bf16[256,4,2048]{0,2,1:T(8,128)(2,1)} %bitcast.51) | data formatting | bytes 8388608 | tf_op jit(solution)/shard_map/reshape;squeeze | solution.py:274
  125.9 33.0 %all-to-all-done.3.wq_mine = bf16[4,2048,256]{2,1,0:T(8,128)(2,1)} async-done(((bf16[4,2048,256]{2,1,0:T(8,128)(2,1)}), bf16[4,2048,256]{2,1,0:T(8,128)(2,1)}, u32[]{:S(2)}, u32[]{:S(2)}) %all-to-all-start.3) | async-done | bytes 4194336 | tf_op jit(solution)/shard_map/all_to_all | solution.py:44
  158.8 4.9 all-to-all-start.8
  164.6 9.5 %collective-permute-start.1 = (bf16[4,64,2048]{2,1,0:T(8,128)(2,1)}, bf16[4,64,2048]{2,1,0:T(8,128)(2,1)}, u32[]{:S(2)}, u32[]{:S(2)}) collective-permute-start(bf16[4,64,2048]{2,1,0:T(8,128)(2,1)} %all_to_all.100), channel_id=1, source_target_pairs={{0,0},{1,1},{2,4},{3,5},{4,8},{5,9},{6,12},{7,13},{8,16},{9,17},{1... | collective-permute-start | bytes 3145736 | tf_op jit(solution)/shard_map/ppermute | solution.py:34
  178.9 29.6 %all-to-all-done.8.wo_mine = bf16[4,256,2048]{2,1,0:T(8,128)(2,1)} async-done(((bf16[4,256,2048]{2,1,0:T(8,128)(2,1)}), bf16[4,256,2048]{2,1,0:T(8,128)(2,1)}, u32[]{:S(2)}, u32[]{:S(2)}) %all-to-all-start.8) | async-done | bytes 4194336 | tf_op jit(solution)/shard_map/all_to_all | solution.py:44
  211.5 4.5 all-to-all-start.7
  220.4 4.6 collective-permute-done.4
  228.3 4.1 project.4
  234.5 32.5 %all-to-all-done.7.cache = bf16[16,4,2,128,128]{4,3,2,1,0:T(8,128)(2,1)} async-done(((bf16[16,4,2,128,128]{4,3,2,1,0:T(8,128)(2,1)}), bf16[16,4,2,128,128]{4,3,2,1,0:T(8,128)(2,1)}, u32[]{:S(2)}, u32[]{:S(2)}) %all-to-all-start.7) | async-done | bytes 4194336 | tf_op jit(solution)/shard_map/all_to_all | solution.py:38
  270.9 7.3 %all-to-all-done.5.parts = bf16[4,64,896]{2,1,0:T(8,128)(2,1)S(1)} async-done(((bf16[4,64,896]{2,1,0:T(8,128)(2,1)}), bf16[4,64,896]{2,1,0:T(8,128)(2,1)S(1)}, u32[]{:S(2)}, u32[]{:S(2)}) %all-to-all-start.5) | async-done | bytes 458784 | tf_op jit(solution)/shard_map/all_to_all | solution.py:44
  293.1 18.6 %all_to_all.102 = bf16[16,16,2048]{2,1,0:T(8,128)(2,1)S(1)} all-to-all(bf16[16,16,2048]{2,1,0:T(8,128)(2,1)S(1)} %output_terms.4), channel_id=1, replica_groups={{0,2,4,6,8,10,12,14,16,18,20,22,24,26,28,30},{1,3,5,7,9,11,13,15,17,19,..., dimensions={0} | all-to-all | bytes 2097152 | tf_op jit(solution)/shard_map/all_to_all | solution.py:38
  312.0 16.8 %all_to_all.103.rows = bf16[16,16,2048]{2,1,0:T(8,128)(2,1)S(1)} all-to-all(bf16[16,16,2048]{2,1,0:T(8,128)(2,1)S(1)} %broadcast_in_dim.85), channel_id=1, replica_groups={{0,2,4,6,8,10,12,14,16,18,20,22,24,26,28,30},{1,3,5,7,9,11,13,15,17,19,..., dimensions={0} | all-to-all | bytes 2097152 | tf_op jit(solution)/shard_map/all_to_all | solution.py:38
  332.9 10.2 %all_to_all.104.parts = bf16[4,64,896]{2,1,0:T(8,128)(2,1)S(1)} all-to-all(bf16[4,64,896]{2,1,0:T(8,128)(2,1)S(1)} %project.5), channel_id=1, replica_groups=mesh['section'=4,'tensor'=32] {'section'}, dimensions={0} | all-to-all | bytes 917504 | tf_op jit(solution)/shard_map/all_to_all | solution.py:44
  358.0 15.8 %all_to_all.105 = bf16[16,16,2048]{2,1,0:T(8,128)(2,1)S(1)} all-to-all(bf16[16,16,2048]{2,1,0:T(8,128)(2,1)S(1)} %output_terms.5), channel_id=1, replica_groups={{0,2,4,6,8,10,12,14,16,18,20,22,24,26,28,30},{1,3,5,7,9,11,13,15,17,19,..., dimensions={0} | all-to-all | bytes 2097152 | tf_op jit(solution)/shard_map/all_to_all | solution.py:38
  374.6 15.8 %all_to_all.106.rows = bf16[16,16,2048]{2,1,0:T(8,128)(2,1)S(1)} all-to-all(bf16[16,16,2048]{2,1,0:T(8,128)(2,1)S(1)} %broadcast_in_dim.86), channel_id=1, replica_groups={{0,2,4,6,8,10,12,14,16,18,20,22,24,26,28,30},{1,3,5,7,9,11,13,15,17,19,..., dimensions={0} | all-to-all | bytes 2097152 | tf_op jit(solution)/shard_map/all_to_all | solution.py:38
  394.5 10.7 %all_to_all.107.parts = bf16[4,64,896]{2,1,0:T(8,128)(2,1)S(1)} all-to-all(bf16[4,64,896]{2,1,0:T(8,128)(2,1)S(1)} %project.6), channel_id=1, replica_groups=mesh['section'=4,'tensor'=32] {'section'}, dimensions={0} | all-to-all | bytes 917504 | tf_op jit(solution)/shard_map/all_to_all | solution.py:44
  419.0 19.8 %all_to_all.108 = bf16[16,16,2048]{2,1,0:T(8,128)(2,1)S(1)} all-to-all(bf16[16,16,2048]{2,1,0:T(8,128)(2,1)S(1)} %output_terms.6), channel_id=1, replica_groups={{0,2,4,6,8,10,12,14,16,18,20,22,24,26,28,30},{1,3,5,7,9,11,13,15,17,19,..., dimensions={0} | all-to-all | bytes 2097152 | tf_op jit(solution)/shard_map/all_to_all | solution.py:38
  439.6 15.9 %all_to_all.109.rows = bf16[16,16,2048]{2,1,0:T(8,128)(2,1)S(1)} all-to-all(bf16[16,16,2048]{2,1,0:T(8,128)(2,1)S(1)} %broadcast_in_dim.87), channel_id=1, replica_groups={{0,2,4,6,8,10,12,14,16,18,20,22,24,26,28,30},{1,3,5,7,9,11,13,15,17,19,..., dimensions={0} | all-to-all | bytes 2097152 | tf_op jit(solution)/shard_map/all_to_all | solution.py:38
  459.6 11.4 %all_to_all.110.parts = bf16[4,64,896]{2,1,0:T(8,128)(2,1)S(1)} all-to-all(bf16[4,64,896]{2,1,0:T(8,128)(2,1)S(1)} %project.7), channel_id=1, replica_groups=mesh['section'=4,'tensor'=32] {'section'}, dimensions={0} | all-to-all | bytes 917504 | tf_op jit(solution)/shard_map/all_to_all | solution.py:44
  482.1 4.4 output_terms.7
  490.5 13.0 %all-to-all-done.18 = bf16[16,16,2048]{2,1,0:T(8,128)(2,1)S(1)} async-done(((bf16[16,16,2048]{2,1,0:T(8,128)(2,1)}), bf16[16,16,2048]{2,1,0:T(8,128)(2,1)S(1)}, u32[]{:S(2)}, u32[]{:S(2)}) %all-to-all-start.18) | async-done | bytes 1048608 | tf_op jit(solution)/shard_map/all_to_all | solution.py:38
  503.8 8.4 %all_to_all.111 = f32[4,4,2048]{2,1,0:T(4,128)S(1)} all-to-all(f32[4,4,2048]{2,1,0:T(4,128)S(1)} %copy.71), channel_id=1, replica_groups=mesh['section'=4,'tensor'=32] {'section'}, dimensions={0} | all-to-all | bytes 262144 | tf_op jit(solution)/shard_map/all_to_all | solution.py:44
  (149 shorter events, 106.1 us)
Async XLA Ops:
  0.0 17.9 %copy-start.14 = (f32[1,8192]{1,0:T(1,128)S(1)}, f32[1,8192]{1,0:T(1,128)}, u32[]{:S(2)}) copy-start(f32[1,8192]{1,0:T(1,128)} %param.10) | copy-start | bytes 98308
  0.0 33.6 %copy-start.13 = (bf16[1,8192,64]{1,2,0:T(8,128)(2,1)S(1)}, bf16[1,8192,64]{1,2,0:T(8,128)(2,1)}, u32[]{:S(2)}) copy-start(bf16[1,8192,64]{1,2,0:T(8,128)(2,1)} %param.12) | copy-start | bytes 3145732
  9.7 18.6 %all-to-all-start = ((bf16[32,24,256]{2,1,0:T(8,128)(2,1)}), bf16[32,24,256]{2,1,0:T(8,128)(2,1)S(1)}, u32[]{:S(2)}, u32[]{:S(2)}) async-start(bf16[32,24,256]{2,1,0:T(8,128)(2,1)} %pad_maximum_fusion.2), calls=%async_computation | async-start | bytes 786432 | tf_op jit(solution)/shard_map/all_to_all | solution.py:62
  29.1 12.8 %all-to-all-start.1 = ((bf16[32,24,256]{2,1,0:T(8,128)(2,1)}), bf16[32,24,256]{2,1,0:T(8,128)(2,1)S(1)}, u32[]{:S(2)}, u32[]{:S(2)}) async-start(bf16[32,24,256]{2,1,0:T(8,128)(2,1)} %fusion.1), calls=%async_computation.1 | async-start | bytes 786432 | tf_op jit(solution)/shard_map/all_to_all | solution.py:44
  42.0 17.4 %copy-start.3 = (bf16[32,24,256]{2,1,0:T(8,128)(2,1)}, bf16[32,24,256]{2,1,0:T(8,128)(2,1)S(1)}, u32[]{:S(2)}) copy-start(bf16[32,24,256]{2,1,0:T(8,128)(2,1)S(1)} %all-to-all-done.1) | copy-start | bytes 1179652
  59.4 28.1 %all-to-all-start.6 = ((bf16[4,128,2,1024]{3,2,1,0:T(2,128)(2,1)}), bf16[4,128,2,1024]{3,2,1,0:T(2,128)(2,1)S(1)}, u32[]{:S(2)}, u32[]{:S(2)}) async-start(bf16[4,128,2,1024]{3,2,1,0:T(2,128)(2,1)} %bitcast.55), calls=%async_computation.6 | async-start | bytes 4194304 | tf_op jit(solution)/shard_map/all_to_all | solution.py:44
  108.3 50.5 %all-to-all-start.3 = ((bf16[4,2048,256]{2,1,0:T(8,128)(2,1)}), bf16[4,2048,256]{2,1,0:T(8,128)(2,1)}, u32[]{:S(2)}, u32[]{:S(2)}) async-start(bf16[4,2048,256]{2,1,0:T(8,128)(2,1)} %bitcast.53), calls=%async_computation.3 | async-start | bytes 8388608 | tf_op jit(solution)/shard_map/all_to_all | solution.py:44
  158.8 49.6 %all-to-all-start.8 = ((bf16[4,256,2048]{2,1,0:T(8,128)(2,1)}), bf16[4,256,2048]{2,1,0:T(8,128)(2,1)}, u32[]{:S(2)}, u32[]{:S(2)}) async-start(bf16[4,256,2048]{2,1,0:T(8,128)(2,1)} %bitcast.50), calls=%async_computation.8 | async-start | bytes 8388608 | tf_op jit(solution)/shard_map/all_to_all | solution.py:44
  163.7 64.5 %collective-permute-start = (bf16[4,2048,256]{2,1,0:T(8,128)(2,1)}, bf16[4,2048,256]{2,1,0:T(8,128)(2,1)}, u32[]{:S(2)}, u32[]{:S(2)}) collective-permute-start(bf16[4,2048,256]{2,1,0:T(8,128)(2,1)} %all-to-all-done.3.wq_mine), channel_id=1, source_target_pairs={{0,1},{1,0},{2,3},{3,2},{4,5},{5,4},{6,7},{7,6},{8,9},{9,8},{10,11... | collective-permute-start | bytes 12582920 | tf_op jit(solution)/shard_map/ppermute | solution.py:29
  163.8 52.4 %collective-permute-start.2 = (bf16[4,64,2048]{2,1,0:T(8,128)(2,1)}, bf16[4,64,2048]{2,1,0:T(8,128)(2,1)}, u32[]{:S(2)}, u32[]{:S(2)}) collective-permute-start(bf16[4,64,2048]{2,1,0:T(8,128)(2,1)} %all_to_all.100), channel_id=1, source_target_pairs={{0,2},{1,3},{2,6},{3,7},{4,10},{5,11},{6,14},{7,15},{8,18},{9,19},... | collective-permute-start | bytes 3145736 | tf_op jit(solution)/shard_map/ppermute | solution.py:34
  164.6 51.6 %collective-permute-start.1 = (bf16[4,64,2048]{2,1,0:T(8,128)(2,1)}, bf16[4,64,2048]{2,1,0:T(8,128)(2,1)}, u32[]{:S(2)}, u32[]{:S(2)}) collective-permute-start(bf16[4,64,2048]{2,1,0:T(8,128)(2,1)} %all_to_all.100), channel_id=1, source_target_pairs={{0,0},{1,1},{2,4},{3,5},{4,8},{5,9},{6,12},{7,13},{8,16},{9,17},{1... | collective-permute-start | bytes 3145736 | tf_op jit(solution)/shard_map/ppermute | solution.py:34
  211.5 55.5 %all-to-all-start.7 = ((bf16[16,4,2,128,128]{4,3,2,1,0:T(8,128)(2,1)}), bf16[16,4,2,128,128]{4,3,2,1,0:T(8,128)(2,1)}, u32[]{:S(2)}, u32[]{:S(2)}) async-start(bf16[16,4,2,128,128]{4,3,2,1,0:T(8,128)(2,1)} %bitcast.49), calls=%async_computation.7 | async-start | bytes 8388608 | tf_op jit(solution)/shard_map/all_to_all | solution.py:38
  216.1 68.3 %collective-permute-start.8 = (bf16[4,256,2048]{2,1,0:T(8,128)(2,1)}, bf16[4,256,2048]{2,1,0:T(8,128)(2,1)}, u32[]{:S(2)}, u32[]{:S(2)}) collective-permute-start(bf16[4,256,2048]{2,1,0:T(8,128)(2,1)} %all-to-all-done.8.wo_mine), channel_id=1, source_target_pairs={{0,1},{1,0},{2,3},{3,2},{4,5},{5,4},{6,7},{7,6},{8,9},{9,8},{10,11... | collective-permute-start | bytes 12582920 | tf_op jit(solution)/shard_map/ppermute | solution.py:29
  217.9 7.0 %collective-permute-start.4 = (bf16[4,64,2048]{2,1,0:T(8,128)(2,1)S(1)}, bf16[4,64,2048]{2,1,0:T(8,128)(2,1)}, u32[]{:S(2)}, u32[]{:S(2)}) collective-permute-start(bf16[4,64,2048]{2,1,0:T(8,128)(2,1)S(1)} %get-tuple-element.11), channel_id=1, source_target_pairs={{0,1},{1,0},{2,3},{3,2},{4,5},{5,4},{6,7},{7,6},{8,9},{9,8},{10,11... | collective-permute-start | bytes 3145736 | tf_op jit(solution)/shard_map/ppermute | solution.py:29
  218.5 8.0 %collective-permute-start.3 = (bf16[4,64,2048]{2,1,0:T(8,128)(2,1)S(1)}, bf16[4,64,2048]{2,1,0:T(8,128)(2,1)}, u32[]{:S(2)}, u32[]{:S(2)}) collective-permute-start(bf16[4,64,2048]{2,1,0:T(8,128)(2,1)S(1)} %get-tuple-element.12), channel_id=1, source_target_pairs={{0,1},{1,0},{2,3},{3,2},{4,5},{5,4},{6,7},{7,6},{8,9},{9,8},{10,11... | collective-permute-start | bytes 3145736 | tf_op jit(solution)/shard_map/ppermute | solution.py:29
  267.0 11.2 %all-to-all-start.5 = ((bf16[4,64,896]{2,1,0:T(8,128)(2,1)}), bf16[4,64,896]{2,1,0:T(8,128)(2,1)S(1)}, u32[]{:S(2)}, u32[]{:S(2)}) async-start(bf16[4,64,896]{2,1,0:T(8,128)(2,1)} %copy-done.2), calls=%async_computation.5 | async-start | bytes 917504 | tf_op jit(solution)/shard_map/all_to_all | solution.py:44
  281.1 4.6 collective-permute-start.7
  283.2 5.8 %collective-permute-start.6 = (bf16[64,512]{1,0:T(8,128)(2,1)S(1)}, bf16[64,512]{1,0:T(8,128)(2,1)S(1)}, u32[]{:S(2)}, u32[]{:S(2)}) collective-permute-start(bf16[64,512]{1,0:T(8,128)(2,1)S(1)} %attend.4.first), channel_id=1, source_target_pairs={{0,64},{32,96},{64,0},{96,32},{1,65},{33,97},{65,1},{97,33},{2,66}... | collective-permute-start | bytes 196616 | tf_op jit(solution)/shard_map/ppermute | solution.py:25
  284.3 5.5 %collective-permute-start.5 = (bf16[64,512]{1,0:T(8,128)(2,1)S(1)}, bf16[64,512]{1,0:T(8,128)(2,1)S(1)}, u32[]{:S(2)}, u32[]{:S(2)}) collective-permute-start(bf16[64,512]{1,0:T(8,128)(2,1)S(1)} %attend.4.first), channel_id=1, source_target_pairs={{0,32},{32,64},{64,96},{96,0},{1,33},{33,65},{65,97},{97,1},{2,34}... | collective-permute-start | bytes 196616 | tf_op jit(solution)/shard_map/ppermute | solution.py:25
  284.4 27.5 %copy-start.9 = (f32[8,2,8,256]{3,2,0,1:T(8,128)S(1)}, f32[8,2,8,256]{3,2,0,1:T(8,128)}, u32[]{:S(2)}) copy-start(f32[8,2,8,256]{3,2,0,1:T(8,128)} %copy-done.8) | copy-start | bytes 393220
  293.1 35.7 %copy-start.1 = (bf16[4,128,2048]{2,1,0:T(8,128)(2,1)S(1)}, bf16[4,128,2048]{2,1,0:T(8,128)(2,1)}, u32[]{:S(2)}) copy-start(bf16[4,128,2048]{2,1,0:T(8,128)(2,1)} %copy-done) | copy-start | bytes 6291460
  346.0 4.3 collective-permute-start.11
  347.3 5.8 %collective-permute-start.10 = (bf16[64,512]{1,0:T(8,128)(2,1)S(1)}, bf16[64,512]{1,0:T(8,128)(2,1)S(1)}, u32[]{:S(2)}, u32[]{:S(2)}) collective-permute-start(bf16[64,512]{1,0:T(8,128)(2,1)S(1)} %attend.5.first), channel_id=1, source_target_pairs={{0,64},{32,96},{64,0},{96,32},{1,65},{33,97},{65,1},{97,33},{2,66}... | collective-permute-start | bytes 196616 | tf_op jit(solution)/shard_map/ppermute | solution.py:25
  349.2 5.5 %collective-permute-start.9 = (bf16[64,512]{1,0:T(8,128)(2,1)S(1)}, bf16[64,512]{1,0:T(8,128)(2,1)S(1)}, u32[]{:S(2)}, u32[]{:S(2)}) collective-permute-start(bf16[64,512]{1,0:T(8,128)(2,1)S(1)} %attend.5.first), channel_id=1, source_target_pairs={{0,32},{32,64},{64,96},{96,0},{1,33},{33,65},{65,97},{97,1},{2,34}... | collective-permute-start | bytes 196616 | tf_op jit(solution)/shard_map/ppermute | solution.py:25
  408.1 4.3 collective-permute-start.14
  408.7 5.8 %collective-permute-start.13 = (bf16[64,512]{1,0:T(8,128)(2,1)S(1)}, bf16[64,512]{1,0:T(8,128)(2,1)S(1)}, u32[]{:S(2)}, u32[]{:S(2)}) collective-permute-start(bf16[64,512]{1,0:T(8,128)(2,1)S(1)} %attend.6.first), channel_id=1, source_target_pairs={{0,64},{32,96},{64,0},{96,32},{1,65},{33,97},{65,1},{97,33},{2,66}... | collective-permute-start | bytes 196616 | tf_op jit(solution)/shard_map/ppermute | solution.py:25
  410.2 5.5 %collective-permute-start.12 = (bf16[64,512]{1,0:T(8,128)(2,1)S(1)}, bf16[64,512]{1,0:T(8,128)(2,1)S(1)}, u32[]{:S(2)}, u32[]{:S(2)}) collective-permute-start(bf16[64,512]{1,0:T(8,128)(2,1)S(1)} %attend.6.first), channel_id=1, source_target_pairs={{0,32},{32,64},{64,96},{96,0},{1,33},{33,65},{65,97},{97,1},{2,34}... | collective-permute-start | bytes 196616 | tf_op jit(solution)/shard_map/ppermute | solution.py:25
  473.9 16.5 %copy-start.11 = (f32[16,2048]{1,0:T(8,128)S(1)}, f32[16,2048]{1,0:T(8,128)}, u32[]{:S(2)}) copy-start(f32[16,2048]{1,0:T(8,128)} %copy-done.10) | copy-start | bytes 393220
  474.0 4.3 collective-permute-start.17
  475.2 5.8 %collective-permute-start.16 = (bf16[64,512]{1,0:T(8,128)(2,1)S(1)}, bf16[64,512]{1,0:T(8,128)(2,1)S(1)}, u32[]{:S(2)}, u32[]{:S(2)}) collective-permute-start(bf16[64,512]{1,0:T(8,128)(2,1)S(1)} %attend.7.first), channel_id=1, source_target_pairs={{0,64},{32,96},{64,0},{96,32},{1,65},{33,97},{65,1},{97,33},{2,66}... | collective-permute-start | bytes 196616 | tf_op jit(solution)/shard_map/ppermute | solution.py:25
  476.7 5.5 %collective-permute-start.15 = (bf16[64,512]{1,0:T(8,128)(2,1)S(1)}, bf16[64,512]{1,0:T(8,128)(2,1)S(1)}, u32[]{:S(2)}, u32[]{:S(2)}) collective-permute-start(bf16[64,512]{1,0:T(8,128)(2,1)S(1)} %attend.7.first), channel_id=1, source_target_pairs={{0,32},{32,64},{64,96},{96,0},{1,33},{33,65},{65,97},{97,1},{2,34}... | collective-permute-start | bytes 196616 | tf_op jit(solution)/shard_map/ppermute | solution.py:25
  486.5 17.0 %all-to-all-start.18 = ((bf16[16,16,2048]{2,1,0:T(8,128)(2,1)}), bf16[16,16,2048]{2,1,0:T(8,128)(2,1)S(1)}, u32[]{:S(2)}, u32[]{:S(2)}) async-start(bf16[16,16,2048]{2,1,0:T(8,128)(2,1)} %output_terms.7), calls=%async_computation.18 | async-start | bytes 2097152 | tf_op jit(solution)/shard_map/all_to_all | solution.py:38
  (9 other events, 42.8 us)

commit v3 on v2

--- a/solution.py
+++ b/solution.py
@@ -50,7 +50,7 @@
     return [part.astype(BF16) for part in (high, middle, values - high - middle)]
 
 
-def embed(token_ids, embedding, prefix_lengths, norm_gain, section_pos, core):
+def embed(token_ids, embedding, prefix_lengths, norm_gain, kv_mat, cached, section_pos, core):
     vocab_part, width = embedding.shape
     local_ids = token_ids.T.reshape(-1) - section_pos * vocab_part
     inside = (local_ids >= 0) & (local_ids < vocab_part)
@@ -67,11 +67,15 @@
     lengths = lax.dynamic_index_in_dim(lengths, section_pos, 1, keepdims=False)
     gains = jnp.stack(in_three(norm_gain.reshape(CHIPS * CORES, width)), axis=1)
     gains = jnp.pad(gains, ((0, 0), (0, 5), (0, 0)))
-    by_quarter = section_exchange(jnp.concatenate([by_row[:, :16], gains], axis=1))
-    by_quarter = by_quarter.reshape(SECTIONS, 8, 24, width).astype(F32)
+    by_row, cached = lax.optimization_barrier((by_row, cached))
+    kv_mat = kv_mat.reshape(64, CHIPS * CORES, width).transpose(1, 0, 2)
+    by_quarter = section_exchange(jnp.concatenate([by_row[:, :16], gains, kv_mat], axis=1))
+    by_quarter = by_quarter.reshape(SECTIONS, 8, 88, width)
+    kv_mine = by_quarter[:, :, 24:].transpose(0, 2, 1, 3).reshape(SECTIONS, 64, -1)
+    by_quarter = by_quarter[:, :, :24].astype(F32)
     columns = jnp.sum(by_quarter[:, :, :16], axis=0).transpose(1, 0, 2).reshape(16, -1)
     gains = (by_quarter[:, :, 16] + by_quarter[:, :, 17]) + by_quarter[:, :, 18]
-    return columns, gains.reshape(SECTIONS, 1, -1), lengths.astype(jnp.int32)
+    return columns, gains.reshape(SECTIONS, 1, -1), lengths.astype(jnp.int32), kv_mine, cached
 
 
 def row_orders(section_pos):
@@ -89,7 +93,9 @@
 SENT = WIDTH + 3 * HD
 
 
-def project_kernel(rows, order, gain, wq_mine, wq_other, keys_t, values_t, out, total):
+def project_kernel(slot, rows, order, gain, *refs):
+    wq_mine, wq_other = refs[:SECTIONS], refs[SECTIONS : 2 * SECTIONS]
+    keys_t, values_t, out, total = refs[2 * SECTIONS :]
     step = pl.program_id(0)
 
     @pl.when(step == 0)
@@ -100,8 +106,13 @@
     block = jnp.dot(order[...], block, preferred_element_type=F32).astype(BF16)
     plain = block.astype(F32) / gain[...]
     half = WIDTH // 2
-    total[:, :half] += jnp.dot(block, wq_mine[...], preferred_element_type=F32)
-    total[:, half:WIDTH] += jnp.dot(block, wq_other[...], preferred_element_type=F32)
+    for d in range(SECTIONS):
+
+        @pl.when(slot[0] == d)
+        def _():
+            total[:, :half] += jnp.dot(block, wq_mine[d][...], preferred_element_type=F32)
+            total[:, half:WIDTH] += jnp.dot(block, wq_other[d][...], preferred_element_type=F32)
+
     for start, weight in ((WIDTH, keys_t), (WIDTH + HD, values_t)):
         total[:, start : start + HD] += lax.dot_general(
             block, weight[...], TRANSPOSED, preferred_element_type=F32
@@ -123,32 +134,43 @@
             out[j, :, WIDTH + 2 * HD :] = parts[own].astype(BF16)
 
 
-def project(rows, order, gain, layer, wq_mine, wq_other, keys_t, values_t):
+def chosen(d, k, slot):
+    return jnp.where(slot[0] == d, k, 0)
+
+
+def project(rows, order, gain, layer, slot, wq_mine, wq_other, keys_t, values_t):
     quarter = rows.shape[2]
     chunk = quarter // 4
     flops = 2 * 256 * quarter * (256 + WIDTH + 2 * HD)
+    pieces = [
+        pl.BlockSpec((chunk, 256), lambda k, slot, d=d: (chosen(d, k, slot), 0))
+        for d in range(SECTIONS)
+    ]
     return pl.pallas_call(
         project_kernel,
-        grid=(quarter // chunk,),
-        in_specs=[
-            pl.BlockSpec((CHIPS, 16, chunk), lambda k: (0, 0, k)),
-            pl.BlockSpec((256, 256), lambda k: (0, 0)),
-            pl.BlockSpec((None, 1, chunk), lambda k: (layer, 0, k)),
-            pl.BlockSpec((None, chunk, 256), lambda k: (layer, k, 0)),
-            pl.BlockSpec((None, chunk, 256), lambda k: (layer, k, 0)),
-            pl.BlockSpec((None, HD, chunk), lambda k: (layer, 0, k)),
-            pl.BlockSpec((None, HD, chunk), lambda k: (layer, 0, k)),
-        ],
-        out_specs=pl.BlockSpec((SECTIONS, 64, SENT), lambda k: (0, 0, 0)),
+        grid_spec=pltpu.PrefetchScalarGridSpec(
+            num_scalar_prefetch=1,
+            grid=(quarter // chunk,),
+            in_specs=[
+                pl.BlockSpec((CHIPS, 16, chunk), lambda k, slot: (0, 0, k)),
+                pl.BlockSpec((256, 256), lambda k, slot: (0, 0)),
+                pl.BlockSpec((None, 1, chunk), lambda k, slot: (layer, 0, k)),
+                *pieces,
+                *pieces,
+                pl.BlockSpec((None, HD, chunk), lambda k, slot: (layer, 0, k)),
+                pl.BlockSpec((None, HD, chunk), lambda k, slot: (layer, 0, k)),
+            ],
+            out_specs=pl.BlockSpec((SECTIONS, 64, SENT), lambda k, slot: (0, 0, 0)),
+            scratch_shapes=[pltpu.VMEM((256, SENT), F32)],
+        ),
         out_shape=jax.ShapeDtypeStruct((SECTIONS, 64, SENT), BF16),
-        scratch_shapes=[pltpu.VMEM((256, SENT), F32)],
         compiler_params=pltpu.CompilerParams(vmem_limit_bytes=32 * 2**20),
         cost_estimate=pl.CostEstimate(flops=flops, bytes_accessed=5 * 2**20, transcendentals=0),
         name="project",
-    )(rows, order, gain, wq_mine, wq_other, keys_t, values_t)
-
-
-def attend_kernel(parts, cosine, sine, bias, cache, out):
+    )(slot, rows, order, gain, *wq_mine, *wq_other, keys_t, values_t)
+
+
+def attend_kernel(slot, parts, cosine, sine, bias, cache, out):
     total = parts[0].astype(F32)
     for i in range(1, SECTIONS):
         total = total + parts[i].astype(F32)
@@ -193,61 +215,76 @@
             out[own, HD * h : HD * (h + 1)] = mixed[16 * h : 16 * (h + 1)]
 
 
-def attend(parts, cosine, sine, bias, cache, layer):
-    whole = lambda *shape: pl.BlockSpec(shape, lambda i: (0,) * len(shape))
+def attend(parts, cosine, sine, bias, cache, slot):
+    whole = lambda *shape: pl.BlockSpec(shape, lambda i, slot: (0,) * len(shape))
     return pl.pallas_call(
         attend_kernel,
-        grid=(1,),
-        in_specs=[
-            whole(SECTIONS, 64, SENT),
-            whole(64, HD),
-            whole(64, HD),
-            whole(64, 512),
-            pl.BlockSpec((CHIPS, None, 2, 128, HD), lambda i: (0, layer, 0, 0, 0)),
-        ],
-        out_specs=whole(64, WIDTH),
+        grid_spec=pltpu.PrefetchScalarGridSpec(
+            num_scalar_prefetch=1,
+            grid=(1,),
+            in_specs=[
+                whole(SECTIONS, 64, SENT),
+                whole(64, HD),
+                whole(64, HD),
+                whole(64, 512),
+                pl.BlockSpec((CHIPS, None, 2, 128, HD), lambda i, slot: (0, slot[0], 0, 0, 0)),
+            ],
+            out_specs=whole(64, WIDTH),
+        ),
         out_shape=jax.ShapeDtypeStruct((64, WIDTH), BF16),
         compiler_params=pltpu.CompilerParams(vmem_limit_bytes=32 * 2**20),
         cost_estimate=pl.CostEstimate(
             flops=2**28, bytes_accessed=2 * 2**20, transcendentals=2**17
         ),
         name="attend",
-    )(parts, cosine, sine, bias, cache)
-
-
-def output_kernel(first, second, third, fourth, order, wo_mine, wo_other, out, ordered):
+    )(slot, parts, cosine, sine, bias, cache)
+
+
+def output_kernel(slot, first, second, third, fourth, order, *refs):
+    wo_mine, wo_other = refs[:SECTIONS], refs[SECTIONS : 2 * SECTIONS]
+    out, ordered = refs[2 * SECTIONS :]
+
     @pl.when(pl.program_id(0) == 0)
     def _():
         mixed = jnp.concatenate([first[...], second[...], third[...], fourth[...]], axis=0)
         ordered[...] = jnp.dot(order[...], mixed, preferred_element_type=F32).astype(BF16)
 
     half = WIDTH // 2
-    terms = jnp.dot(ordered[:, :half], wo_mine[...], preferred_element_type=F32)
-    terms = terms + jnp.dot(ordered[:, half:], wo_other[...], preferred_element_type=F32)
-    out[...] = terms.astype(BF16).reshape(out.shape)
-
-
-def output_terms(gathered, order, wo_mine, wo_other, layer):
-    quarter = wo_mine.shape[2]
+    for d in range(SECTIONS):
+
+        @pl.when(slot[0] == d)
+        def _():
+            terms = jnp.dot(ordered[:, :half], wo_mine[d][...], preferred_element_type=F32)
+            terms = terms + jnp.dot(
+                ordered[:, half:], wo_other[d][...], preferred_element_type=F32
+            )
+            out[...] = terms.astype(BF16).reshape(out.shape)
+
+
+def output_terms(gathered, order, slot, wo_mine, wo_other):
+    quarter = wo_mine[0].shape[1]
     chunk = quarter // 4
+    pieces = [
+        pl.BlockSpec((256, chunk), lambda n, slot, d=d: (0, chosen(d, n, slot)))
+        for d in range(SECTIONS)
+    ]
     return pl.pallas_call(
         output_kernel,
-        grid=(quarter // chunk,),
-        in_specs=[pl.BlockSpec((64, WIDTH), lambda n: (0, 0))] * SECTIONS
-        + [
-            pl.BlockSpec((256, 256), lambda n: (0, 0)),
-            pl.BlockSpec((None, 256, chunk), lambda n: (layer, 0, n)),
-            pl.BlockSpec((None, 256, chunk), lambda n: (layer, 0, n)),
-        ],
-        out_specs=pl.BlockSpec((CHIPS, 16, chunk), lambda n: (0, 0, n)),
+        grid_spec=pltpu.PrefetchScalarGridSpec(
+            num_scalar_prefetch=1,
+            grid=(quarter // chunk,),
+            in_specs=[pl.BlockSpec((64, WIDTH), lambda n, slot: (0, 0))] * SECTIONS
+            + [pl.BlockSpec((256, 256), lambda n, slot: (0, 0)), *pieces, *pieces],
+            out_specs=pl.BlockSpec((CHIPS, 16, chunk), lambda n, slot: (0, 0, n)),
+            scratch_shapes=[pltpu.VMEM((256, WIDTH), BF16)],
+        ),
         out_shape=jax.ShapeDtypeStruct((CHIPS, 16, quarter), BF16),
-        scratch_shapes=[pltpu.VMEM((256, WIDTH), BF16)],
         compiler_params=pltpu.CompilerParams(vmem_limit_bytes=32 * 2**20),
         cost_estimate=pl.CostEstimate(
             flops=2 * 256 * WIDTH * quarter, bytes_accessed=4 * 2**20, transcendentals=0
         ),
         name="output_terms",
-    )(*gathered, order, wo_mine, wo_other)
+    )(slot, *gathered, order, *wo_mine, *wo_other)
 
 
 def body(
@@ -265,16 +302,29 @@
     core, chip = tensor_pos % CORES, tensor_pos // CORES
     quarter = query_weight.shape[1] // SECTIONS
 
-    kv_mine = section_exchange(keyval_weight[0].T.reshape(64, SECTIONS, quarter).transpose(1, 0, 2))
-    wq_mine = section_exchange(query_weight[0].reshape(SECTIONS, quarter, 256))
-    hidden, gains, lengths = embed(
-        token_ids, embedding, prefix_lengths, norm_gain, section_pos, core
+    def share(array, axis, size, distance):
+        start = (section_pos + distance) % SECTIONS * size
+        return section_send(lax.dynamic_slice_in_dim(array, start, size, axis), distance)
+
+    distances = range(SECTIONS)
+    wq_mine = [share(query_weight[0], 0, quarter, d) for d in distances]
+    cached = [share(prefix_cache[0], 0, 1, d) for d in distances]
+    hidden, gains, lengths, kv_mine, cached = embed(
+        token_ids,
+        embedding,
+        prefix_lengths,
+        norm_gain,
+        keyval_weight[0].T,
+        cached,
+        section_pos,
+        core,
     )
-    cache = section_exchange(prefix_cache[0])
-    wo_mine = section_exchange(output_weight[0].reshape(256, SECTIONS, quarter).transpose(1, 0, 2))
-    wq_other = core_swap(wq_mine)
-    wo_other = core_swap(wo_mine)
-
+    cached, wq_mine[1], wq_mine[3] = lax.optimization_barrier((cached, wq_mine[1], wq_mine[3]))
+    cached = [c.reshape(1, 128, 2, 8, HD).transpose(3, 0, 2, 1, 4) for c in cached]
+    cache = plane_exchange(jnp.repeat(jnp.concatenate(cached, axis=1), 2, axis=0))
+    hidden, cache, wq_mine[2] = lax.optimization_barrier((hidden, cache, wq_mine[2]))
+    wo_mine = [share(output_weight[0], 1, quarter, d) for d in distances]
+    wq_other = [core_swap(w) for w in wq_mine]
     first = chip_send(kv_mine, lambda p: 2 * p if p < 8 else 2 * (p - 8) + 1)
     second = chip_send(kv_mine, lambda p: 2 * p + 1 if p < 8 else 2 * (p - 8))
     even = chip % 2 == 0
@@ -286,9 +336,12 @@
         heads_t.append(jnp.concatenate([low, high], axis=1))
     keys_t, values_t = heads_t
 
-    cache = cache.reshape(SECTIONS, 128, 2, 8, HD).transpose(3, 0, 2, 1, 4)
-    cache = plane_exchange(jnp.repeat(cache, 2, axis=0))
-
+    def gather_rows(layer):
+        scaled = (hidden * gains[layer]).astype(BF16)
+        return plane_exchange(jnp.broadcast_to(scaled[None], (CHIPS, 16, quarter)))
+
+    rows = gather_rows(0)
+    rows, wo_mine[1], wo_mine[3] = lax.optimization_barrier((rows, wo_mine[1], wo_mine[3]))
     frequency = ROPE_BASE ** (-(jnp.arange(HD // 2, dtype=F32) * 2.0 / HD))
     positions = (lengths[:, None] + jnp.arange(STEPS)[None, :]).reshape(-1).astype(F32)
     angles = positions[:, None] * frequency[None, :]
@@ -301,12 +354,17 @@
     forward, backward = row_orders(section_pos)
 
     for layer in range(SECTIONS):
-        scaled = (hidden * gains[layer]).astype(BF16)
-        rows = plane_exchange(jnp.broadcast_to(scaled[None], (CHIPS, 16, quarter)))
-        partial = project(rows, forward, gains, layer, wq_mine, wq_other, keys_t, values_t)
-        mixed = attend(section_exchange(partial), cosine, sine, bias, cache, layer)
-        gathered = [section_send(mixed, d) for d in range(SECTIONS)]
-        terms = plane_exchange(output_terms(gathered, backward, wo_mine, wo_other, layer))
+        slot = ((section_pos - layer) % SECTIONS).reshape(1)
+        if layer > 0:
+            rows = gather_rows(layer)
+        partial = project(rows, forward, gains, layer, slot, wq_mine, wq_other, keys_t, values_t)
+        parts = section_exchange(partial)
+        if layer == 0:
+            parts, wo_mine = lax.optimization_barrier((parts, wo_mine))
+            wo_other = [core_swap(w) for w in wo_mine]
+        mixed = attend(parts, cosine, sine, bias, cache, slot)
+        gathered = [section_send(mixed, d) for d in distances]
+        terms = plane_exchange(output_terms(gathered, backward, slot, wo_mine, wo_other))
         hidden = hidden + jnp.sum(terms.astype(F32), axis=0)
 
     finals = section_exchange(hidden.reshape(4, STEPS, quarter).transpose(1, 0, 2))

time: 516 us -> 523 us (1.014)
  blocking collectives: 181 us -> 121 us
  starting transfers between devices: 60.6 us -> 90.3 us
  local copies, waits for them, and re-layouts: 33.6 us -> 61.4 us
  waiting for transfers between devices: 183 us -> 173 us
  other arithmetic: 11.7 us -> 21.2 us
    all_to_all x5 -> x2, waiting for transfers between devices: 101 us -> 13.1 us  [section_exchange(): lax.all_to_all(blocks, 'section', split_axis=0, concat_axis=0, tiled=True)]
    ppermute x2, waiting for transfers between devices: 0.01 us -> 56.1 us  [chip_send(): return lax.ppermute(block, 'tensor', route)]
    all_to_all x7 -> x4, blocking collectives: 123 us -> 68.9 us  [plane_exchange(): lax.all_to_all(blocks, 'tensor', split_axis=0, concat_axis=0, tiled=True,...]
    ppermute x12 -> x21, waiting for transfers between devices: 21.3 us -> 51.1 us  [section_send(): return lax.ppermute(block, 'section', route)]
    all_to_all x2 -> x5, starting transfers between devices: 8.19 us -> 32.4 us  [plane_exchange(): lax.all_to_all(blocks, 'tensor', split_axis=0, concat_axis=0, tiled=True,...]
    ppermute x12 -> x21, starting transfers between devices: 11.7 us -> 27.3 us  [section_send(): return lax.ppermute(block, 'section', route)]
    dynamic_slice x0 -> x7, local copies, waits for them, and re-layouts: none -> 15 us  [share(): lax.dynamic_slice_in_dim(array, start, size, axis)]
    all_to_all x5 -> x2, starting transfers between devices: 21.3 us -> 8.61 us  [section_exchange(): lax.all_to_all(blocks, 'section', split_axis=0, concat_axis=0, tiled=True)]
  transfers between devices with their start and end apart: 26 -> 41, of which waited for: 22 -> 23; matrix products, arithmetic and copies ran while one was open for 6% -> 8% of each run, Pallas kernels for 1% -> 2%
where the time goes in v3:
time: 523 us; the launch traced here: 516 us
  waiting for transfers between devices  173 us (33%)
  blocking collectives  121 us (23%)
  starting transfers between devices  90.3 us (17%)
  local copies, waits for them, and re-layouts  61.4 us (12%)
  Pallas kernels  47.4 us (9%)
  other arithmetic  21.2 us (4%)
    all_to_all x4, blocking collectives, plane_exchange(): lax.all_to_all(blocks, 'tensor', split_axis=0, concat_axis=0, tiled=True,...  68.9 us
    ppermute x2, waiting for transfers between devices, chip_send(): return lax.ppermute(block, 'tensor', route)  56.1 us
    all_to_all x5, waiting for transfers between devices, plane_exchange(): lax.all_to_all(blocks, 'tensor', split_axis=0, concat_axis=0, tiled=True,...  52.7 us
    all_to_all x4, blocking collectives, section_exchange(): lax.all_to_all(blocks, 'section', split_axis=0, concat_axis=0, tiled=True)  52.6 us
    ppermute x21, waiting for transfers between devices, section_send(): return lax.ppermute(block, 'section', route)  51.1 us
    all_to_all x5, starting transfers between devices, plane_exchange(): lax.all_to_all(blocks, 'tensor', split_axis=0, concat_axis=0, tiled=True,...  32.4 us
    ppermute x21, starting transfers between devices, section_send(): return lax.ppermute(block, 'section', route)  27.3 us
    pallas_call x4, Pallas kernels, project(): pl.pallas_call(project_kernel, grid_spec=pltpu.PrefetchScalarGridSpec(num...  22.1 us
  transfers between devices with their start and end apart: 41, of which 23 were waited for; matrix products, arithmetic and copies ran while one was open for 8% of the time, Pallas kernels for 2%

profile of v3, /device:TPU:0, one launch (start us, length us, event | category | flops | bytes accessed | tf_op | source)
XLA Modules:
  0.0 516.1 jit_solution(14520856669235672778)
XLA Ops:
  2.6 6.1 %gather_fusion = bf16[512,256]{1,0:T(8,128)(2,1)S(1)} fusion(bf16[16032,256]{1,0:T(8,128)(2,1)} %param.9, s32[1024]{0:T(1024)S(1)} %pad_clamp_fusion), kind=kCustom, calls=%fused_computation | custom fusion | bytes 526336 | tf_op jit(solution)/shard_map/jit(_take)/gather | solution.py:57
  9.7 8.2 %all-to-all-start = ((bf16[32,24,256]{2,1,0:T(8,128)(2,1)}), bf16[32,24,256]{2,1,0:T(8,128)(2,1)S(1)}, u32[]{:S(2)}, u32[]{:S(2)}) async-start(bf16[32,24,256]{2,1,0:T(8,128)(2,1)} %pad_maximum_fusion.4), calls=%async_computation | async-start | bytes 786432 | tf_op jit(solution)/shard_map/all_to_all | solution.py:62
  30.7 4.4 dynamic-slice_bitcast_fusion.2
  41.3 10.1 %collective-permute-done.1 = bf16[1,128,2,1024]{1,3,2,0:T(8,128)(2,1)} collective-permute-done((bf16[1,128,2,1024]{1,3,2,0:T(8,128)(2,1)}, bf16[1,128,2,1024]{1,3,2,0:T(8,128)(2,1)}, u32[]{:S(2)}, u32[]{:S(2)}) %collective-permute-start.1) | collective-permute-done | bytes 524320 | tf_op jit(solution)/shard_map/ppermute | solution.py:25
  55.2 4.5 all-to-all-start.1
  59.7 13.5 %collective-permute-done.3.refs_1_ = bf16[2048,256]{1,0:T(8,128)(2,1)S(1)} collective-permute-done((bf16[2048,256]{1,0:T(8,128)(2,1)}, bf16[2048,256]{1,0:T(8,128)(2,1)S(1)}, u32[]{:S(2)}, u32[]{:S(2)}) %collective-permute-start.3) | collective-permute-done | bytes 1048608 | tf_op jit(solution)/shard_map/ppermute | solution.py:25
  82.1 6.4 %all-to-all-done.1 = bf16[32,88,256]{2,1,0:T(8,128)(2,1)S(1)} async-done(((bf16[32,88,256]{2,1,0:T(8,128)(2,1)}), bf16[32,88,256]{2,1,0:T(8,128)(2,1)S(1)}, u32[]{:S(2)}, u32[]{:S(2)}) %all-to-all-start.1) | async-done | bytes 1441824 | tf_op jit(solution)/shard_map/all_to_all | solution.py:44
  88.5 5.6 %broadcast_in_dim.48 = bf16[8,2,4,2,128,128]{5,4,3,2,1,0:T(8,128)(2,1)} broadcast(bf16[8,4,2,128,128]{4,3,2,1,0:T(8,128)(2,1)} %copy.53), dimensions={0,2,3,4,5} | broadcast | bytes 6291456 | tf_op jit(solution)/shard_map/broadcast_in_dim | solution.py:324
  94.1 7.0 %all-to-all-start.2 = ((bf16[16,4,2,128,128]{4,3,2,1,0:T(8,128)(2,1)}), bf16[16,4,2,128,128]{4,3,2,1,0:T(8,128)(2,1)}, u32[]{:S(2)}, u32[]{:S(2)}) async-start(bf16[16,4,2,128,128]{4,3,2,1,0:T(8,128)(2,1)} %bitcast.78), calls=%async_computation.2 | async-start | bytes 8388608 | tf_op jit(solution)/shard_map/all_to_all | solution.py:38
  104.3 9.5 %collective-permute-start.12 = (bf16[4,64,2048]{2,1,0:T(8,128)(2,1)}, bf16[4,64,2048]{2,1,0:T(8,128)(2,1)}, u32[]{:S(2)}, u32[]{:S(2)}) collective-permute-start(bf16[4,64,2048]{2,1,0:T(8,128)(2,1)} %bitcast.54), channel_id=1, source_target_pairs={{0,0},{1,1},{2,4},{3,5},{4,8},{5,9},{6,12},{7,13},{8,16},{9,17},{1... | collective-permute-start | bytes 3145736 | tf_op jit(solution)/shard_map/ppermute | solution.py:34
  121.8 56.1 %collective-permute-done.13 = bf16[4,64,2048]{2,1,0:T(8,128)(2,1)} collective-permute-done((bf16[4,64,2048]{2,1,0:T(8,128)(2,1)}, bf16[4,64,2048]{2,1,0:T(8,128)(2,1)}, u32[]{:S(2)}, u32[]{:S(2)}) %collective-permute-start.13) | collective-permute-done | bytes 1048608 | tf_op jit(solution)/shard_map/ppermute | solution.py:34
  184.5 12.4 %all-to-all-start.3 = ((bf16[16,16,2048]{2,1,0:T(8,128)(2,1)}), bf16[16,16,2048]{2,1,0:T(8,128)(2,1)}, u32[]{:S(2)}, u32[]{:S(2)}) async-start(bf16[16,16,2048]{2,1,0:T(8,128)(2,1)} %broadcast_in_dim.82), calls=%async_computation.3 | async-start | bytes 2097152 | tf_op jit(solution)/shard_map/all_to_all | solution.py:38
  203.4 12.2 %all-to-all-done.3.rows = bf16[16,16,2048]{2,1,0:T(8,128)(2,1)} async-done(((bf16[16,16,2048]{2,1,0:T(8,128)(2,1)}), bf16[16,16,2048]{2,1,0:T(8,128)(2,1)}, u32[]{:S(2)}, u32[]{:S(2)}) %all-to-all-start.3) | async-done | bytes 1048608 | tf_op jit(solution)/shard_map/all_to_all | solution.py:38
  219.7 5.5 %project.4 = bf16[4,64,896]{2,1,0:T(8,128)(2,1)S(1)} custom-call(s32[1]{0:T(128)} %bitcast.26.slot, bf16[16,16,2048]{2,1,0:T(8,128)(2,1)} %all-to-all-done.3.rows, bf16[256,256]{1,0:T(8,128)(2,1)S(1)} %fusion.3.order, f32[4,1,2048]{2,1,0:T(1,128)S(1)} %bitcast.74, bf16[2048,256]{1,0:T(8,128)(2,1)} %get-tuple-element.59.refs_0_, ...), custom_call_target="tpu_custom_call" | custom-call | flops 1073741824 | bytes 5242880 | tf_op jit(solution)/shard_map/project/pallas_call | solution.py:149
  231.7 6.7 %all-to-all-done.4.parts = bf16[4,64,896]{2,1,0:T(8,128)(2,1)} async-done(((bf16[4,64,896]{2,1,0:T(8,128)(2,1)}), bf16[4,64,896]{2,1,0:T(8,128)(2,1)}, u32[]{:S(2)}, u32[]{:S(2)}) %all-to-all-start.4) | async-done | bytes 458784 | tf_op jit(solution)/shard_map/all_to_all | solution.py:44
  243.7 4.9 collective-permute-done.17.second
  248.6 5.8 %collective-permute-done.18.third = bf16[64,512]{1,0:T(8,128)(2,1)S(1)} collective-permute-done((bf16[64,512]{1,0:T(8,128)(2,1)S(1)}, bf16[64,512]{1,0:T(8,128)(2,1)S(1)}, u32[]{:S(2)}, u32[]{:S(2)}) %collective-permute-start.18) | collective-permute-done | bytes 65568 | tf_op jit(solution)/shard_map/ppermute | solution.py:25
  262.1 17.9 %all_to_all.80 = bf16[16,16,2048]{2,1,0:T(8,128)(2,1)S(1)} all-to-all(bf16[16,16,2048]{2,1,0:T(8,128)(2,1)S(1)} %output_terms.4), channel_id=1, replica_groups={{0,2,4,6,8,10,12,14,16,18,20,22,24,26,28,30},{1,3,5,7,9,11,13,15,17,19,..., dimensions={0} | all-to-all | bytes 2097152 | tf_op jit(solution)/shard_map/all_to_all | solution.py:38
  286.4 13.8 %all-to-all-done.6.rows = bf16[16,16,2048]{2,1,0:T(8,128)(2,1)} async-done(((bf16[16,16,2048]{2,1,0:T(8,128)(2,1)}), bf16[16,16,2048]{2,1,0:T(8,128)(2,1)}, u32[]{:S(2)}, u32[]{:S(2)}) %all-to-all-start.6) | async-done | bytes 1048608 | tf_op jit(solution)/shard_map/all_to_all | solution.py:38
  305.0 5.5 %project.5 = bf16[4,64,896]{2,1,0:T(8,128)(2,1)S(1)} custom-call(s32[1]{0:T(128)} %bitcast.35.slot, bf16[16,16,2048]{2,1,0:T(8,128)(2,1)} %all-to-all-done.6.rows, bf16[256,256]{1,0:T(8,128)(2,1)S(1)} %fusion.3.order, f32[4,1,2048]{2,1,0:T(1,128)S(1)} %bitcast.75, bf16[2048,256]{1,0:T(8,128)(2,1)} %get-tuple-element.59.refs_0_, ...), custom_call_target="tpu_custom_call" | custom-call | flops 1073741824 | bytes 5242880 | tf_op jit(solution)/shard_map/project/pallas_call | solution.py:149
  310.6 20.4 %all_to_all.81.parts = bf16[4,64,896]{2,1,0:T(8,128)(2,1)S(1)} all-to-all(bf16[4,64,896]{2,1,0:T(8,128)(2,1)S(1)} %project.5), channel_id=1, replica_groups=mesh['section'=4,'tensor'=32] {'section'}, dimensions={0} | all-to-all | bytes 917504 | tf_op jit(solution)/shard_map/all_to_all | solution.py:44
  344.3 16.9 %all_to_all.82 = bf16[16,16,2048]{2,1,0:T(8,128)(2,1)S(1)} all-to-all(bf16[16,16,2048]{2,1,0:T(8,128)(2,1)S(1)} %output_terms.5), channel_id=1, replica_groups={{0,2,4,6,8,10,12,14,16,18,20,22,24,26,28,30},{1,3,5,7,9,11,13,15,17,19,..., dimensions={0} | all-to-all | bytes 2097152 | tf_op jit(solution)/shard_map/all_to_all | solution.py:38
  363.2 4.3 all-to-all-start.9
  367.6 13.3 %all-to-all-done.9.rows = bf16[16,16,2048]{2,1,0:T(8,128)(2,1)} async-done(((bf16[16,16,2048]{2,1,0:T(8,128)(2,1)}), bf16[16,16,2048]{2,1,0:T(8,128)(2,1)}, u32[]{:S(2)}, u32[]{:S(2)}) %all-to-all-start.9) | async-done | bytes 1048608 | tf_op jit(solution)/shard_map/all_to_all | solution.py:38
  385.7 5.6 %project.6 = bf16[4,64,896]{2,1,0:T(8,128)(2,1)S(1)} custom-call(s32[1]{0:T(128)} %bitcast.37.slot, bf16[16,16,2048]{2,1,0:T(8,128)(2,1)} %all-to-all-done.9.rows, bf16[256,256]{1,0:T(8,128)(2,1)S(1)} %fusion.3.order, f32[4,1,2048]{2,1,0:T(1,128)S(1)} %bitcast.76, bf16[2048,256]{1,0:T(8,128)(2,1)} %get-tuple-element.59.refs_0_, ...), custom_call_target="tpu_custom_call" | custom-call | flops 1073741824 | bytes 5242880 | tf_op jit(solution)/shard_map/project/pallas_call | solution.py:149
  391.3 11.7 %all_to_all.83.parts = bf16[4,64,896]{2,1,0:T(8,128)(2,1)S(1)} all-to-all(bf16[4,64,896]{2,1,0:T(8,128)(2,1)S(1)} %project.6), channel_id=1, replica_groups=mesh['section'=4,'tensor'=32] {'section'}, dimensions={0} | all-to-all | bytes 917504 | tf_op jit(solution)/shard_map/all_to_all | solution.py:44
  417.0 18.0 %all_to_all.84 = bf16[16,16,2048]{2,1,0:T(8,128)(2,1)S(1)} all-to-all(bf16[16,16,2048]{2,1,0:T(8,128)(2,1)S(1)} %output_terms.6), channel_id=1, replica_groups={{0,2,4,6,8,10,12,14,16,18,20,22,24,26,28,30},{1,3,5,7,9,11,13,15,17,19,..., dimensions={0} | all-to-all | bytes 2097152 | tf_op jit(solution)/shard_map/all_to_all | solution.py:38
  441.4 13.3 %all-to-all-done.12.rows = bf16[16,16,2048]{2,1,0:T(8,128)(2,1)} async-done(((bf16[16,16,2048]{2,1,0:T(8,128)(2,1)}), bf16[16,16,2048]{2,1,0:T(8,128)(2,1)}, u32[]{:S(2)}, u32[]{:S(2)}) %all-to-all-start.12) | async-done | bytes 1048608 | tf_op jit(solution)/shard_map/all_to_all | solution.py:38
  459.6 5.5 %project.7 = bf16[4,64,896]{2,1,0:T(8,128)(2,1)S(1)} custom-call(s32[1]{0:T(128)} %bitcast.39.slot, bf16[16,16,2048]{2,1,0:T(8,128)(2,1)} %all-to-all-done.12.rows, bf16[256,256]{1,0:T(8,128)(2,1)S(1)} %fusion.3.order, f32[4,1,2048]{2,1,0:T(1,128)S(1)} %bitcast.77, bf16[2048,256]{1,0:T(8,128)(2,1)} %get-tuple-element.59.refs_0_, ...), custom_call_target="tpu_custom_call" | custom-call | flops 1073741824 | bytes 5242880 | tf_op jit(solution)/shard_map/project/pallas_call | solution.py:149
  465.1 10.9 %all_to_all.85.parts = bf16[4,64,896]{2,1,0:T(8,128)(2,1)S(1)} all-to-all(bf16[4,64,896]{2,1,0:T(8,128)(2,1)S(1)} %project.7), channel_id=1, replica_groups=mesh['section'=4,'tensor'=32] {'section'}, dimensions={0} | all-to-all | bytes 917504 | tf_op jit(solution)/shard_map/all_to_all | solution.py:44
  489.3 16.0 %all_to_all.86 = bf16[16,16,2048]{2,1,0:T(8,128)(2,1)S(1)} all-to-all(bf16[16,16,2048]{2,1,0:T(8,128)(2,1)S(1)} %output_terms.7), channel_id=1, replica_groups={{0,2,4,6,8,10,12,14,16,18,20,22,24,26,28,30},{1,3,5,7,9,11,13,15,17,19,..., dimensions={0} | all-to-all | bytes 2097152 | tf_op jit(solution)/shard_map/all_to_all | solution.py:38
  505.6 9.7 %all_to_all.87 = f32[4,4,2048]{2,1,0:T(4,128)S(1)} all-to-all(f32[4,4,2048]{2,1,0:T(4,128)S(1)} %copy.55), channel_id=1, replica_groups=mesh['section'=4,'tensor'=32] {'section'}, dimensions={0} | all-to-all | bytes 262144 | tf_op jit(solution)/shard_map/all_to_all | solution.py:44
  (278 shorter events, 153.1 us)
Async XLA Ops:
  9.7 31.5 %all-to-all-start = ((bf16[32,24,256]{2,1,0:T(8,128)(2,1)}), bf16[32,24,256]{2,1,0:T(8,128)(2,1)S(1)}, u32[]{:S(2)}, u32[]{:S(2)}) async-start(bf16[32,24,256]{2,1,0:T(8,128)(2,1)} %pad_maximum_fusion.4), calls=%async_computation | async-start | bytes 786432 | tf_op jit(solution)/shard_map/all_to_all | solution.py:62
  22.5 18.7 %collective-permute-start = (bf16[1,128,2,1024]{1,3,2,0:T(8,128)(2,1)}, bf16[1,128,2,1024]{1,3,2,0:T(8,128)(2,1)}, u32[]{:S(2)}, u32[]{:S(2)}) collective-permute-start(bf16[1,128,2,1024]{1,3,2,0:T(8,128)(2,1)} %bitcast.6), channel_id=1, source_target_pairs={{0,32},{32,64},{64,96},{96,0},{1,33},{33,65},{65,97},{97,1},{2,34}... | collective-permute-start | bytes 1572872 | tf_op jit(solution)/shard_map/ppermute | solution.py:25
  25.3 26.1 %collective-permute-start.1 = (bf16[1,128,2,1024]{1,3,2,0:T(8,128)(2,1)}, bf16[1,128,2,1024]{1,3,2,0:T(8,128)(2,1)}, u32[]{:S(2)}, u32[]{:S(2)}) collective-permute-start(bf16[1,128,2,1024]{1,3,2,0:T(8,128)(2,1)} %bitcast.7), channel_id=1, source_target_pairs={{0,64},{32,96},{64,0},{96,32},{1,65},{33,97},{65,1},{97,33},{2,66}... | collective-permute-start | bytes 1572872 | tf_op jit(solution)/shard_map/ppermute | solution.py:25
  29.4 22.8 %collective-permute-start.2 = (bf16[1,128,2,1024]{1,3,2,0:T(8,128)(2,1)}, bf16[1,128,2,1024]{1,3,2,0:T(8,128)(2,1)}, u32[]{:S(2)}, u32[]{:S(2)}) collective-permute-start(bf16[1,128,2,1024]{1,3,2,0:T(8,128)(2,1)} %bitcast.8), channel_id=1, source_target_pairs={{0,96},{32,0},{64,32},{96,64},{1,97},{33,1},{65,33},{97,65},{2,98}... | collective-permute-start | bytes 1572872 | tf_op jit(solution)/shard_map/ppermute | solution.py:25
  35.1 38.1 %collective-permute-start.3 = (bf16[2048,256]{1,0:T(8,128)(2,1)}, bf16[2048,256]{1,0:T(8,128)(2,1)S(1)}, u32[]{:S(2)}, u32[]{:S(2)}) collective-permute-start(bf16[2048,256]{1,0:T(8,128)(2,1)} %get-tuple-element.61), channel_id=1, source_target_pairs={{0,32},{32,64},{64,96},{96,0},{1,33},{33,65},{65,97},{97,1},{2,34}... | collective-permute-start | bytes 3145736 | tf_op jit(solution)/shard_map/ppermute | solution.py:25
  35.7 38.8 %collective-permute-start.4 = (bf16[2048,256]{1,0:T(8,128)(2,1)}, bf16[2048,256]{1,0:T(8,128)(2,1)S(1)}, u32[]{:S(2)}, u32[]{:S(2)}) collective-permute-start(bf16[2048,256]{1,0:T(8,128)(2,1)} %get-tuple-element.60), channel_id=1, source_target_pairs={{0,96},{32,0},{64,32},{96,64},{1,97},{33,1},{65,33},{97,65},{2,98}... | collective-permute-start | bytes 3145736 | tf_op jit(solution)/shard_map/ppermute | solution.py:25
  55.2 33.3 %all-to-all-start.1 = ((bf16[32,88,256]{2,1,0:T(8,128)(2,1)}), bf16[32,88,256]{2,1,0:T(8,128)(2,1)S(1)}, u32[]{:S(2)}, u32[]{:S(2)}) async-start(bf16[32,88,256]{2,1,0:T(8,128)(2,1)} %copy.51), calls=%async_computation.1 | async-start | bytes 2883584 | tf_op jit(solution)/shard_map/all_to_all | solution.py:44
  94.1 89.3 %all-to-all-start.2 = ((bf16[16,4,2,128,128]{4,3,2,1,0:T(8,128)(2,1)}), bf16[16,4,2,128,128]{4,3,2,1,0:T(8,128)(2,1)}, u32[]{:S(2)}, u32[]{:S(2)}) async-start(bf16[16,4,2,128,128]{4,3,2,1,0:T(8,128)(2,1)} %bitcast.78), calls=%async_computation.2 | async-start | bytes 8388608 | tf_op jit(solution)/shard_map/all_to_all | solution.py:38
  102.5 75.4 %collective-permute-start.13 = (bf16[4,64,2048]{2,1,0:T(8,128)(2,1)}, bf16[4,64,2048]{2,1,0:T(8,128)(2,1)}, u32[]{:S(2)}, u32[]{:S(2)}) collective-permute-start(bf16[4,64,2048]{2,1,0:T(8,128)(2,1)} %bitcast.54), channel_id=1, source_target_pairs={{0,2},{1,3},{2,6},{3,7},{4,10},{5,11},{6,14},{7,15},{8,18},{9,19},... | collective-permute-start | bytes 3145736 | tf_op jit(solution)/shard_map/ppermute | solution.py:34
  104.3 73.6 %collective-permute-start.12 = (bf16[4,64,2048]{2,1,0:T(8,128)(2,1)}, bf16[4,64,2048]{2,1,0:T(8,128)(2,1)}, u32[]{:S(2)}, u32[]{:S(2)}) collective-permute-start(bf16[4,64,2048]{2,1,0:T(8,128)(2,1)} %bitcast.54), channel_id=1, source_target_pairs={{0,0},{1,1},{2,4},{3,5},{4,8},{5,9},{6,12},{7,13},{8,16},{9,17},{1... | collective-permute-start | bytes 3145736 | tf_op jit(solution)/shard_map/ppermute | solution.py:34
  113.8 69.4 %collective-permute-start.5 = (bf16[2048,256]{1,0:T(8,128)(2,1)}, bf16[2048,256]{1,0:T(8,128)(2,1)}, u32[]{:S(2)}, u32[]{:S(2)}) collective-permute-start(bf16[2048,256]{1,0:T(8,128)(2,1)} %get-tuple-element.62), channel_id=1, source_target_pairs={{0,64},{32,96},{64,0},{96,32},{1,65},{33,97},{65,1},{97,33},{2,66}... | collective-permute-start | bytes 3145736 | tf_op jit(solution)/shard_map/ppermute | solution.py:25
  116.4 80.6 %collective-permute-start.6 = (bf16[256,2048]{1,0:T(8,128)(2,1)}, bf16[256,2048]{1,0:T(8,128)(2,1)S(1)}, u32[]{:S(2)}, u32[]{:S(2)}) collective-permute-start(bf16[256,2048]{1,0:T(8,128)(2,1)} %get-tuple-element.57), channel_id=1, source_target_pairs={{0,32},{32,64},{64,96},{96,0},{1,33},{33,65},{65,97},{97,1},{2,34}... | collective-permute-start | bytes 3145736 | tf_op jit(solution)/shard_map/ppermute | solution.py:25
  119.8 77.5 %collective-permute-start.7 = (bf16[256,2048]{1,0:T(8,128)(2,1)}, bf16[256,2048]{1,0:T(8,128)(2,1)S(1)}, u32[]{:S(2)}, u32[]{:S(2)}) collective-permute-start(bf16[256,2048]{1,0:T(8,128)(2,1)} %get-tuple-element.56), channel_id=1, source_target_pairs={{0,96},{32,0},{64,32},{96,64},{1,97},{33,1},{65,33},{97,65},{2,98}... | collective-permute-start | bytes 3145736 | tf_op jit(solution)/shard_map/ppermute | solution.py:25
  181.0 16.6 %collective-permute-start.14 = (bf16[4,64,2048]{2,1,0:T(8,128)(2,1)}, bf16[4,64,2048]{2,1,0:T(8,128)(2,1)}, u32[]{:S(2)}, u32[]{:S(2)}) collective-permute-start(bf16[4,64,2048]{2,1,0:T(8,128)(2,1)} %get-tuple-element.66), channel_id=1, source_target_pairs={{0,1},{1,0},{2,3},{3,2},{4,5},{5,4},{6,7},{7,6},{8,9},{9,8},{10,11... | collective-permute-start | bytes 3145736 | tf_op jit(solution)/shard_map/ppermute | solution.py:29
  182.7 16.8 %collective-permute-start.15 = (bf16[4,64,2048]{2,1,0:T(8,128)(2,1)}, bf16[4,64,2048]{2,1,0:T(8,128)(2,1)}, u32[]{:S(2)}, u32[]{:S(2)}) collective-permute-start(bf16[4,64,2048]{2,1,0:T(8,128)(2,1)} %get-tuple-element.65), channel_id=1, source_target_pairs={{0,1},{1,0},{2,3},{3,2},{4,5},{5,4},{6,7},{7,6},{8,9},{9,8},{10,11... | collective-permute-start | bytes 3145736 | tf_op jit(solution)/shard_map/ppermute | solution.py:29
  183.3 32.3 %collective-permute-start.8 = (bf16[2048,256]{1,0:T(8,128)(2,1)}, bf16[2048,256]{1,0:T(8,128)(2,1)}, u32[]{:S(2)}, u32[]{:S(2)}) collective-permute-start(bf16[2048,256]{1,0:T(8,128)(2,1)} %get-tuple-element.59.refs_0_), channel_id=1, source_target_pairs={{0,1},{1,0},{2,3},{3,2},{4,5},{5,4},{6,7},{7,6},{8,9},{9,8},{10,11... | collective-permute-start | bytes 3145736 | tf_op jit(solution)/shard_map/ppermute | solution.py:29
  184.5 31.1 %all-to-all-start.3 = ((bf16[16,16,2048]{2,1,0:T(8,128)(2,1)}), bf16[16,16,2048]{2,1,0:T(8,128)(2,1)}, u32[]{:S(2)}, u32[]{:S(2)}) async-start(bf16[16,16,2048]{2,1,0:T(8,128)(2,1)} %broadcast_in_dim.82), calls=%async_computation.3 | async-start | bytes 2097152 | tf_op jit(solution)/shard_map/all_to_all | solution.py:38
  197.0 18.6 %collective-permute-start.9 = (bf16[2048,256]{1,0:T(8,128)(2,1)}, bf16[2048,256]{1,0:T(8,128)(2,1)}, u32[]{:S(2)}, u32[]{:S(2)}) collective-permute-start(bf16[2048,256]{1,0:T(8,128)(2,1)} %copy-done.30), channel_id=1, source_target_pairs={{0,1},{1,0},{2,3},{3,2},{4,5},{5,4},{6,7},{7,6},{8,9},{9,8},{10,11... | collective-permute-start | bytes 3145736 | tf_op jit(solution)/shard_map/ppermute | solution.py:29
  197.3 18.4 %collective-permute-start.11 = (bf16[2048,256]{1,0:T(8,128)(2,1)}, bf16[2048,256]{1,0:T(8,128)(2,1)}, u32[]{:S(2)}, u32[]{:S(2)}) collective-permute-start(bf16[2048,256]{1,0:T(8,128)(2,1)} %copy-done.35), channel_id=1, source_target_pairs={{0,1},{1,0},{2,3},{3,2},{4,5},{5,4},{6,7},{7,6},{8,9},{9,8},{10,11... | collective-permute-start | bytes 3145736 | tf_op jit(solution)/shard_map/ppermute | solution.py:29
  197.6 18.1 %collective-permute-start.10 = (bf16[2048,256]{1,0:T(8,128)(2,1)}, bf16[2048,256]{1,0:T(8,128)(2,1)}, u32[]{:S(2)}, u32[]{:S(2)}) collective-permute-start(bf16[2048,256]{1,0:T(8,128)(2,1)} %collective-permute-done.5.refs_2_), channel_id=1, source_target_pairs={{0,1},{1,0},{2,3},{3,2},{4,5},{5,4},{6,7},{7,6},{8,9},{9,8},{10,11... | collective-permute-start | bytes 3145736 | tf_op jit(solution)/shard_map/ppermute | solution.py:29
  199.5 32.2 %collective-permute-start.16 = (bf16[256,2048]{1,0:T(8,128)(2,1)}, bf16[256,2048]{1,0:T(8,128)(2,1)}, u32[]{:S(2)}, u32[]{:S(2)}) collective-permute-start(bf16[256,2048]{1,0:T(8,128)(2,1)} %get-tuple-element.55), channel_id=1, source_target_pairs={{0,64},{32,96},{64,0},{96,32},{1,65},{33,97},{65,1},{97,33},{2,66}... | collective-permute-start | bytes 3145736 | tf_op jit(solution)/shard_map/ppermute | solution.py:25
  225.9 12.5 %all-to-all-start.4 = ((bf16[4,64,896]{2,1,0:T(8,128)(2,1)}), bf16[4,64,896]{2,1,0:T(8,128)(2,1)}, u32[]{:S(2)}, u32[]{:S(2)}) async-start(bf16[4,64,896]{2,1,0:T(8,128)(2,1)} %copy-done.40), calls=%async_computation.4 | async-start | bytes 917504 | tf_op jit(solution)/shard_map/all_to_all | solution.py:44
  238.4 20.3 %collective-permute-start.20 = (bf16[256,2048]{1,0:T(8,128)(2,1)S(1)}, bf16[256,2048]{1,0:T(8,128)(2,1)S(1)}, u32[]{:S(2)}, u32[]{:S(2)}) collective-permute-start(bf16[256,2048]{1,0:T(8,128)(2,1)S(1)} %get-tuple-element.45.refs_0_), channel_id=1, source_target_pairs={{0,1},{1,0},{2,3},{3,2},{4,5},{5,4},{6,7},{7,6},{8,9},{9,8},{10,11... | collective-permute-start | bytes 3145736 | tf_op jit(solution)/shard_map/ppermute | solution.py:29
  238.4 20.3 %collective-permute-start.21 = (bf16[256,2048]{1,0:T(8,128)(2,1)}, bf16[256,2048]{1,0:T(8,128)(2,1)S(1)}, u32[]{:S(2)}, u32[]{:S(2)}) collective-permute-start(bf16[256,2048]{1,0:T(8,128)(2,1)} %copy-done.4), channel_id=1, source_target_pairs={{0,1},{1,0},{2,3},{3,2},{4,5},{5,4},{6,7},{7,6},{8,9},{9,8},{10,11... | collective-permute-start | bytes 3145736 | tf_op jit(solution)/shard_map/ppermute | solution.py:29
  238.9 19.8 %collective-permute-start.22 = (bf16[256,2048]{1,0:T(8,128)(2,1)}, bf16[256,2048]{1,0:T(8,128)(2,1)S(1)}, u32[]{:S(2)}, u32[]{:S(2)}) collective-permute-start(bf16[256,2048]{1,0:T(8,128)(2,1)} %collective-permute-done.16.refs_2_), channel_id=1, source_target_pairs={{0,1},{1,0},{2,3},{3,2},{4,5},{5,4},{6,7},{7,6},{8,9},{9,8},{10,11... | collective-permute-start | bytes 3145736 | tf_op jit(solution)/shard_map/ppermute | solution.py:29
  238.9 19.8 %collective-permute-start.23 = (bf16[256,2048]{1,0:T(8,128)(2,1)}, bf16[256,2048]{1,0:T(8,128)(2,1)S(1)}, u32[]{:S(2)}, u32[]{:S(2)}) collective-permute-start(bf16[256,2048]{1,0:T(8,128)(2,1)} %copy-done.9), channel_id=1, source_target_pairs={{0,1},{1,0},{2,3},{3,2},{4,5},{5,4},{6,7},{7,6},{8,9},{9,8},{10,11... | collective-permute-start | bytes 3145736 | tf_op jit(solution)/shard_map/ppermute | solution.py:29
  248.6 5.8 %collective-permute-start.18 = (bf16[64,512]{1,0:T(8,128)(2,1)S(1)}, bf16[64,512]{1,0:T(8,128)(2,1)S(1)}, u32[]{:S(2)}, u32[]{:S(2)}) collective-permute-start(bf16[64,512]{1,0:T(8,128)(2,1)S(1)} %attend.4.first), channel_id=1, source_target_pairs={{0,64},{32,96},{64,0},{96,32},{1,65},{33,97},{65,1},{97,33},{2,66}... | collective-permute-start | bytes 196616 | tf_op jit(solution)/shard_map/ppermute | solution.py:25
  282.0 18.2 %all-to-all-start.6 = ((bf16[16,16,2048]{2,1,0:T(8,128)(2,1)}), bf16[16,16,2048]{2,1,0:T(8,128)(2,1)}, u32[]{:S(2)}, u32[]{:S(2)}) async-start(bf16[16,16,2048]{2,1,0:T(8,128)(2,1)} %broadcast_in_dim.85), calls=%async_computation.6 | async-start | bytes 2097152 | tf_op jit(solution)/shard_map/all_to_all | solution.py:38
  334.6 5.8 %collective-permute-start.25 = (bf16[64,512]{1,0:T(8,128)(2,1)S(1)}, bf16[64,512]{1,0:T(8,128)(2,1)S(1)}, u32[]{:S(2)}, u32[]{:S(2)}) collective-permute-start(bf16[64,512]{1,0:T(8,128)(2,1)S(1)} %attend.5.first), channel_id=1, source_target_pairs={{0,64},{32,96},{64,0},{96,32},{1,65},{33,97},{65,1},{97,33},{2,66}... | collective-permute-start | bytes 196616 | tf_op jit(solution)/shard_map/ppermute | solution.py:25
  363.2 17.7 %all-to-all-start.9 = ((bf16[16,16,2048]{2,1,0:T(8,128)(2,1)}), bf16[16,16,2048]{2,1,0:T(8,128)(2,1)}, u32[]{:S(2)}, u32[]{:S(2)}) async-start(bf16[16,16,2048]{2,1,0:T(8,128)(2,1)} %broadcast_in_dim.86), calls=%async_computation.9 | async-start | bytes 2097152 | tf_op jit(solution)/shard_map/all_to_all | solution.py:38
  406.7 5.8 %collective-permute-start.28 = (bf16[64,512]{1,0:T(8,128)(2,1)S(1)}, bf16[64,512]{1,0:T(8,128)(2,1)S(1)}, u32[]{:S(2)}, u32[]{:S(2)}) collective-permute-start(bf16[64,512]{1,0:T(8,128)(2,1)S(1)} %attend.6.first), channel_id=1, source_target_pairs={{0,64},{32,96},{64,0},{96,32},{1,65},{33,97},{65,1},{97,33},{2,66}... | collective-permute-start | bytes 196616 | tf_op jit(solution)/shard_map/ppermute | solution.py:25
  437.1 17.7 %all-to-all-start.12 = ((bf16[16,16,2048]{2,1,0:T(8,128)(2,1)}), bf16[16,16,2048]{2,1,0:T(8,128)(2,1)}, u32[]{:S(2)}, u32[]{:S(2)}) async-start(bf16[16,16,2048]{2,1,0:T(8,128)(2,1)} %broadcast_in_dim.87), calls=%async_computation.12 | async-start | bytes 2097152 | tf_op jit(solution)/shard_map/all_to_all | solution.py:38
  (74 other events, 749.8 us)

commit v4 on v3

--- a/solution.py
+++ b/solution.py
@@ -50,7 +50,7 @@
     return [part.astype(BF16) for part in (high, middle, values - high - middle)]
 
 
-def embed(token_ids, embedding, prefix_lengths, norm_gain, kv_mat, cached, section_pos, core):
+def embed(token_ids, embedding, prefix_lengths, norm_gain, early, section_pos, core):
     vocab_part, width = embedding.shape
     local_ids = token_ids.T.reshape(-1) - section_pos * vocab_part
     inside = (local_ids >= 0) & (local_ids < vocab_part)
@@ -59,23 +59,21 @@
     picked = picked.reshape(CHIPS * CORES, 16, width)
     extra = jnp.pad(prefix_lengths.astype(BF16)[None, :], ((0, 7), (0, width - 4)))
     extra = jnp.broadcast_to(extra[None], (CHIPS * CORES, 8, width))
-    by_row = lax.all_to_all(
-        jnp.concatenate([picked, extra], axis=1), "tensor", split_axis=0, concat_axis=0, tiled=True
-    )
+    picked = jnp.concatenate([picked, extra], axis=1)
+    kv_mine, cached = early
+    picked, kv_mine = lax.optimization_barrier((picked, kv_mine))
+    by_row = lax.all_to_all(picked, "tensor", split_axis=0, concat_axis=0, tiled=True)
+    by_row, cached = lax.optimization_barrier((by_row, cached))
     lengths = by_row[:, 16, :4].reshape(CHIPS, CORES, 4)
     lengths = lax.dynamic_index_in_dim(lengths, core, 1, keepdims=False)
     lengths = lax.dynamic_index_in_dim(lengths, section_pos, 1, keepdims=False)
     gains = jnp.stack(in_three(norm_gain.reshape(CHIPS * CORES, width)), axis=1)
     gains = jnp.pad(gains, ((0, 0), (0, 5), (0, 0)))
-    by_row, cached = lax.optimization_barrier((by_row, cached))
-    kv_mat = kv_mat.reshape(64, CHIPS * CORES, width).transpose(1, 0, 2)
-    by_quarter = section_exchange(jnp.concatenate([by_row[:, :16], gains, kv_mat], axis=1))
-    by_quarter = by_quarter.reshape(SECTIONS, 8, 88, width)
-    kv_mine = by_quarter[:, :, 24:].transpose(0, 2, 1, 3).reshape(SECTIONS, 64, -1)
-    by_quarter = by_quarter[:, :, :24].astype(F32)
+    by_quarter = section_exchange(jnp.concatenate([by_row[:, :16], gains], axis=1))
+    by_quarter = by_quarter.reshape(SECTIONS, 8, 24, width).astype(F32)
     columns = jnp.sum(by_quarter[:, :, :16], axis=0).transpose(1, 0, 2).reshape(16, -1)
     gains = (by_quarter[:, :, 16] + by_quarter[:, :, 17]) + by_quarter[:, :, 18]
-    return columns, gains.reshape(SECTIONS, 1, -1), lengths.astype(jnp.int32), kv_mine, cached
+    return columns, gains.reshape(SECTIONS, 1, -1), lengths.astype(jnp.int32), (kv_mine, cached)
 
 
 def row_orders(section_pos):
@@ -93,9 +91,30 @@
 SENT = WIDTH + 3 * HD
 
 
-def project_kernel(slot, rows, order, gain, *refs):
-    wq_mine, wq_other = refs[:SECTIONS], refs[SECTIONS : 2 * SECTIONS]
-    keys_t, values_t, out, total = refs[2 * SECTIONS :]
+def by_head_kernel(first, second, third, fourth, out):
+    for d, piece in enumerate((first, second, third, fourth)):
+        for p in range(CHIPS):
+            for i in range(2):
+                start = 1024 * i + HD * (p // 2)
+                out[p, d, i] = piece[:, start : start + HD]
+
+
+def by_head(pieces):
+    whole = pl.BlockSpec(pieces[0].shape, lambda i: (0, 0))
+    shape = (CHIPS, SECTIONS, 2, 128, HD)
+    return pl.pallas_call(
+        by_head_kernel,
+        grid=(1,),
+        in_specs=[whole] * SECTIONS,
+        out_specs=pl.BlockSpec(shape, lambda i: (0, 0, 0, 0, 0)),
+        out_shape=jax.ShapeDtypeStruct(shape, BF16),
+        compiler_params=pltpu.CompilerParams(vmem_limit_bytes=32 * 2**20),
+        cost_estimate=pl.CostEstimate(flops=0, bytes_accessed=7 * 2**20, transcendentals=0),
+        name="by_head",
+    )(*pieces)
+
+
+def project_kernel(slot, rows, order, gain, wq_mine, wq_other, keys_t, values_t, out, total):
     step = pl.program_id(0)
 
     @pl.when(step == 0)
@@ -106,13 +125,8 @@
     block = jnp.dot(order[...], block, preferred_element_type=F32).astype(BF16)
     plain = block.astype(F32) / gain[...]
     half = WIDTH // 2
-    for d in range(SECTIONS):
-
-        @pl.when(slot[0] == d)
-        def _():
-            total[:, :half] += jnp.dot(block, wq_mine[d][...], preferred_element_type=F32)
-            total[:, half:WIDTH] += jnp.dot(block, wq_other[d][...], preferred_element_type=F32)
-
+    total[:, :half] += jnp.dot(block, wq_mine[...], preferred_element_type=F32)
+    total[:, half:WIDTH] += jnp.dot(block, wq_other[...], preferred_element_type=F32)
     for start, weight in ((WIDTH, keys_t), (WIDTH + HD, values_t)):
         total[:, start : start + HD] += lax.dot_general(
             block, weight[...], TRANSPOSED, preferred_element_type=F32
@@ -134,18 +148,10 @@
             out[j, :, WIDTH + 2 * HD :] = parts[own].astype(BF16)
 
 
-def chosen(d, k, slot):
-    return jnp.where(slot[0] == d, k, 0)
-
-
 def project(rows, order, gain, layer, slot, wq_mine, wq_other, keys_t, values_t):
     quarter = rows.shape[2]
     chunk = quarter // 4
     flops = 2 * 256 * quarter * (256 + WIDTH + 2 * HD)
-    pieces = [
-        pl.BlockSpec((chunk, 256), lambda k, slot, d=d: (chosen(d, k, slot), 0))
-        for d in range(SECTIONS)
-    ]
     return pl.pallas_call(
         project_kernel,
         grid_spec=pltpu.PrefetchScalarGridSpec(
@@ -155,19 +161,19 @@
                 pl.BlockSpec((CHIPS, 16, chunk), lambda k, slot: (0, 0, k)),
                 pl.BlockSpec((256, 256), lambda k, slot: (0, 0)),
                 pl.BlockSpec((None, 1, chunk), lambda k, slot: (layer, 0, k)),
-                *pieces,
-                *pieces,
-                pl.BlockSpec((None, HD, chunk), lambda k, slot: (layer, 0, k)),
-                pl.BlockSpec((None, HD, chunk), lambda k, slot: (layer, 0, k)),
+                pl.BlockSpec((chunk, 256), lambda k, slot: (k, 0)),
+                pl.BlockSpec((chunk, 256), lambda k, slot: (k, 0)),
+                pl.BlockSpec((HD, chunk), lambda k, slot: (0, k)),
+                pl.BlockSpec((HD, chunk), lambda k, slot: (0, k)),
             ],
             out_specs=pl.BlockSpec((SECTIONS, 64, SENT), lambda k, slot: (0, 0, 0)),
             scratch_shapes=[pltpu.VMEM((256, SENT), F32)],
         ),
         out_shape=jax.ShapeDtypeStruct((SECTIONS, 64, SENT), BF16),
-        compiler_params=pltpu.CompilerParams(vmem_limit_bytes=32 * 2**20),
+        compiler_params=pltpu.CompilerParams(vmem_limit_bytes=24 * 2**20),
         cost_estimate=pl.CostEstimate(flops=flops, bytes_accessed=5 * 2**20, transcendentals=0),
         name="project",
-    )(slot, rows, order, gain, *wq_mine, *wq_other, keys_t, values_t)
+    )(slot, rows, order, gain, wq_mine, wq_other, keys_t, values_t)
 
 
 def attend_kernel(slot, parts, cosine, sine, bias, cache, out):
@@ -240,51 +246,42 @@
     )(slot, parts, cosine, sine, bias, cache)
 
 
-def output_kernel(slot, first, second, third, fourth, order, *refs):
-    wo_mine, wo_other = refs[:SECTIONS], refs[SECTIONS : 2 * SECTIONS]
-    out, ordered = refs[2 * SECTIONS :]
-
+def output_kernel(slot, first, second, third, fourth, order, wo_mine, wo_other, out, ordered):
     @pl.when(pl.program_id(0) == 0)
     def _():
         mixed = jnp.concatenate([first[...], second[...], third[...], fourth[...]], axis=0)
         ordered[...] = jnp.dot(order[...], mixed, preferred_element_type=F32).astype(BF16)
 
     half = WIDTH // 2
-    for d in range(SECTIONS):
-
-        @pl.when(slot[0] == d)
-        def _():
-            terms = jnp.dot(ordered[:, :half], wo_mine[d][...], preferred_element_type=F32)
-            terms = terms + jnp.dot(
-                ordered[:, half:], wo_other[d][...], preferred_element_type=F32
-            )
-            out[...] = terms.astype(BF16).reshape(out.shape)
+    terms = jnp.dot(ordered[:, :half], wo_mine[...], preferred_element_type=F32)
+    terms = terms + jnp.dot(ordered[:, half:], wo_other[...], preferred_element_type=F32)
+    out[...] = terms.astype(BF16).reshape(out.shape)
 
 
 def output_terms(gathered, order, slot, wo_mine, wo_other):
-    quarter = wo_mine[0].shape[1]
+    quarter = wo_mine.shape[1]
     chunk = quarter // 4
-    pieces = [
-        pl.BlockSpec((256, chunk), lambda n, slot, d=d: (0, chosen(d, n, slot)))
-        for d in range(SECTIONS)
-    ]
     return pl.pallas_call(
         output_kernel,
         grid_spec=pltpu.PrefetchScalarGridSpec(
             num_scalar_prefetch=1,
             grid=(quarter // chunk,),
             in_specs=[pl.BlockSpec((64, WIDTH), lambda n, slot: (0, 0))] * SECTIONS
-            + [pl.BlockSpec((256, 256), lambda n, slot: (0, 0)), *pieces, *pieces],
+            + [
+                pl.BlockSpec((256, 256), lambda n, slot: (0, 0)),
+                pl.BlockSpec((256, chunk), lambda n, slot: (0, n)),
+                pl.BlockSpec((256, chunk), lambda n, slot: (0, n)),
+            ],
             out_specs=pl.BlockSpec((CHIPS, 16, chunk), lambda n, slot: (0, 0, n)),
             scratch_shapes=[pltpu.VMEM((256, WIDTH), BF16)],
         ),
         out_shape=jax.ShapeDtypeStruct((CHIPS, 16, quarter), BF16),
-        compiler_params=pltpu.CompilerParams(vmem_limit_bytes=32 * 2**20),
+        compiler_params=pltpu.CompilerParams(vmem_limit_bytes=24 * 2**20),
         cost_estimate=pl.CostEstimate(
             flops=2 * 256 * WIDTH * quarter, bytes_accessed=4 * 2**20, transcendentals=0
         ),
         name="output_terms",
-    )(slot, *gathered, order, *wo_mine, *wo_other)
+    )(slot, *gathered, order, wo_mine, wo_other)
 
 
 def body(
@@ -302,31 +299,47 @@
     core, chip = tensor_pos % CORES, tensor_pos // CORES
     quarter = query_weight.shape[1] // SECTIONS
 
+    def own(array, axis, size, distance):
+        start = (section_pos + distance) % SECTIONS * size
+        return lax.dynamic_slice_in_dim(array, start, size, axis)
+
     def share(array, axis, size, distance):
-        start = (section_pos + distance) % SECTIONS * size
-        return section_send(lax.dynamic_slice_in_dim(array, start, size, axis), distance)
+        return section_send(own(array, axis, size, distance), distance)
 
     distances = range(SECTIONS)
-    wq_mine = [share(query_weight[0], 0, quarter, d) for d in distances]
-    cached = [share(prefix_cache[0], 0, 1, d) for d in distances]
-    hidden, gains, lengths, kv_mine, cached = embed(
+    kv_mine = [share(keyval_weight[0].T, 1, quarter, d) for d in distances]
+    rows_first = prefix_cache[0].reshape(SECTIONS, 128, -1)
+    cached = [section_send(own(rows_first, 0, 1, d)[0], d) for d in distances]
+    hidden, gains, lengths, (kv_mine, cached) = embed(
         token_ids,
         embedding,
         prefix_lengths,
         norm_gain,
-        keyval_weight[0].T,
-        cached,
+        (kv_mine, cached),
         section_pos,
         core,
     )
-    cached, wq_mine[1], wq_mine[3] = lax.optimization_barrier((cached, wq_mine[1], wq_mine[3]))
-    cached = [c.reshape(1, 128, 2, 8, HD).transpose(3, 0, 2, 1, 4) for c in cached]
-    cache = plane_exchange(jnp.repeat(jnp.concatenate(cached, axis=1), 2, axis=0))
-    hidden, cache, wq_mine[2] = lax.optimization_barrier((hidden, cache, wq_mine[2]))
-    wo_mine = [share(output_weight[0], 1, quarter, d) for d in distances]
-    wq_other = [core_swap(w) for w in wq_mine]
+    kv_mine = jnp.stack(kv_mine)
     first = chip_send(kv_mine, lambda p: 2 * p if p < 8 else 2 * (p - 8) + 1)
     second = chip_send(kv_mine, lambda p: 2 * p + 1 if p < 8 else 2 * (p - 8))
+    hidden, query_mat = lax.optimization_barrier((hidden, query_weight[0]))
+    wq_mine = [share(query_mat, 0, quarter, d) if d != 2 else None for d in distances]
+
+    def gather_rows(layer):
+        scaled = (hidden * gains[layer]).astype(BF16)
+        return plane_exchange(jnp.broadcast_to(scaled[None], (CHIPS, 16, quarter)))
+
+    rows = gather_rows(0)
+    rows, cached, first, second, wq_mine[1], wq_mine[3], query_mat = lax.optimization_barrier(
+        (rows, cached, first, second, wq_mine[1], wq_mine[3], query_mat)
+    )
+    wq_mine[2] = share(query_mat, 0, quarter, 2)
+    cache = plane_exchange(by_head(cached))
+    wq_mine, output_mat = lax.optimization_barrier((wq_mine, output_weight[0]))
+    wo_mine = [share(output_mat, 1, quarter, d) for d in distances]
+    wq_other = jnp.stack([core_swap(w) for w in wq_mine])
+    wq_mine = jnp.stack(wq_mine)
+    wq_mine, wq_other = lax.optimization_barrier((wq_mine, wq_other))
     even = chip % 2 == 0
     heads_t = []
     for half in (jnp.where(even, first, second), jnp.where(even, second, first)):
@@ -336,12 +349,6 @@
         heads_t.append(jnp.concatenate([low, high], axis=1))
     keys_t, values_t = heads_t
 
-    def gather_rows(layer):
-        scaled = (hidden * gains[layer]).astype(BF16)
-        return plane_exchange(jnp.broadcast_to(scaled[None], (CHIPS, 16, quarter)))
-
-    rows = gather_rows(0)
-    rows, wo_mine[1], wo_mine[3] = lax.optimization_barrier((rows, wo_mine[1], wo_mine[3]))
     frequency = ROPE_BASE ** (-(jnp.arange(HD // 2, dtype=F32) * 2.0 / HD))
     positions = (lengths[:, None] + jnp.arange(STEPS)[None, :]).reshape(-1).astype(F32)
     angles = positions[:, None] * frequency[None, :]
@@ -355,16 +362,23 @@
 
     for layer in range(SECTIONS):
         slot = ((section_pos - layer) % SECTIONS).reshape(1)
+        pick = lambda held: lax.dynamic_index_in_dim(held, slot[0], 0, keepdims=False)
         if layer > 0:
             rows = gather_rows(layer)
-        partial = project(rows, forward, gains, layer, slot, wq_mine, wq_other, keys_t, values_t)
+        weights = [pick(w) for w in (wq_mine, wq_other, keys_t, values_t)]
+        partial = project(rows, forward, gains, layer, slot, *weights)
+        if layer == 0:
+            partial, cache = lax.optimization_barrier((partial, cache))
         parts = section_exchange(partial)
         if layer == 0:
             parts, wo_mine = lax.optimization_barrier((parts, wo_mine))
-            wo_other = [core_swap(w) for w in wo_mine]
+            wo_other = jnp.stack([core_swap(w) for w in wo_mine])
+            wo_mine = jnp.stack(wo_mine)
         mixed = attend(parts, cosine, sine, bias, cache, slot)
         gathered = [section_send(mixed, d) for d in distances]
-        terms = plane_exchange(output_terms(gathered, backward, slot, wo_mine, wo_other))
+        terms = plane_exchange(
+            output_terms(gathered, backward, slot, pick(wo_mine), pick(wo_other))
+        )
         hidden = hidden + jnp.sum(terms.astype(F32), axis=0)
 
     finals = section_exchange(hidden.reshape(4, STEPS, quarter).transpose(1, 0, 2))

time: 523 us -> 429 us (0.82)
  waiting for transfers between devices: 173 us -> 110 us
  blocking collectives: 121 us -> 166 us
  local copies, waits for them, and re-layouts: 61.4 us -> 34.2 us
  starting transfers between devices: 90.3 us -> 68.2 us
  Pallas kernels: 47.4 us -> 29.7 us
    all_to_all x4 -> x7, blocking collectives: 68.9 us -> 125 us  [plane_exchange(): lax.all_to_all(blocks, 'tensor', split_axis=0, concat_axis=0, tiled=True,...]
    ppermute x2, waiting for transfers between devices: 56.1 us -> 6.13 us  [chip_send(): return lax.ppermute(block, 'tensor', route)]
    all_to_all x5 -> x2, starting transfers between devices: 32.4 us -> 10.4 us  [plane_exchange(): lax.all_to_all(blocks, 'tensor', split_axis=0, concat_axis=0, tiled=True,...]
    unnamed x134 -> x47, local copies, waits for them, and re-layouts: 20.4 us -> 3.59 us
    all_to_all x4, blocking collectives: 52.6 us -> 40.4 us  [section_exchange(): lax.all_to_all(blocks, 'section', split_axis=0, concat_axis=0, tiled=True)]
    pallas_call x4, Pallas kernels: 22.1 us -> 10.7 us  [project(): pl.pallas_call(project_kernel, grid_spec=pltpu.PrefetchScalarGridSpec(num...]
    all_to_all x5 -> x2, waiting for transfers between devices: 52.7 us -> 43 us  [plane_exchange(): lax.all_to_all(blocks, 'tensor', split_axis=0, concat_axis=0, tiled=True,...]
    all_to_all x2, waiting for transfers between devices: 13.1 us -> 4.87 us  [section_exchange(): lax.all_to_all(blocks, 'section', split_axis=0, concat_axis=0, tiled=True)]
  transfers between devices with their start and end apart: 41 -> 41, of which waited for: 23 -> 21; matrix products, arithmetic and copies ran while one was open for 8% -> 10% of each run, Pallas kernels for 2% -> 1%
where the time goes in v4:
time: 429 us; the launch traced here: 427 us
  blocking collectives  166 us (39%)
  waiting for transfers between devices  110 us (26%)
  starting transfers between devices  68.2 us (16%)
  local copies, waits for them, and re-layouts  34.2 us (8%)
  Pallas kernels  29.7 us (7%)
  other arithmetic  18.4 us (4%)
    all_to_all x7, blocking collectives, plane_exchange(): lax.all_to_all(blocks, 'tensor', split_axis=0, concat_axis=0, tiled=True,...  125 us
    ppermute x24, waiting for transfers between devices, section_send(): return lax.ppermute(block, 'section', route)  47.6 us
    all_to_all x2, waiting for transfers between devices, plane_exchange(): lax.all_to_all(blocks, 'tensor', split_axis=0, concat_axis=0, tiled=True,...  43 us
    all_to_all x4, blocking collectives, section_exchange(): lax.all_to_all(blocks, 'section', split_axis=0, concat_axis=0, tiled=True)  40.4 us
    ppermute x24, starting transfers between devices, section_send(): return lax.ppermute(block, 'section', route)  29.7 us
    dynamic_slice x4, local copies, waits for them, and re-layouts, own(): return lax.dynamic_slice_in_dim(array, start, size, axis)  12.4 us
    pallas_call x4, Pallas kernels, attend(): pl.pallas_call(attend_kernel, grid_spec=pltpu.PrefetchScalarGridSpec(num_...  11.8 us
    pallas_call x4, Pallas kernels, project(): pl.pallas_call(project_kernel, grid_spec=pltpu.PrefetchScalarGridSpec(num...  10.7 us
  transfers between devices with their start and end apart: 41, of which 21 were waited for; matrix products, arithmetic and copies ran while one was open for 10% of the time, Pallas kernels for 1%

profile of v4, /device:TPU:0, one launch (start us, length us, event | category | flops | bytes accessed | tf_op | source)
XLA Modules:
  0.0 427.1 jit_solution(11010496958463311141)
XLA Ops:
  2.1 3.1 collective-permute-start.2
  7.4 3.3 reshape_squeeze.6
  16.6 5.9 %gather_fusion = bf16[512,256]{1,0:T(8,128)(2,1)S(1)} fusion(bf16[16032,256]{1,0:T(8,128)(2,1)} %param.9, s32[1024]{0:T(1024)S(1)} %pad_clamp_fusion), kind=kCustom, calls=%fused_computation | custom fusion | bytes 526336 | tf_op jit(solution)/shard_map/jit(_take)/gather | solution.py:57
  23.6 8.5 %collective-permute-done = bf16[64,2048]{1,0:T(8,128)(2,1)} collective-permute-done((bf16[64,2048]{1,0:T(8,128)(2,1)}, bf16[64,2048]{1,0:T(8,128)(2,1)}, u32[]{:S(2)}, u32[]{:S(2)}) %collective-permute-start) | collective-permute-done | bytes 262176 | tf_op jit(solution)/shard_map/ppermute | solution.py:25
  32.2 8.2 %all-to-all-start = ((bf16[32,24,256]{2,1,0:T(8,128)(2,1)}), bf16[32,24,256]{2,1,0:T(8,128)(2,1)S(1)}, u32[]{:S(2)}, u32[]{:S(2)}) async-start(bf16[32,24,256]{2,1,0:T(8,128)(2,1)} %pad_maximum_fusion.5), calls=%async_computation | async-start | bytes 786432 | tf_op jit(solution)/shard_map/all_to_all | solution.py:65
  42.5 8.2 %all-to-all-done = bf16[32,24,256]{2,1,0:T(8,128)(2,1)S(1)} async-done(((bf16[32,24,256]{2,1,0:T(8,128)(2,1)}), bf16[32,24,256]{2,1,0:T(8,128)(2,1)S(1)}, u32[]{:S(2)}, u32[]{:S(2)}) %all-to-all-start) | async-done | bytes 393248 | tf_op jit(solution)/shard_map/all_to_all | solution.py:65
  51.5 3.5 all-to-all-start.1
  57.8 9.5 %collective-permute-start.6 = (bf16[4,64,2048]{2,1,0:T(8,128)(2,1)}, bf16[4,64,2048]{2,1,0:T(8,128)(2,1)}, u32[]{:S(2)}, u32[]{:S(2)}) collective-permute-start(bf16[4,64,2048]{2,1,0:T(8,128)(2,1)} %pad_maximum_fusion.4), channel_id=1, source_target_pairs={{0,0},{1,1},{2,4},{3,5},{4,8},{5,9},{6,12},{7,13},{8,16},{9,17},{1... | collective-permute-start | bytes 3145736 | tf_op jit(solution)/shard_map/ppermute | solution.py:34
  67.5 3.6 constant_dynamic-slice_fusion.6
  71.1 3.2 collective-permute-start.9
  75.4 3.7 all-to-all-start.2
  79.1 6.1 %collective-permute-done.7 = bf16[4,64,2048]{2,1,0:T(8,128)(2,1)} collective-permute-done((bf16[4,64,2048]{2,1,0:T(8,128)(2,1)}, bf16[4,64,2048]{2,1,0:T(8,128)(2,1)}, u32[]{:S(2)}, u32[]{:S(2)}) %collective-permute-start.7) | collective-permute-done | bytes 1048608 | tf_op jit(solution)/shard_map/ppermute | solution.py:34
  85.2 13.6 %all-to-all-done.2.rows = bf16[16,16,2048]{2,1,0:T(8,128)(2,1)S(1)} async-done(((bf16[16,16,2048]{2,1,0:T(8,128)(2,1)}), bf16[16,16,2048]{2,1,0:T(8,128)(2,1)S(1)}, u32[]{:S(2)}, u32[]{:S(2)}) %all-to-all-start.2) | async-done | bytes 1048608 | tf_op jit(solution)/shard_map/all_to_all | solution.py:38
  110.3 6.7 %all-to-all-start.3 = ((bf16[16,4,2,128,128]{4,3,2,1,0:T(8,128)(2,1)}), bf16[16,4,2,128,128]{4,3,2,1,0:T(8,128)(2,1)}, u32[]{:S(2)}, u32[]{:S(2)}) async-start(bf16[16,4,2,128,128]{4,3,2,1,0:T(8,128)(2,1)} %copy-done), calls=%async_computation.3 | async-start | bytes 8388608 | tf_op jit(solution)/shard_map/all_to_all | solution.py:38
  117.4 11.1 %collective-permute-done.10 = bf16[2048,256]{1,0:T(8,128)(2,1)} collective-permute-done((bf16[2048,256]{1,0:T(8,128)(2,1)}, bf16[2048,256]{1,0:T(8,128)(2,1)}, u32[]{:S(2)}, u32[]{:S(2)}) %collective-permute-start.10) | collective-permute-done | bytes 1048608 | tf_op jit(solution)/shard_map/ppermute | solution.py:25
  129.0 4.4 %constant_dynamic-slice_fusion.1 = (bf16[256,2048]{1,0:T(8,128)(2,1)}, bf16[256,2048]{1,0:T(8,128)(2,1)}, bf16[256,2048]{1,0:T(8,128)(2,1)}, bf16[256,2048]{1,0:T(8,128)(2,1)}) fusion(bf16[256,8192]{1,0:T(8,128)(2,1)} %bitcast.130, s32[]{:T(128)S(6)} %select_n.369, s32[]{:T(128)S(6)} %select_n.367, s32[]{:T(128)S(6)} %select_n.365, s32[]{:T(128)S(6)} %select_n.363), kind=kLoop, calls=%fused_computation.102 | loop fusion | bytes 8388624 | tf_op jit(solution)/shard_map/dynamic_slice | solution.py:304
  152.0 29.4 %all-to-all-done.3.cache = bf16[16,4,2,128,128]{4,3,2,1,0:T(8,128)(2,1)} async-done(((bf16[16,4,2,128,128]{4,3,2,1,0:T(8,128)(2,1)}), bf16[16,4,2,128,128]{4,3,2,1,0:T(8,128)(2,1)}, u32[]{:S(2)}, u32[]{:S(2)}) %all-to-all-start.3) | async-done | bytes 4194336 | tf_op jit(solution)/shard_map/all_to_all | solution.py:38
  181.4 4.1 all-to-all-start.4
  187.2 5.3 %collective-permute-done.17 = bf16[256,2048]{1,0:T(8,128)(2,1)} collective-permute-done((bf16[256,2048]{1,0:T(8,128)(2,1)}, bf16[256,2048]{1,0:T(8,128)(2,1)}, u32[]{:S(2)}, u32[]{:S(2)}) %collective-permute-start.17) | collective-permute-done | bytes 1048608 | tf_op jit(solution)/shard_map/ppermute | solution.py:25
  192.6 4.9 %all-to-all-done.4.parts = bf16[4,64,896]{2,1,0:T(8,128)(2,1)} async-done(((bf16[4,64,896]{2,1,0:T(8,128)(2,1)}), bf16[4,64,896]{2,1,0:T(8,128)(2,1)}, u32[]{:S(2)}, u32[]{:S(2)}) %all-to-all-start.4) | async-done | bytes 458784 | tf_op jit(solution)/shard_map/all_to_all | solution.py:44
  213.0 23.2 %all_to_all.80 = bf16[16,16,2048]{2,1,0:T(8,128)(2,1)S(1)} all-to-all(bf16[16,16,2048]{2,1,0:T(8,128)(2,1)S(1)} %output_terms.4), channel_id=1, replica_groups={{0,2,4,6,8,10,12,14,16,18,20,22,24,26,28,30},{1,3,5,7,9,11,13,15,17,19,..., dimensions={0} | all-to-all | bytes 2097152 | tf_op jit(solution)/shard_map/all_to_all | solution.py:38
  236.5 19.2 %all_to_all.81.rows = bf16[16,16,2048]{2,1,0:T(8,128)(2,1)S(1)} all-to-all(bf16[16,16,2048]{2,1,0:T(8,128)(2,1)S(1)} %broadcast_in_dim.81), channel_id=1, replica_groups={{0,2,4,6,8,10,12,14,16,18,20,22,24,26,28,30},{1,3,5,7,9,11,13,15,17,19,..., dimensions={0} | all-to-all | bytes 2097152 | tf_op jit(solution)/shard_map/all_to_all | solution.py:38
  258.4 10.1 %all_to_all.82.parts = bf16[4,64,896]{2,1,0:T(8,128)(2,1)S(1)} all-to-all(bf16[4,64,896]{2,1,0:T(8,128)(2,1)S(1)} %project.5), channel_id=1, replica_groups=mesh['section'=4,'tensor'=32] {'section'}, dimensions={0} | all-to-all | bytes 917504 | tf_op jit(solution)/shard_map/all_to_all | solution.py:44
  281.3 15.9 %all_to_all.83 = bf16[16,16,2048]{2,1,0:T(8,128)(2,1)S(1)} all-to-all(bf16[16,16,2048]{2,1,0:T(8,128)(2,1)S(1)} %output_terms.5), channel_id=1, replica_groups={{0,2,4,6,8,10,12,14,16,18,20,22,24,26,28,30},{1,3,5,7,9,11,13,15,17,19,..., dimensions={0} | all-to-all | bytes 2097152 | tf_op jit(solution)/shard_map/all_to_all | solution.py:38
  297.5 15.9 %all_to_all.84.rows = bf16[16,16,2048]{2,1,0:T(8,128)(2,1)S(1)} all-to-all(bf16[16,16,2048]{2,1,0:T(8,128)(2,1)S(1)} %broadcast_in_dim.82), channel_id=1, replica_groups={{0,2,4,6,8,10,12,14,16,18,20,22,24,26,28,30},{1,3,5,7,9,11,13,15,17,19,..., dimensions={0} | all-to-all | bytes 2097152 | tf_op jit(solution)/shard_map/all_to_all | solution.py:38
  316.2 11.1 %all_to_all.85.parts = bf16[4,64,896]{2,1,0:T(8,128)(2,1)S(1)} all-to-all(bf16[4,64,896]{2,1,0:T(8,128)(2,1)S(1)} %project.6), channel_id=1, replica_groups=mesh['section'=4,'tensor'=32] {'section'}, dimensions={0} | all-to-all | bytes 917504 | tf_op jit(solution)/shard_map/all_to_all | solution.py:44
  334.5 3.1 collective-permute-done.31.third
  340.0 19.6 %all_to_all.86 = bf16[16,16,2048]{2,1,0:T(8,128)(2,1)S(1)} all-to-all(bf16[16,16,2048]{2,1,0:T(8,128)(2,1)S(1)} %output_terms.6), channel_id=1, replica_groups={{0,2,4,6,8,10,12,14,16,18,20,22,24,26,28,30},{1,3,5,7,9,11,13,15,17,19,..., dimensions={0} | all-to-all | bytes 2097152 | tf_op jit(solution)/shard_map/all_to_all | solution.py:38
  359.9 15.6 %all_to_all.87.rows = bf16[16,16,2048]{2,1,0:T(8,128)(2,1)S(1)} all-to-all(bf16[16,16,2048]{2,1,0:T(8,128)(2,1)S(1)} %broadcast_in_dim.83), channel_id=1, replica_groups={{0,2,4,6,8,10,12,14,16,18,20,22,24,26,28,30},{1,3,5,7,9,11,13,15,17,19,..., dimensions={0} | all-to-all | bytes 2097152 | tf_op jit(solution)/shard_map/all_to_all | solution.py:38
  378.2 10.8 %all_to_all.88.parts = bf16[4,64,896]{2,1,0:T(8,128)(2,1)S(1)} all-to-all(bf16[4,64,896]{2,1,0:T(8,128)(2,1)S(1)} %project.7), channel_id=1, replica_groups=mesh['section'=4,'tensor'=32] {'section'}, dimensions={0} | all-to-all | bytes 917504 | tf_op jit(solution)/shard_map/all_to_all | solution.py:44
  401.8 15.9 %all_to_all.89 = bf16[16,16,2048]{2,1,0:T(8,128)(2,1)S(1)} all-to-all(bf16[16,16,2048]{2,1,0:T(8,128)(2,1)S(1)} %output_terms.7), channel_id=1, replica_groups={{0,2,4,6,8,10,12,14,16,18,20,22,24,26,28,30},{1,3,5,7,9,11,13,15,17,19,..., dimensions={0} | all-to-all | bytes 2097152 | tf_op jit(solution)/shard_map/all_to_all | solution.py:38
  418.1 8.4 %all_to_all.90 = f32[4,4,2048]{2,1,0:T(4,128)S(1)} all-to-all(f32[4,4,2048]{2,1,0:T(4,128)S(1)} %copy.43), channel_id=1, replica_groups=mesh['section'=4,'tensor'=32] {'section'}, dimensions={0} | all-to-all | bytes 262144 | tf_op jit(solution)/shard_map/all_to_all | solution.py:44
  (197 shorter events, 111.1 us)
Async XLA Ops:
  2.1 20.6 %collective-permute-start.2 = (bf16[64,2048]{1,0:T(8,128)(2,1)}, bf16[64,2048]{1,0:T(8,128)(2,1)}, u32[]{:S(2)}, u32[]{:S(2)}) collective-permute-start(bf16[64,2048]{1,0:T(8,128)(2,1)} %get-tuple-element.124), channel_id=1, source_target_pairs={{0,96},{32,0},{64,32},{96,64},{1,97},{33,1},{65,33},{97,65},{2,98}... | collective-permute-start | bytes 786440 | tf_op jit(solution)/shard_map/ppermute | solution.py:25
  5.2 27.0 %collective-permute-start = (bf16[64,2048]{1,0:T(8,128)(2,1)}, bf16[64,2048]{1,0:T(8,128)(2,1)}, u32[]{:S(2)}, u32[]{:S(2)}) collective-permute-start(bf16[64,2048]{1,0:T(8,128)(2,1)} %get-tuple-element.125), channel_id=1, source_target_pairs={{0,32},{32,64},{64,96},{96,0},{1,33},{33,65},{65,97},{97,1},{2,34}... | collective-permute-start | bytes 786440 | tf_op jit(solution)/shard_map/ppermute | solution.py:25
  5.2 27.0 %collective-permute-start.1 = (bf16[64,2048]{1,0:T(8,128)(2,1)}, bf16[64,2048]{1,0:T(8,128)(2,1)}, u32[]{:S(2)}, u32[]{:S(2)}) collective-permute-start(bf16[64,2048]{1,0:T(8,128)(2,1)} %get-tuple-element.127), channel_id=1, source_target_pairs={{0,64},{32,96},{64,0},{96,32},{1,65},{33,97},{65,1},{97,33},{2,66}... | collective-permute-start | bytes 786440 | tf_op jit(solution)/shard_map/ppermute | solution.py:25
  12.0 28.5 %collective-permute-start.5 = (bf16[128,2048]{1,0:T(8,128)(2,1)}, bf16[128,2048]{1,0:T(8,128)(2,1)S(1)}, u32[]{:S(2)}, u32[]{:S(2)}) collective-permute-start(bf16[128,2048]{1,0:T(8,128)(2,1)} %get-tuple-element.120), channel_id=1, source_target_pairs={{0,96},{32,0},{64,32},{96,64},{1,97},{33,1},{65,33},{97,65},{2,98}... | collective-permute-start | bytes 1572872 | tf_op jit(solution)/shard_map/ppermute | solution.py:25
  13.0 27.4 %collective-permute-start.4 = (bf16[128,2048]{1,0:T(8,128)(2,1)}, bf16[128,2048]{1,0:T(8,128)(2,1)S(1)}, u32[]{:S(2)}, u32[]{:S(2)}) collective-permute-start(bf16[128,2048]{1,0:T(8,128)(2,1)} %get-tuple-element.121), channel_id=1, source_target_pairs={{0,64},{32,96},{64,0},{96,32},{1,65},{33,97},{65,1},{97,33},{2,66}... | collective-permute-start | bytes 1572872 | tf_op jit(solution)/shard_map/ppermute | solution.py:25
  22.7 19.7 %collective-permute-start.3 = (bf16[128,2048]{1,0:T(8,128)(2,1)S(1)}, bf16[128,2048]{1,0:T(8,128)(2,1)S(1)}, u32[]{:S(2)}, u32[]{:S(2)}) collective-permute-start(bf16[128,2048]{1,0:T(8,128)(2,1)S(1)} %get-tuple-element.122), channel_id=1, source_target_pairs={{0,32},{32,64},{64,96},{96,0},{1,33},{33,65},{65,97},{97,1},{2,34}... | collective-permute-start | bytes 1572872 | tf_op jit(solution)/shard_map/ppermute | solution.py:25
  32.2 18.5 %all-to-all-start = ((bf16[32,24,256]{2,1,0:T(8,128)(2,1)}), bf16[32,24,256]{2,1,0:T(8,128)(2,1)S(1)}, u32[]{:S(2)}, u32[]{:S(2)}) async-start(bf16[32,24,256]{2,1,0:T(8,128)(2,1)} %pad_maximum_fusion.5), calls=%async_computation | async-start | bytes 786432 | tf_op jit(solution)/shard_map/all_to_all | solution.py:65
  51.5 15.7 %all-to-all-start.1 = ((bf16[32,24,256]{2,1,0:T(8,128)(2,1)}), bf16[32,24,256]{2,1,0:T(8,128)(2,1)S(1)}, u32[]{:S(2)}, u32[]{:S(2)}) async-start(bf16[32,24,256]{2,1,0:T(8,128)(2,1)} %fusion.17), calls=%async_computation.1 | async-start | bytes 786432 | tf_op jit(solution)/shard_map/all_to_all | solution.py:44
  57.2 28.0 %collective-permute-start.7 = (bf16[4,64,2048]{2,1,0:T(8,128)(2,1)}, bf16[4,64,2048]{2,1,0:T(8,128)(2,1)}, u32[]{:S(2)}, u32[]{:S(2)}) collective-permute-start(bf16[4,64,2048]{2,1,0:T(8,128)(2,1)} %pad_maximum_fusion.4), channel_id=1, source_target_pairs={{0,2},{1,3},{2,6},{3,7},{4,10},{5,11},{6,14},{7,15},{8,18},{9,19},... | collective-permute-start | bytes 3145736 | tf_op jit(solution)/shard_map/ppermute | solution.py:34
  57.8 27.5 %collective-permute-start.6 = (bf16[4,64,2048]{2,1,0:T(8,128)(2,1)}, bf16[4,64,2048]{2,1,0:T(8,128)(2,1)}, u32[]{:S(2)}, u32[]{:S(2)}) collective-permute-start(bf16[4,64,2048]{2,1,0:T(8,128)(2,1)} %pad_maximum_fusion.4), channel_id=1, source_target_pairs={{0,0},{1,1},{2,4},{3,5},{4,8},{5,9},{6,12},{7,13},{8,16},{9,17},{1... | collective-permute-start | bytes 3145736 | tf_op jit(solution)/shard_map/ppermute | solution.py:34
  71.1 27.8 %collective-permute-start.9 = (bf16[2048,256]{1,0:T(8,128)(2,1)}, bf16[2048,256]{1,0:T(8,128)(2,1)}, u32[]{:S(2)}, u32[]{:S(2)}) collective-permute-start(bf16[2048,256]{1,0:T(8,128)(2,1)} %get-tuple-element.104), channel_id=1, source_target_pairs={{0,96},{32,0},{64,32},{96,64},{1,97},{33,1},{65,33},{97,65},{2,98}... | collective-permute-start | bytes 3145736 | tf_op jit(solution)/shard_map/ppermute | solution.py:25
  74.3 26.2 %collective-permute-start.8 = (bf16[2048,256]{1,0:T(8,128)(2,1)}, bf16[2048,256]{1,0:T(8,128)(2,1)}, u32[]{:S(2)}, u32[]{:S(2)}) collective-permute-start(bf16[2048,256]{1,0:T(8,128)(2,1)} %get-tuple-element.105), channel_id=1, source_target_pairs={{0,32},{32,64},{64,96},{96,0},{1,33},{33,65},{65,97},{97,1},{2,34}... | collective-permute-start | bytes 3145736 | tf_op jit(solution)/shard_map/ppermute | solution.py:25
  75.4 23.4 %all-to-all-start.2 = ((bf16[16,16,2048]{2,1,0:T(8,128)(2,1)}), bf16[16,16,2048]{2,1,0:T(8,128)(2,1)S(1)}, u32[]{:S(2)}, u32[]{:S(2)}) async-start(bf16[16,16,2048]{2,1,0:T(8,128)(2,1)} %broadcast_in_dim.46), calls=%async_computation.2 | async-start | bytes 2097152 | tf_op jit(solution)/shard_map/all_to_all | solution.py:38
  102.8 25.8 %collective-permute-start.10 = (bf16[2048,256]{1,0:T(8,128)(2,1)}, bf16[2048,256]{1,0:T(8,128)(2,1)}, u32[]{:S(2)}, u32[]{:S(2)}) collective-permute-start(bf16[2048,256]{1,0:T(8,128)(2,1)} %constant_dynamic-slice_fusion.5), channel_id=1, source_target_pairs={{0,64},{32,96},{64,0},{96,32},{1,65},{33,97},{65,1},{97,33},{2,66}... | collective-permute-start | bytes 3145736 | tf_op jit(solution)/shard_map/ppermute | solution.py:25
  107.7 25.8 %collective-permute-start.16 = (bf16[4,64,2048]{2,1,0:T(8,128)(2,1)}, bf16[4,64,2048]{2,1,0:T(8,128)(2,1)}, u32[]{:S(2)}, u32[]{:S(2)}) collective-permute-start(bf16[4,64,2048]{2,1,0:T(8,128)(2,1)} %get-tuple-element.116), channel_id=1, source_target_pairs={{0,1},{1,0},{2,3},{3,2},{4,5},{5,4},{6,7},{7,6},{8,9},{9,8},{10,11... | collective-permute-start | bytes 3145736 | tf_op jit(solution)/shard_map/ppermute | solution.py:29
  110.3 71.1 %all-to-all-start.3 = ((bf16[16,4,2,128,128]{4,3,2,1,0:T(8,128)(2,1)}), bf16[16,4,2,128,128]{4,3,2,1,0:T(8,128)(2,1)}, u32[]{:S(2)}, u32[]{:S(2)}) async-start(bf16[16,4,2,128,128]{4,3,2,1,0:T(8,128)(2,1)} %copy-done), calls=%async_computation.3 | async-start | bytes 8388608 | tf_op jit(solution)/shard_map/all_to_all | solution.py:38
  117.1 18.5 %collective-permute-start.15 = (bf16[4,64,2048]{2,1,0:T(8,128)(2,1)S(1)}, bf16[4,64,2048]{2,1,0:T(8,128)(2,1)S(1)}, u32[]{:S(2)}, u32[]{:S(2)}) collective-permute-start(bf16[4,64,2048]{2,1,0:T(8,128)(2,1)S(1)} %copy-done.13), channel_id=1, source_target_pairs={{0,1},{1,0},{2,3},{3,2},{4,5},{5,4},{6,7},{7,6},{8,9},{9,8},{10,11... | collective-permute-start | bytes 3145736 | tf_op jit(solution)/shard_map/ppermute | solution.py:29
  128.5 14.8 %collective-permute-start.11 = (bf16[2048,256]{1,0:T(8,128)(2,1)}, bf16[2048,256]{1,0:T(8,128)(2,1)S(1)}, u32[]{:S(2)}, u32[]{:S(2)}) collective-permute-start(bf16[2048,256]{1,0:T(8,128)(2,1)} %get-tuple-element.57), channel_id=1, source_target_pairs={{0,1},{1,0},{2,3},{3,2},{4,5},{5,4},{6,7},{7,6},{8,9},{9,8},{10,11... | collective-permute-start | bytes 3145736 | tf_op jit(solution)/shard_map/ppermute | solution.py:29
  128.5 15.7 %collective-permute-start.12 = (bf16[2048,256]{1,0:T(8,128)(2,1)}, bf16[2048,256]{1,0:T(8,128)(2,1)S(1)}, u32[]{:S(2)}, u32[]{:S(2)}) collective-permute-start(bf16[2048,256]{1,0:T(8,128)(2,1)} %collective-permute-done.8), channel_id=1, source_target_pairs={{0,1},{1,0},{2,3},{3,2},{4,5},{5,4},{6,7},{7,6},{8,9},{9,8},{10,11... | collective-permute-start | bytes 3145736 | tf_op jit(solution)/shard_map/ppermute | solution.py:29
  129.0 16.1 %collective-permute-start.13 = (bf16[2048,256]{1,0:T(8,128)(2,1)}, bf16[2048,256]{1,0:T(8,128)(2,1)S(1)}, u32[]{:S(2)}, u32[]{:S(2)}) collective-permute-start(bf16[2048,256]{1,0:T(8,128)(2,1)} %collective-permute-done.10), channel_id=1, source_target_pairs={{0,1},{1,0},{2,3},{3,2},{4,5},{5,4},{6,7},{7,6},{8,9},{9,8},{10,11... | collective-permute-start | bytes 3145736 | tf_op jit(solution)/shard_map/ppermute | solution.py:29
  133.4 11.7 %collective-permute-start.14 = (bf16[2048,256]{1,0:T(8,128)(2,1)}, bf16[2048,256]{1,0:T(8,128)(2,1)S(1)}, u32[]{:S(2)}, u32[]{:S(2)}) collective-permute-start(bf16[2048,256]{1,0:T(8,128)(2,1)} %collective-permute-done.9), channel_id=1, source_target_pairs={{0,1},{1,0},{2,3},{3,2},{4,5},{5,4},{6,7},{7,6},{8,9},{9,8},{10,11... | collective-permute-start | bytes 3145736 | tf_op jit(solution)/shard_map/ppermute | solution.py:29
  135.6 51.6 %collective-permute-start.19 = (bf16[256,2048]{1,0:T(8,128)(2,1)}, bf16[256,2048]{1,0:T(8,128)(2,1)}, u32[]{:S(2)}, u32[]{:S(2)}) collective-permute-start(bf16[256,2048]{1,0:T(8,128)(2,1)} %get-tuple-element.99), channel_id=1, source_target_pairs={{0,96},{32,0},{64,32},{96,64},{1,97},{33,1},{65,33},{97,65},{2,98}... | collective-permute-start | bytes 3145736 | tf_op jit(solution)/shard_map/ppermute | solution.py:25
  143.3 43.9 %collective-permute-start.18 = (bf16[256,2048]{1,0:T(8,128)(2,1)}, bf16[256,2048]{1,0:T(8,128)(2,1)}, u32[]{:S(2)}, u32[]{:S(2)}) collective-permute-start(bf16[256,2048]{1,0:T(8,128)(2,1)} %get-tuple-element.100), channel_id=1, source_target_pairs={{0,64},{32,96},{64,0},{96,32},{1,65},{33,97},{65,1},{97,33},{2,66}... | collective-permute-start | bytes 3145736 | tf_op jit(solution)/shard_map/ppermute | solution.py:25
  144.2 48.3 %collective-permute-start.17 = (bf16[256,2048]{1,0:T(8,128)(2,1)}, bf16[256,2048]{1,0:T(8,128)(2,1)}, u32[]{:S(2)}, u32[]{:S(2)}) collective-permute-start(bf16[256,2048]{1,0:T(8,128)(2,1)} %get-tuple-element.101), channel_id=1, source_target_pairs={{0,32},{32,64},{64,96},{96,0},{1,33},{33,65},{65,97},{97,1},{2,34}... | collective-permute-start | bytes 3145736 | tf_op jit(solution)/shard_map/ppermute | solution.py:25
  181.4 16.0 %all-to-all-start.4 = ((bf16[4,64,896]{2,1,0:T(8,128)(2,1)}), bf16[4,64,896]{2,1,0:T(8,128)(2,1)}, u32[]{:S(2)}, u32[]{:S(2)}) async-start(bf16[4,64,896]{2,1,0:T(8,128)(2,1)} %copy-done.12), calls=%async_computation.4 | async-start | bytes 917504 | tf_op jit(solution)/shard_map/all_to_all | solution.py:44
  197.4 6.7 %collective-permute-start.23 = (bf16[256,2048]{1,0:T(8,128)(2,1)}, bf16[256,2048]{1,0:T(8,128)(2,1)S(1)}, u32[]{:S(2)}, u32[]{:S(2)}) collective-permute-start(bf16[256,2048]{1,0:T(8,128)(2,1)} %get-tuple-element.73), channel_id=1, source_target_pairs={{0,1},{1,0},{2,3},{3,2},{4,5},{5,4},{6,7},{7,6},{8,9},{9,8},{10,11... | collective-permute-start | bytes 3145736 | tf_op jit(solution)/shard_map/ppermute | solution.py:29
  197.4 7.6 %collective-permute-start.24 = (bf16[256,2048]{1,0:T(8,128)(2,1)}, bf16[256,2048]{1,0:T(8,128)(2,1)S(1)}, u32[]{:S(2)}, u32[]{:S(2)}) collective-permute-start(bf16[256,2048]{1,0:T(8,128)(2,1)} %collective-permute-done.17), channel_id=1, source_target_pairs={{0,1},{1,0},{2,3},{3,2},{4,5},{5,4},{6,7},{7,6},{8,9},{9,8},{10,11... | collective-permute-start | bytes 3145736 | tf_op jit(solution)/shard_map/ppermute | solution.py:29
  197.9 8.5 %collective-permute-start.25 = (bf16[256,2048]{1,0:T(8,128)(2,1)}, bf16[256,2048]{1,0:T(8,128)(2,1)S(1)}, u32[]{:S(2)}, u32[]{:S(2)}) collective-permute-start(bf16[256,2048]{1,0:T(8,128)(2,1)} %collective-permute-done.18), channel_id=1, source_target_pairs={{0,1},{1,0},{2,3},{3,2},{4,5},{5,4},{6,7},{7,6},{8,9},{9,8},{10,11... | collective-permute-start | bytes 3145736 | tf_op jit(solution)/shard_map/ppermute | solution.py:29
  198.0 8.5 %collective-permute-start.26 = (bf16[256,2048]{1,0:T(8,128)(2,1)}, bf16[256,2048]{1,0:T(8,128)(2,1)S(1)}, u32[]{:S(2)}, u32[]{:S(2)}) collective-permute-start(bf16[256,2048]{1,0:T(8,128)(2,1)} %collective-permute-done.19), channel_id=1, source_target_pairs={{0,1},{1,0},{2,3},{3,2},{4,5},{5,4},{6,7},{7,6},{8,9},{9,8},{10,11... | collective-permute-start | bytes 3145736 | tf_op jit(solution)/shard_map/ppermute | solution.py:29
  201.9 6.8 %collective-permute-start.22 = (bf16[64,512]{1,0:T(8,128)(2,1)S(1)}, bf16[64,512]{1,0:T(8,128)(2,1)S(1)}, u32[]{:S(2)}, u32[]{:S(2)}) collective-permute-start(bf16[64,512]{1,0:T(8,128)(2,1)S(1)} %attend.4.first), channel_id=1, source_target_pairs={{0,96},{32,0},{64,32},{96,64},{1,97},{33,1},{65,33},{97,65},{2,98}... | collective-permute-start | bytes 196616 | tf_op jit(solution)/shard_map/ppermute | solution.py:25
  204.2 6.0 %collective-permute-start.21 = (bf16[64,512]{1,0:T(8,128)(2,1)S(1)}, bf16[64,512]{1,0:T(8,128)(2,1)S(1)}, u32[]{:S(2)}, u32[]{:S(2)}) collective-permute-start(bf16[64,512]{1,0:T(8,128)(2,1)S(1)} %attend.4.first), channel_id=1, source_target_pairs={{0,64},{32,96},{64,0},{96,32},{1,65},{33,97},{65,1},{97,33},{2,66}... | collective-permute-start | bytes 196616 | tf_op jit(solution)/shard_map/ppermute | solution.py:25
  205.1 6.2 %collective-permute-start.20 = (bf16[64,512]{1,0:T(8,128)(2,1)S(1)}, bf16[64,512]{1,0:T(8,128)(2,1)S(1)}, u32[]{:S(2)}, u32[]{:S(2)}) collective-permute-start(bf16[64,512]{1,0:T(8,128)(2,1)S(1)} %attend.4.first), channel_id=1, source_target_pairs={{0,32},{32,64},{64,96},{96,0},{1,33},{33,65},{65,97},{97,1},{2,34}... | collective-permute-start | bytes 196616 | tf_op jit(solution)/shard_map/ppermute | solution.py:25
  (31 other events, 498.5 us)

commit v5 on v4

--- a/solution.py
+++ b/solution.py
@@ -60,10 +60,10 @@
     extra = jnp.pad(prefix_lengths.astype(BF16)[None, :], ((0, 7), (0, width - 4)))
     extra = jnp.broadcast_to(extra[None], (CHIPS * CORES, 8, width))
     picked = jnp.concatenate([picked, extra], axis=1)
-    kv_mine, cached = early
+    kv_mine, wq_mine = early
     picked, kv_mine = lax.optimization_barrier((picked, kv_mine))
     by_row = lax.all_to_all(picked, "tensor", split_axis=0, concat_axis=0, tiled=True)
-    by_row, cached = lax.optimization_barrier((by_row, cached))
+    by_row, wq_mine = lax.optimization_barrier((by_row, wq_mine))
     lengths = by_row[:, 16, :4].reshape(CHIPS, CORES, 4)
     lengths = lax.dynamic_index_in_dim(lengths, core, 1, keepdims=False)
     lengths = lax.dynamic_index_in_dim(lengths, section_pos, 1, keepdims=False)
@@ -73,7 +73,7 @@
     by_quarter = by_quarter.reshape(SECTIONS, 8, 24, width).astype(F32)
     columns = jnp.sum(by_quarter[:, :, :16], axis=0).transpose(1, 0, 2).reshape(16, -1)
     gains = (by_quarter[:, :, 16] + by_quarter[:, :, 17]) + by_quarter[:, :, 18]
-    return columns, gains.reshape(SECTIONS, 1, -1), lengths.astype(jnp.int32), (kv_mine, cached)
+    return columns, gains.reshape(SECTIONS, 1, -1), lengths.astype(jnp.int32), (kv_mine, wq_mine)
 
 
 def row_orders(section_pos):
@@ -308,30 +308,31 @@
 
     distances = range(SECTIONS)
     kv_mine = [share(keyval_weight[0].T, 1, quarter, d) for d in distances]
-    rows_first = prefix_cache[0].reshape(SECTIONS, 128, -1)
-    cached = [section_send(own(rows_first, 0, 1, d)[0], d) for d in distances]
-    hidden, gains, lengths, (kv_mine, cached) = embed(
+    wq_mine = [share(query_weight[0], 0, quarter, d) if d != 2 else None for d in distances]
+    hidden, gains, lengths, (kv_mine, (wq_mine[1], wq_mine[3])) = embed(
         token_ids,
         embedding,
         prefix_lengths,
         norm_gain,
-        (kv_mine, cached),
+        (kv_mine, (wq_mine[1], wq_mine[3])),
         section_pos,
         core,
     )
     kv_mine = jnp.stack(kv_mine)
     first = chip_send(kv_mine, lambda p: 2 * p if p < 8 else 2 * (p - 8) + 1)
     second = chip_send(kv_mine, lambda p: 2 * p + 1 if p < 8 else 2 * (p - 8))
-    hidden, query_mat = lax.optimization_barrier((hidden, query_weight[0]))
-    wq_mine = [share(query_mat, 0, quarter, d) if d != 2 else None for d in distances]
+    rows_first = prefix_cache[0].reshape(SECTIONS, 128, -1)
+    cached = [own(rows_first, 0, 1, d)[0] for d in distances]
+    hidden, cached = lax.optimization_barrier((hidden, cached))
+    cached = [section_send(piece, d) for d, piece in enumerate(cached)]
 
     def gather_rows(layer):
         scaled = (hidden * gains[layer]).astype(BF16)
         return plane_exchange(jnp.broadcast_to(scaled[None], (CHIPS, 16, quarter)))
 
     rows = gather_rows(0)
-    rows, cached, first, second, wq_mine[1], wq_mine[3], query_mat = lax.optimization_barrier(
-        (rows, cached, first, second, wq_mine[1], wq_mine[3], query_mat)
+    rows, cached, first, second, query_mat = lax.optimization_barrier(
+        (rows, cached, first, second, query_weight[0])
     )
     wq_mine[2] = share(query_mat, 0, quarter, 2)
     cache = plane_exchange(by_head(cached))

time: 429 us -> 425 us (level)
  waiting for transfers between devices: 110 us -> 99.7 us
  starting transfers between devices: 68.2 us -> 74.5 us
    all_to_all x2, waiting for transfers between devices: 43 us -> 30.8 us  [plane_exchange(): lax.all_to_all(blocks, 'tensor', split_axis=0, concat_axis=0, tiled=True,...]
    ppermute x24, waiting for transfers between devices: 47.6 us -> 54.4 us  [section_send(): return lax.ppermute(block, 'section', route)]
where the time goes in v5:
time: 425 us; the launch traced here: 423 us
  blocking collectives  166 us (39%)
  waiting for transfers between devices  99.7 us (23%)
  starting transfers between devices  74.5 us (18%)
  local copies, waits for them, and re-layouts  34.6 us (8%)
  Pallas kernels  29.7 us (7%)
  other arithmetic  17.3 us (4%)
    all_to_all x7, blocking collectives, plane_exchange(): lax.all_to_all(blocks, 'tensor', split_axis=0, concat_axis=0, tiled=True,...  126 us
    ppermute x24, waiting for transfers between devices, section_send(): return lax.ppermute(block, 'section', route)  54.4 us
    all_to_all x4, blocking collectives, section_exchange(): lax.all_to_all(blocks, 'section', split_axis=0, concat_axis=0, tiled=True)  40.4 us
    ppermute x24, starting transfers between devices, section_send(): return lax.ppermute(block, 'section', route)  31.4 us
    all_to_all x2, waiting for transfers between devices, plane_exchange(): lax.all_to_all(blocks, 'tensor', split_axis=0, concat_axis=0, tiled=True,...  30.8 us
    all_to_all x2, starting transfers between devices, plane_exchange(): lax.all_to_all(blocks, 'tensor', split_axis=0, concat_axis=0, tiled=True,...  14 us
    dynamic_slice x4, local copies, waits for them, and re-layouts, own(): return lax.dynamic_slice_in_dim(array, start, size, axis)  11.9 us
    pallas_call x4, Pallas kernels, attend(): pl.pallas_call(attend_kernel, grid_spec=pltpu.PrefetchScalarGridSpec(num_...  11.8 us
  transfers between devices with their start and end apart: 41, of which 21 were waited for; matrix products, arithmetic and copies ran while one was open for 10% of the time, Pallas kernels for 1%

profile of v5, /device:TPU:0, one launch (start us, length us, event | category | flops | bytes accessed | tf_op | source)
XLA Modules:
  0.0 423.0 jit_solution(1506056288495672828)
XLA Ops:
  1.3 3.2 collective-permute-start.2
  6.7 3.6 dynamic-slice_bitcast_fusion.16
  12.9 5.9 %gather_fusion = bf16[512,256]{1,0:T(8,128)(2,1)S(1)} fusion(bf16[16032,256]{1,0:T(8,128)(2,1)} %param.9, s32[1024]{0:T(1024)S(1)} %pad_clamp_fusion), kind=kCustom, calls=%fused_computation | custom fusion | bytes 526336 | tf_op jit(solution)/shard_map/jit(_take)/gather | solution.py:57
  19.9 8.2 %all-to-all-start = ((bf16[32,24,256]{2,1,0:T(8,128)(2,1)}), bf16[32,24,256]{2,1,0:T(8,128)(2,1)S(1)}, u32[]{:S(2)}, u32[]{:S(2)}) async-start(bf16[32,24,256]{2,1,0:T(8,128)(2,1)} %pad_maximum_fusion.5), calls=%async_computation | async-start | bytes 786432 | tf_op jit(solution)/shard_map/all_to_all | solution.py:65
  28.2 3.3 reshape_squeeze.6
  31.6 6.8 %all-to-all-done = bf16[32,24,256]{2,1,0:T(8,128)(2,1)S(1)} async-done(((bf16[32,24,256]{2,1,0:T(8,128)(2,1)}), bf16[32,24,256]{2,1,0:T(8,128)(2,1)S(1)}, u32[]{:S(2)}, u32[]{:S(2)}) %all-to-all-start) | async-done | bytes 393248 | tf_op jit(solution)/shard_map/all_to_all | solution.py:65
  38.4 3.2 collective-permute-done.3
  42.4 3.5 all-to-all-start.1
  50.0 9.5 %collective-permute-start.8 = (bf16[4,64,2048]{2,1,0:T(8,128)(2,1)}, bf16[4,64,2048]{2,1,0:T(8,128)(2,1)}, u32[]{:S(2)}, u32[]{:S(2)}) collective-permute-start(bf16[4,64,2048]{2,1,0:T(8,128)(2,1)} %pad_maximum_fusion.4), channel_id=1, source_target_pairs={{0,0},{1,1},{2,4},{3,5},{4,8},{5,9},{6,12},{7,13},{8,16},{9,17},{1... | collective-permute-start | bytes 3145736 | tf_op jit(solution)/shard_map/ppermute | solution.py:34
  61.4 6.9 %all-to-all-start.2 = ((bf16[16,16,2048]{2,1,0:T(8,128)(2,1)}), bf16[16,16,2048]{2,1,0:T(8,128)(2,1)S(1)}, u32[]{:S(2)}, u32[]{:S(2)}) async-start(bf16[16,16,2048]{2,1,0:T(8,128)(2,1)} %broadcast_in_dim.46), calls=%async_computation.2 | async-start | bytes 2097152 | tf_op jit(solution)/shard_map/all_to_all | solution.py:38
  77.4 6.5 %collective-permute-done.5.second = bf16[128,2048]{1,0:T(8,128)(2,1)S(1)} collective-permute-done((bf16[128,2048]{1,0:T(8,128)(2,1)}, bf16[128,2048]{1,0:T(8,128)(2,1)S(1)}, u32[]{:S(2)}, u32[]{:S(2)}) %collective-permute-start.5) | collective-permute-done | bytes 524320 | tf_op jit(solution)/shard_map/ppermute | solution.py:25
  83.9 11.0 %collective-permute-done.6.third = bf16[128,2048]{1,0:T(8,128)(2,1)S(1)} collective-permute-done((bf16[128,2048]{1,0:T(8,128)(2,1)}, bf16[128,2048]{1,0:T(8,128)(2,1)S(1)}, u32[]{:S(2)}, u32[]{:S(2)}) %collective-permute-start.6) | collective-permute-done | bytes 524320 | tf_op jit(solution)/shard_map/ppermute | solution.py:25
  105.8 7.1 %all-to-all-start.3 = ((bf16[16,4,2,128,128]{4,3,2,1,0:T(8,128)(2,1)}), bf16[16,4,2,128,128]{4,3,2,1,0:T(8,128)(2,1)}, u32[]{:S(2)}, u32[]{:S(2)}) async-start(bf16[16,4,2,128,128]{4,3,2,1,0:T(8,128)(2,1)} %copy-done), calls=%async_computation.3 | async-start | bytes 8388608 | tf_op jit(solution)/shard_map/all_to_all | solution.py:38
  113.3 9.7 %collective-permute-done.10 = bf16[2048,256]{1,0:T(8,128)(2,1)} collective-permute-done((bf16[2048,256]{1,0:T(8,128)(2,1)}, bf16[2048,256]{1,0:T(8,128)(2,1)}, u32[]{:S(2)}, u32[]{:S(2)}) %collective-permute-start.10) | collective-permute-done | bytes 1048608 | tf_op jit(solution)/shard_map/ppermute | solution.py:25
  123.5 4.4 %constant_dynamic-slice_fusion.1 = (bf16[256,2048]{1,0:T(8,128)(2,1)}, bf16[256,2048]{1,0:T(8,128)(2,1)}, bf16[256,2048]{1,0:T(8,128)(2,1)}, bf16[256,2048]{1,0:T(8,128)(2,1)}) fusion(bf16[256,8192]{1,0:T(8,128)(2,1)} %bitcast.136, s32[]{:T(128)S(6)} %select_n.369, s32[]{:T(128)S(6)} %select_n.367, s32[]{:T(128)S(6)} %select_n.365, s32[]{:T(128)S(6)} %select_n.363), kind=kLoop, calls=%fused_computation.105 | loop fusion | bytes 8388624 | tf_op jit(solution)/shard_map/dynamic_slice | solution.py:304
  130.1 3.8 collective-permute-start.19
  146.4 30.8 %all-to-all-done.3.cache = bf16[16,4,2,128,128]{4,3,2,1,0:T(8,128)(2,1)} async-done(((bf16[16,4,2,128,128]{4,3,2,1,0:T(8,128)(2,1)}), bf16[16,4,2,128,128]{4,3,2,1,0:T(8,128)(2,1)}, u32[]{:S(2)}, u32[]{:S(2)}) %all-to-all-start.3) | async-done | bytes 4194336 | tf_op jit(solution)/shard_map/all_to_all | solution.py:38
  177.3 4.1 all-to-all-start.4
  183.1 4.7 %collective-permute-done.17 = bf16[256,2048]{1,0:T(8,128)(2,1)} collective-permute-done((bf16[256,2048]{1,0:T(8,128)(2,1)}, bf16[256,2048]{1,0:T(8,128)(2,1)}, u32[]{:S(2)}, u32[]{:S(2)}) %collective-permute-start.17) | collective-permute-done | bytes 1048608 | tf_op jit(solution)/shard_map/ppermute | solution.py:25
  187.9 4.9 %all-to-all-done.4.parts = bf16[4,64,896]{2,1,0:T(8,128)(2,1)} async-done(((bf16[4,64,896]{2,1,0:T(8,128)(2,1)}), bf16[4,64,896]{2,1,0:T(8,128)(2,1)}, u32[]{:S(2)}, u32[]{:S(2)}) %all-to-all-start.4) | async-done | bytes 458784 | tf_op jit(solution)/shard_map/all_to_all | solution.py:44
  208.3 23.8 %all_to_all.80 = bf16[16,16,2048]{2,1,0:T(8,128)(2,1)S(1)} all-to-all(bf16[16,16,2048]{2,1,0:T(8,128)(2,1)S(1)} %output_terms.4), channel_id=1, replica_groups={{0,2,4,6,8,10,12,14,16,18,20,22,24,26,28,30},{1,3,5,7,9,11,13,15,17,19,..., dimensions={0} | all-to-all | bytes 2097152 | tf_op jit(solution)/shard_map/all_to_all | solution.py:38
  232.4 19.2 %all_to_all.81.rows = bf16[16,16,2048]{2,1,0:T(8,128)(2,1)S(1)} all-to-all(bf16[16,16,2048]{2,1,0:T(8,128)(2,1)S(1)} %broadcast_in_dim.81), channel_id=1, replica_groups={{0,2,4,6,8,10,12,14,16,18,20,22,24,26,28,30},{1,3,5,7,9,11,13,15,17,19,..., dimensions={0} | all-to-all | bytes 2097152 | tf_op jit(solution)/shard_map/all_to_all | solution.py:38
  254.3 10.1 %all_to_all.82.parts = bf16[4,64,896]{2,1,0:T(8,128)(2,1)S(1)} all-to-all(bf16[4,64,896]{2,1,0:T(8,128)(2,1)S(1)} %project.5), channel_id=1, replica_groups=mesh['section'=4,'tensor'=32] {'section'}, dimensions={0} | all-to-all | bytes 917504 | tf_op jit(solution)/shard_map/all_to_all | solution.py:44
  277.3 15.9 %all_to_all.83 = bf16[16,16,2048]{2,1,0:T(8,128)(2,1)S(1)} all-to-all(bf16[16,16,2048]{2,1,0:T(8,128)(2,1)S(1)} %output_terms.5), channel_id=1, replica_groups={{0,2,4,6,8,10,12,14,16,18,20,22,24,26,28,30},{1,3,5,7,9,11,13,15,17,19,..., dimensions={0} | all-to-all | bytes 2097152 | tf_op jit(solution)/shard_map/all_to_all | solution.py:38
  293.5 15.9 %all_to_all.84.rows = bf16[16,16,2048]{2,1,0:T(8,128)(2,1)S(1)} all-to-all(bf16[16,16,2048]{2,1,0:T(8,128)(2,1)S(1)} %broadcast_in_dim.82), channel_id=1, replica_groups={{0,2,4,6,8,10,12,14,16,18,20,22,24,26,28,30},{1,3,5,7,9,11,13,15,17,19,..., dimensions={0} | all-to-all | bytes 2097152 | tf_op jit(solution)/shard_map/all_to_all | solution.py:38
  312.1 11.1 %all_to_all.85.parts = bf16[4,64,896]{2,1,0:T(8,128)(2,1)S(1)} all-to-all(bf16[4,64,896]{2,1,0:T(8,128)(2,1)S(1)} %project.6), channel_id=1, replica_groups=mesh['section'=4,'tensor'=32] {'section'}, dimensions={0} | all-to-all | bytes 917504 | tf_op jit(solution)/shard_map/all_to_all | solution.py:44
  330.4 3.1 collective-permute-done.31.third
  335.9 19.6 %all_to_all.86 = bf16[16,16,2048]{2,1,0:T(8,128)(2,1)S(1)} all-to-all(bf16[16,16,2048]{2,1,0:T(8,128)(2,1)S(1)} %output_terms.6), channel_id=1, replica_groups={{0,2,4,6,8,10,12,14,16,18,20,22,24,26,28,30},{1,3,5,7,9,11,13,15,17,19,..., dimensions={0} | all-to-all | bytes 2097152 | tf_op jit(solution)/shard_map/all_to_all | solution.py:38
  355.9 15.6 %all_to_all.87.rows = bf16[16,16,2048]{2,1,0:T(8,128)(2,1)S(1)} all-to-all(bf16[16,16,2048]{2,1,0:T(8,128)(2,1)S(1)} %broadcast_in_dim.83), channel_id=1, replica_groups={{0,2,4,6,8,10,12,14,16,18,20,22,24,26,28,30},{1,3,5,7,9,11,13,15,17,19,..., dimensions={0} | all-to-all | bytes 2097152 | tf_op jit(solution)/shard_map/all_to_all | solution.py:38
  374.1 10.8 %all_to_all.88.parts = bf16[4,64,896]{2,1,0:T(8,128)(2,1)S(1)} all-to-all(bf16[4,64,896]{2,1,0:T(8,128)(2,1)S(1)} %project.7), channel_id=1, replica_groups=mesh['section'=4,'tensor'=32] {'section'}, dimensions={0} | all-to-all | bytes 917504 | tf_op jit(solution)/shard_map/all_to_all | solution.py:44
  397.7 15.9 %all_to_all.89 = bf16[16,16,2048]{2,1,0:T(8,128)(2,1)S(1)} all-to-all(bf16[16,16,2048]{2,1,0:T(8,128)(2,1)S(1)} %output_terms.7), channel_id=1, replica_groups={{0,2,4,6,8,10,12,14,16,18,20,22,24,26,28,30},{1,3,5,7,9,11,13,15,17,19,..., dimensions={0} | all-to-all | bytes 2097152 | tf_op jit(solution)/shard_map/all_to_all | solution.py:38
  414.0 8.4 %all_to_all.90 = f32[4,4,2048]{2,1,0:T(4,128)S(1)} all-to-all(f32[4,4,2048]{2,1,0:T(4,128)S(1)} %copy.43), channel_id=1, replica_groups=mesh['section'=4,'tensor'=32] {'section'}, dimensions={0} | all-to-all | bytes 262144 | tf_op jit(solution)/shard_map/all_to_all | solution.py:44
  (209 shorter events, 111.5 us)
Async XLA Ops:
  1.3 18.6 %collective-permute-start.2 = (bf16[64,2048]{1,0:T(8,128)(2,1)S(1)}, bf16[64,2048]{1,0:T(8,128)(2,1)S(1)}, u32[]{:S(2)}, u32[]{:S(2)}) collective-permute-start(bf16[64,2048]{1,0:T(8,128)(2,1)S(1)} %get-tuple-element.122), channel_id=1, source_target_pairs={{0,96},{32,0},{64,32},{96,64},{1,97},{33,1},{65,33},{97,65},{2,98}... | collective-permute-start | bytes 786440 | tf_op jit(solution)/shard_map/ppermute | solution.py:25
  4.5 15.5 %collective-permute-start = (bf16[64,2048]{1,0:T(8,128)(2,1)S(1)}, bf16[64,2048]{1,0:T(8,128)(2,1)S(1)}, u32[]{:S(2)}, u32[]{:S(2)}) collective-permute-start(bf16[64,2048]{1,0:T(8,128)(2,1)S(1)} %get-tuple-element.123), channel_id=1, source_target_pairs={{0,32},{32,64},{64,96},{96,0},{1,33},{33,65},{65,97},{97,1},{2,34}... | collective-permute-start | bytes 786440 | tf_op jit(solution)/shard_map/ppermute | solution.py:25
  4.5 15.5 %collective-permute-start.1 = (bf16[64,2048]{1,0:T(8,128)(2,1)S(1)}, bf16[64,2048]{1,0:T(8,128)(2,1)S(1)}, u32[]{:S(2)}, u32[]{:S(2)}) collective-permute-start(bf16[64,2048]{1,0:T(8,128)(2,1)S(1)} %get-tuple-element.125), channel_id=1, source_target_pairs={{0,64},{32,96},{64,0},{96,32},{1,65},{33,97},{65,1},{97,33},{2,66}... | collective-permute-start | bytes 786440 | tf_op jit(solution)/shard_map/ppermute | solution.py:25
  10.2 28.2 %collective-permute-start.4 = (bf16[2048,256]{1,0:T(8,128)(2,1)}, bf16[2048,256]{1,0:T(8,128)(2,1)}, u32[]{:S(2)}, u32[]{:S(2)}) collective-permute-start(bf16[2048,256]{1,0:T(8,128)(2,1)} %get-tuple-element.102), channel_id=1, source_target_pairs={{0,96},{32,0},{64,32},{96,64},{1,97},{33,1},{65,33},{97,65},{2,98}... | collective-permute-start | bytes 3145736 | tf_op jit(solution)/shard_map/ppermute | solution.py:25
  11.3 30.3 %collective-permute-start.3 = (bf16[2048,256]{1,0:T(8,128)(2,1)}, bf16[2048,256]{1,0:T(8,128)(2,1)}, u32[]{:S(2)}, u32[]{:S(2)}) collective-permute-start(bf16[2048,256]{1,0:T(8,128)(2,1)} %get-tuple-element.103), channel_id=1, source_target_pairs={{0,32},{32,64},{64,96},{96,0},{1,33},{33,65},{65,97},{97,1},{2,34}... | collective-permute-start | bytes 3145736 | tf_op jit(solution)/shard_map/ppermute | solution.py:25
  19.9 18.5 %all-to-all-start = ((bf16[32,24,256]{2,1,0:T(8,128)(2,1)}), bf16[32,24,256]{2,1,0:T(8,128)(2,1)S(1)}, u32[]{:S(2)}, u32[]{:S(2)}) async-start(bf16[32,24,256]{2,1,0:T(8,128)(2,1)} %pad_maximum_fusion.5), calls=%async_computation | async-start | bytes 786432 | tf_op jit(solution)/shard_map/all_to_all | solution.py:65
  42.4 17.0 %all-to-all-start.1 = ((bf16[32,24,256]{2,1,0:T(8,128)(2,1)}), bf16[32,24,256]{2,1,0:T(8,128)(2,1)S(1)}, u32[]{:S(2)}, u32[]{:S(2)}) async-start(bf16[32,24,256]{2,1,0:T(8,128)(2,1)} %fusion.17), calls=%async_computation.1 | async-start | bytes 786432 | tf_op jit(solution)/shard_map/all_to_all | solution.py:44
  48.5 28.9 %collective-permute-start.9 = (bf16[4,64,2048]{2,1,0:T(8,128)(2,1)}, bf16[4,64,2048]{2,1,0:T(8,128)(2,1)}, u32[]{:S(2)}, u32[]{:S(2)}) collective-permute-start(bf16[4,64,2048]{2,1,0:T(8,128)(2,1)} %pad_maximum_fusion.4), channel_id=1, source_target_pairs={{0,2},{1,3},{2,6},{3,7},{4,10},{5,11},{6,14},{7,15},{8,18},{9,19},... | collective-permute-start | bytes 3145736 | tf_op jit(solution)/shard_map/ppermute | solution.py:34
  50.0 27.4 %collective-permute-start.8 = (bf16[4,64,2048]{2,1,0:T(8,128)(2,1)}, bf16[4,64,2048]{2,1,0:T(8,128)(2,1)}, u32[]{:S(2)}, u32[]{:S(2)}) collective-permute-start(bf16[4,64,2048]{2,1,0:T(8,128)(2,1)} %pad_maximum_fusion.4), channel_id=1, source_target_pairs={{0,0},{1,1},{2,4},{3,5},{4,8},{5,9},{6,12},{7,13},{8,16},{9,17},{1... | collective-permute-start | bytes 3145736 | tf_op jit(solution)/shard_map/ppermute | solution.py:34
  61.4 33.4 %all-to-all-start.2 = ((bf16[16,16,2048]{2,1,0:T(8,128)(2,1)}), bf16[16,16,2048]{2,1,0:T(8,128)(2,1)S(1)}, u32[]{:S(2)}, u32[]{:S(2)}) async-start(bf16[16,16,2048]{2,1,0:T(8,128)(2,1)} %broadcast_in_dim.46), calls=%async_computation.2 | async-start | bytes 2097152 | tf_op jit(solution)/shard_map/all_to_all | solution.py:38
  68.4 15.5 %collective-permute-start.5 = (bf16[128,2048]{1,0:T(8,128)(2,1)}, bf16[128,2048]{1,0:T(8,128)(2,1)S(1)}, u32[]{:S(2)}, u32[]{:S(2)}) collective-permute-start(bf16[128,2048]{1,0:T(8,128)(2,1)} %get-tuple-element.44), channel_id=1, source_target_pairs={{0,32},{32,64},{64,96},{96,0},{1,33},{33,65},{65,97},{97,1},{2,34}... | collective-permute-start | bytes 1572872 | tf_op jit(solution)/shard_map/ppermute | solution.py:25
  70.5 24.3 %collective-permute-start.6 = (bf16[128,2048]{1,0:T(8,128)(2,1)}, bf16[128,2048]{1,0:T(8,128)(2,1)S(1)}, u32[]{:S(2)}, u32[]{:S(2)}) collective-permute-start(bf16[128,2048]{1,0:T(8,128)(2,1)} %get-tuple-element.45), channel_id=1, source_target_pairs={{0,64},{32,96},{64,0},{96,32},{1,65},{33,97},{65,1},{97,33},{2,66}... | collective-permute-start | bytes 1572872 | tf_op jit(solution)/shard_map/ppermute | solution.py:25
  73.2 21.7 %collective-permute-start.7 = (bf16[128,2048]{1,0:T(8,128)(2,1)}, bf16[128,2048]{1,0:T(8,128)(2,1)S(1)}, u32[]{:S(2)}, u32[]{:S(2)}) collective-permute-start(bf16[128,2048]{1,0:T(8,128)(2,1)} %get-tuple-element.46), channel_id=1, source_target_pairs={{0,96},{32,0},{64,32},{96,64},{1,97},{33,1},{65,33},{97,65},{2,98}... | collective-permute-start | bytes 1572872 | tf_op jit(solution)/shard_map/ppermute | solution.py:25
  97.5 25.5 %collective-permute-start.10 = (bf16[2048,256]{1,0:T(8,128)(2,1)}, bf16[2048,256]{1,0:T(8,128)(2,1)}, u32[]{:S(2)}, u32[]{:S(2)}) collective-permute-start(bf16[2048,256]{1,0:T(8,128)(2,1)} %constant_dynamic-slice_fusion.5), channel_id=1, source_target_pairs={{0,64},{32,96},{64,0},{96,32},{1,65},{33,97},{65,1},{97,33},{2,66}... | collective-permute-start | bytes 3145736 | tf_op jit(solution)/shard_map/ppermute | solution.py:25
  103.2 24.7 %collective-permute-start.16 = (bf16[4,64,2048]{2,1,0:T(8,128)(2,1)}, bf16[4,64,2048]{2,1,0:T(8,128)(2,1)}, u32[]{:S(2)}, u32[]{:S(2)}) collective-permute-start(bf16[4,64,2048]{2,1,0:T(8,128)(2,1)} %get-tuple-element.114), channel_id=1, source_target_pairs={{0,1},{1,0},{2,3},{3,2},{4,5},{5,4},{6,7},{7,6},{8,9},{9,8},{10,11... | collective-permute-start | bytes 3145736 | tf_op jit(solution)/shard_map/ppermute | solution.py:29
  105.8 71.5 %all-to-all-start.3 = ((bf16[16,4,2,128,128]{4,3,2,1,0:T(8,128)(2,1)}), bf16[16,4,2,128,128]{4,3,2,1,0:T(8,128)(2,1)}, u32[]{:S(2)}, u32[]{:S(2)}) async-start(bf16[16,4,2,128,128]{4,3,2,1,0:T(8,128)(2,1)} %copy-done), calls=%async_computation.3 | async-start | bytes 8388608 | tf_op jit(solution)/shard_map/all_to_all | solution.py:38
  113.0 17.1 %collective-permute-start.15 = (bf16[4,64,2048]{2,1,0:T(8,128)(2,1)S(1)}, bf16[4,64,2048]{2,1,0:T(8,128)(2,1)S(1)}, u32[]{:S(2)}, u32[]{:S(2)}) collective-permute-start(bf16[4,64,2048]{2,1,0:T(8,128)(2,1)S(1)} %copy-done.13), channel_id=1, source_target_pairs={{0,1},{1,0},{2,3},{3,2},{4,5},{5,4},{6,7},{7,6},{8,9},{9,8},{10,11... | collective-permute-start | bytes 3145736 | tf_op jit(solution)/shard_map/ppermute | solution.py:29
  123.0 15.6 %collective-permute-start.11 = (bf16[2048,256]{1,0:T(8,128)(2,1)S(1)}, bf16[2048,256]{1,0:T(8,128)(2,1)S(1)}, u32[]{:S(2)}, u32[]{:S(2)}) collective-permute-start(bf16[2048,256]{1,0:T(8,128)(2,1)S(1)} %copy-done.15), channel_id=1, source_target_pairs={{0,1},{1,0},{2,3},{3,2},{4,5},{5,4},{6,7},{7,6},{8,9},{9,8},{10,11... | collective-permute-start | bytes 3145736 | tf_op jit(solution)/shard_map/ppermute | solution.py:29
  123.0 15.9 %collective-permute-start.12 = (bf16[2048,256]{1,0:T(8,128)(2,1)}, bf16[2048,256]{1,0:T(8,128)(2,1)S(1)}, u32[]{:S(2)}, u32[]{:S(2)}) collective-permute-start(bf16[2048,256]{1,0:T(8,128)(2,1)} %collective-permute-done.3), channel_id=1, source_target_pairs={{0,1},{1,0},{2,3},{3,2},{4,5},{5,4},{6,7},{7,6},{8,9},{9,8},{10,11... | collective-permute-start | bytes 3145736 | tf_op jit(solution)/shard_map/ppermute | solution.py:29
  123.5 16.0 %collective-permute-start.13 = (bf16[2048,256]{1,0:T(8,128)(2,1)}, bf16[2048,256]{1,0:T(8,128)(2,1)S(1)}, u32[]{:S(2)}, u32[]{:S(2)}) collective-permute-start(bf16[2048,256]{1,0:T(8,128)(2,1)} %collective-permute-done.10), channel_id=1, source_target_pairs={{0,1},{1,0},{2,3},{3,2},{4,5},{5,4},{6,7},{7,6},{8,9},{9,8},{10,11... | collective-permute-start | bytes 3145736 | tf_op jit(solution)/shard_map/ppermute | solution.py:29
  127.9 11.7 %collective-permute-start.14 = (bf16[2048,256]{1,0:T(8,128)(2,1)}, bf16[2048,256]{1,0:T(8,128)(2,1)S(1)}, u32[]{:S(2)}, u32[]{:S(2)}) collective-permute-start(bf16[2048,256]{1,0:T(8,128)(2,1)} %collective-permute-done.4), channel_id=1, source_target_pairs={{0,1},{1,0},{2,3},{3,2},{4,5},{5,4},{6,7},{7,6},{8,9},{9,8},{10,11... | collective-permute-start | bytes 3145736 | tf_op jit(solution)/shard_map/ppermute | solution.py:29
  130.1 53.0 %collective-permute-start.19 = (bf16[256,2048]{1,0:T(8,128)(2,1)}, bf16[256,2048]{1,0:T(8,128)(2,1)}, u32[]{:S(2)}, u32[]{:S(2)}) collective-permute-start(bf16[256,2048]{1,0:T(8,128)(2,1)} %get-tuple-element.97), channel_id=1, source_target_pairs={{0,96},{32,0},{64,32},{96,64},{1,97},{33,1},{65,33},{97,65},{2,98}... | collective-permute-start | bytes 3145736 | tf_op jit(solution)/shard_map/ppermute | solution.py:25
  138.6 44.5 %collective-permute-start.18 = (bf16[256,2048]{1,0:T(8,128)(2,1)}, bf16[256,2048]{1,0:T(8,128)(2,1)}, u32[]{:S(2)}, u32[]{:S(2)}) collective-permute-start(bf16[256,2048]{1,0:T(8,128)(2,1)} %get-tuple-element.98), channel_id=1, source_target_pairs={{0,64},{32,96},{64,0},{96,32},{1,65},{33,97},{65,1},{97,33},{2,66}... | collective-permute-start | bytes 3145736 | tf_op jit(solution)/shard_map/ppermute | solution.py:25
  139.0 48.9 %collective-permute-start.17 = (bf16[256,2048]{1,0:T(8,128)(2,1)}, bf16[256,2048]{1,0:T(8,128)(2,1)}, u32[]{:S(2)}, u32[]{:S(2)}) collective-permute-start(bf16[256,2048]{1,0:T(8,128)(2,1)} %get-tuple-element.99), channel_id=1, source_target_pairs={{0,32},{32,64},{64,96},{96,0},{1,33},{33,65},{65,97},{97,1},{2,34}... | collective-permute-start | bytes 3145736 | tf_op jit(solution)/shard_map/ppermute | solution.py:25
  177.3 15.4 %all-to-all-start.4 = ((bf16[4,64,896]{2,1,0:T(8,128)(2,1)}), bf16[4,64,896]{2,1,0:T(8,128)(2,1)}, u32[]{:S(2)}, u32[]{:S(2)}) async-start(bf16[4,64,896]{2,1,0:T(8,128)(2,1)} %copy-done.12), calls=%async_computation.4 | async-start | bytes 917504 | tf_op jit(solution)/shard_map/all_to_all | solution.py:44
  192.7 6.7 %collective-permute-start.23 = (bf16[256,2048]{1,0:T(8,128)(2,1)}, bf16[256,2048]{1,0:T(8,128)(2,1)S(1)}, u32[]{:S(2)}, u32[]{:S(2)}) collective-permute-start(bf16[256,2048]{1,0:T(8,128)(2,1)} %get-tuple-element.71), channel_id=1, source_target_pairs={{0,1},{1,0},{2,3},{3,2},{4,5},{5,4},{6,7},{7,6},{8,9},{9,8},{10,11... | collective-permute-start | bytes 3145736 | tf_op jit(solution)/shard_map/ppermute | solution.py:29
  192.7 7.1 %collective-permute-start.24 = (bf16[256,2048]{1,0:T(8,128)(2,1)}, bf16[256,2048]{1,0:T(8,128)(2,1)S(1)}, u32[]{:S(2)}, u32[]{:S(2)}) collective-permute-start(bf16[256,2048]{1,0:T(8,128)(2,1)} %collective-permute-done.17), channel_id=1, source_target_pairs={{0,1},{1,0},{2,3},{3,2},{4,5},{5,4},{6,7},{7,6},{8,9},{9,8},{10,11... | collective-permute-start | bytes 3145736 | tf_op jit(solution)/shard_map/ppermute | solution.py:29
  193.2 8.4 %collective-permute-start.25 = (bf16[256,2048]{1,0:T(8,128)(2,1)}, bf16[256,2048]{1,0:T(8,128)(2,1)S(1)}, u32[]{:S(2)}, u32[]{:S(2)}) collective-permute-start(bf16[256,2048]{1,0:T(8,128)(2,1)} %collective-permute-done.18), channel_id=1, source_target_pairs={{0,1},{1,0},{2,3},{3,2},{4,5},{5,4},{6,7},{7,6},{8,9},{9,8},{10,11... | collective-permute-start | bytes 3145736 | tf_op jit(solution)/shard_map/ppermute | solution.py:29
  193.2 8.4 %collective-permute-start.26 = (bf16[256,2048]{1,0:T(8,128)(2,1)}, bf16[256,2048]{1,0:T(8,128)(2,1)S(1)}, u32[]{:S(2)}, u32[]{:S(2)}) collective-permute-start(bf16[256,2048]{1,0:T(8,128)(2,1)} %collective-permute-done.19), channel_id=1, source_target_pairs={{0,1},{1,0},{2,3},{3,2},{4,5},{5,4},{6,7},{7,6},{8,9},{9,8},{10,11... | collective-permute-start | bytes 3145736 | tf_op jit(solution)/shard_map/ppermute | solution.py:29
  197.2 6.7 %collective-permute-start.22 = (bf16[64,512]{1,0:T(8,128)(2,1)S(1)}, bf16[64,512]{1,0:T(8,128)(2,1)S(1)}, u32[]{:S(2)}, u32[]{:S(2)}) collective-permute-start(bf16[64,512]{1,0:T(8,128)(2,1)S(1)} %attend.4.first), channel_id=1, source_target_pairs={{0,96},{32,0},{64,32},{96,64},{1,97},{33,1},{65,33},{97,65},{2,98}... | collective-permute-start | bytes 196616 | tf_op jit(solution)/shard_map/ppermute | solution.py:25
  199.4 6.0 %collective-permute-start.21 = (bf16[64,512]{1,0:T(8,128)(2,1)S(1)}, bf16[64,512]{1,0:T(8,128)(2,1)S(1)}, u32[]{:S(2)}, u32[]{:S(2)}) collective-permute-start(bf16[64,512]{1,0:T(8,128)(2,1)S(1)} %attend.4.first), channel_id=1, source_target_pairs={{0,64},{32,96},{64,0},{96,32},{1,65},{33,97},{65,1},{97,33},{2,66}... | collective-permute-start | bytes 196616 | tf_op jit(solution)/shard_map/ppermute | solution.py:25
  199.8 6.8 %collective-permute-start.20 = (bf16[64,512]{1,0:T(8,128)(2,1)S(1)}, bf16[64,512]{1,0:T(8,128)(2,1)S(1)}, u32[]{:S(2)}, u32[]{:S(2)}) collective-permute-start(bf16[64,512]{1,0:T(8,128)(2,1)S(1)} %attend.4.first), channel_id=1, source_target_pairs={{0,32},{32,64},{64,96},{96,0},{1,33},{33,65},{65,97},{97,1},{2,34}... | collective-permute-start | bytes 196616 | tf_op jit(solution)/shard_map/ppermute | solution.py:25
  (37 other events, 540.6 us)

commit v6 on v5

--- a/solution.py
+++ b/solution.py
@@ -337,7 +337,7 @@
     wq_mine[2] = share(query_mat, 0, quarter, 2)
     cache = plane_exchange(by_head(cached))
     wq_mine, output_mat = lax.optimization_barrier((wq_mine, output_weight[0]))
-    wo_mine = [share(output_mat, 1, quarter, d) for d in distances]
+    wo_mine = [share(output_mat, 1, quarter, d) if d != 2 else None for d in distances]
     wq_other = jnp.stack([core_swap(w) for w in wq_mine])
     wq_mine = jnp.stack(wq_mine)
     wq_mine, wq_other = lax.optimization_barrier((wq_mine, wq_other))
@@ -369,10 +369,13 @@
         weights = [pick(w) for w in (wq_mine, wq_other, keys_t, values_t)]
         partial = project(rows, forward, gains, layer, slot, *weights)
         if layer == 0:
-            partial, cache = lax.optimization_barrier((partial, cache))
+            partial, cache, output_mat = lax.optimization_barrier((partial, cache, output_mat))
+            wo_mine[2] = share(output_mat, 1, quarter, 2)
         parts = section_exchange(partial)
         if layer == 0:
-            parts, wo_mine = lax.optimization_barrier((parts, wo_mine))
+            parts, wo_mine[1], wo_mine[3] = lax.optimization_barrier(
+                (parts, wo_mine[1], wo_mine[3])
+            )
             wo_other = jnp.stack([core_swap(w) for w in wo_mine])
             wo_mine = jnp.stack(wo_mine)
         mixed = attend(parts, cosine, sine, bias, cache, slot)

time: 425 us -> 442 us (1.040)
  waiting for transfers between devices: 99.7 us -> 116 us
    all_to_all x2, waiting for transfers between devices: 4.87 us -> 24.4 us  [section_exchange(): lax.all_to_all(blocks, 'section', split_axis=0, concat_axis=0, tiled=True)]
    ppermute x24, waiting for transfers between devices: 54.4 us -> 49.5 us  [section_send(): return lax.ppermute(block, 'section', route)]
    dynamic_slice x4 -> x5, local copies, waits for them, and re-layouts: 11.9 us -> 13.5 us  [own(): return lax.dynamic_slice_in_dim(array, start, size, axis)]
  transfers between devices with their start and end apart: 41 -> 41, of which waited for: 21 -> 20; matrix products, arithmetic and copies ran while one was open for 10% -> 10% of each run, Pallas kernels for 1% -> 1%
where the time goes in v6:
time: 442 us; the launch traced here: 440 us
  blocking collectives  165 us (37%)
  waiting for transfers between devices  116 us (26%)
  starting transfers between devices  74.4 us (17%)
  local copies, waits for them, and re-layouts  36.1 us (8%)
  Pallas kernels  29.7 us (7%)
  other arithmetic  18.3 us (4%)
    all_to_all x7, blocking collectives, plane_exchange(): lax.all_to_all(blocks, 'tensor', split_axis=0, concat_axis=0, tiled=True,...  124 us
    ppermute x24, waiting for transfers between devices, section_send(): return lax.ppermute(block, 'section', route)  49.5 us
    all_to_all x4, blocking collectives, section_exchange(): lax.all_to_all(blocks, 'section', split_axis=0, concat_axis=0, tiled=True)  40.3 us
    all_to_all x2, waiting for transfers between devices, plane_exchange(): lax.all_to_all(blocks, 'tensor', split_axis=0, concat_axis=0, tiled=True,...  32.4 us
    ppermute x24, starting transfers between devices, section_send(): return lax.ppermute(block, 'section', route)  31.7 us
    all_to_all x2, waiting for transfers between devices, section_exchange(): lax.all_to_all(blocks, 'section', split_axis=0, concat_axis=0, tiled=True)  24.4 us
    all_to_all x2, starting transfers between devices, plane_exchange(): lax.all_to_all(blocks, 'tensor', split_axis=0, concat_axis=0, tiled=True,...  14 us
    dynamic_slice x5, local copies, waits for them, and re-layouts, own(): return lax.dynamic_slice_in_dim(array, start, size, axis)  13.5 us
  transfers between devices with their start and end apart: 41, of which 20 were waited for; matrix products, arithmetic and copies ran while one was open for 10% of the time, Pallas kernels for 1%

profile of v6, /device:TPU:0, one launch (start us, length us, event | category | flops | bytes accessed | tf_op | source)
XLA Modules:
  0.0 440.2 jit_solution(14068583377053052902)
XLA Ops:
  1.3 3.2 collective-permute-start.2
  6.7 3.6 dynamic-slice_bitcast_fusion.16
  12.9 5.9 %gather_fusion = bf16[512,256]{1,0:T(8,128)(2,1)S(1)} fusion(bf16[16032,256]{1,0:T(8,128)(2,1)} %param.9, s32[1024]{0:T(1024)S(1)} %pad_clamp_fusion), kind=kCustom, calls=%fused_computation | custom fusion | bytes 526336 | tf_op jit(solution)/shard_map/jit(_take)/gather | solution.py:57
  19.9 8.2 %all-to-all-start = ((bf16[32,24,256]{2,1,0:T(8,128)(2,1)}), bf16[32,24,256]{2,1,0:T(8,128)(2,1)S(1)}, u32[]{:S(2)}, u32[]{:S(2)}) async-start(bf16[32,24,256]{2,1,0:T(8,128)(2,1)} %pad_maximum_fusion.5), calls=%async_computation | async-start | bytes 786432 | tf_op jit(solution)/shard_map/all_to_all | solution.py:65
  28.2 3.3 reshape_squeeze.6
  31.6 6.8 %all-to-all-done = bf16[32,24,256]{2,1,0:T(8,128)(2,1)S(1)} async-done(((bf16[32,24,256]{2,1,0:T(8,128)(2,1)}), bf16[32,24,256]{2,1,0:T(8,128)(2,1)S(1)}, u32[]{:S(2)}, u32[]{:S(2)}) %all-to-all-start) | async-done | bytes 393248 | tf_op jit(solution)/shard_map/all_to_all | solution.py:65
  38.4 3.2 collective-permute-done.3
  42.4 3.5 all-to-all-start.1
  50.0 9.5 %collective-permute-start.8 = (bf16[4,64,2048]{2,1,0:T(8,128)(2,1)}, bf16[4,64,2048]{2,1,0:T(8,128)(2,1)}, u32[]{:S(2)}, u32[]{:S(2)}) collective-permute-start(bf16[4,64,2048]{2,1,0:T(8,128)(2,1)} %pad_maximum_fusion.4), channel_id=1, source_target_pairs={{0,0},{1,1},{2,4},{3,5},{4,8},{5,9},{6,12},{7,13},{8,16},{9,17},{1... | collective-permute-start | bytes 3145736 | tf_op jit(solution)/shard_map/ppermute | solution.py:34
  61.4 6.9 %all-to-all-start.2 = ((bf16[16,16,2048]{2,1,0:T(8,128)(2,1)}), bf16[16,16,2048]{2,1,0:T(8,128)(2,1)S(1)}, u32[]{:S(2)}, u32[]{:S(2)}) async-start(bf16[16,16,2048]{2,1,0:T(8,128)(2,1)} %broadcast_in_dim.46), calls=%async_computation.2 | async-start | bytes 2097152 | tf_op jit(solution)/shard_map/all_to_all | solution.py:38
  77.4 6.5 %collective-permute-done.5.second = bf16[128,2048]{1,0:T(8,128)(2,1)S(1)} collective-permute-done((bf16[128,2048]{1,0:T(8,128)(2,1)}, bf16[128,2048]{1,0:T(8,128)(2,1)S(1)}, u32[]{:S(2)}, u32[]{:S(2)}) %collective-permute-start.5) | collective-permute-done | bytes 524320 | tf_op jit(solution)/shard_map/ppermute | solution.py:25
  83.9 11.0 %collective-permute-done.6.third = bf16[128,2048]{1,0:T(8,128)(2,1)S(1)} collective-permute-done((bf16[128,2048]{1,0:T(8,128)(2,1)}, bf16[128,2048]{1,0:T(8,128)(2,1)S(1)}, u32[]{:S(2)}, u32[]{:S(2)}) %collective-permute-start.6) | collective-permute-done | bytes 524320 | tf_op jit(solution)/shard_map/ppermute | solution.py:25
  105.8 7.1 %all-to-all-start.3 = ((bf16[16,4,2,128,128]{4,3,2,1,0:T(8,128)(2,1)}), bf16[16,4,2,128,128]{4,3,2,1,0:T(8,128)(2,1)}, u32[]{:S(2)}, u32[]{:S(2)}) async-start(bf16[16,4,2,128,128]{4,3,2,1,0:T(8,128)(2,1)} %copy-done), calls=%async_computation.3 | async-start | bytes 8388608 | tf_op jit(solution)/shard_map/all_to_all | solution.py:38
  113.4 9.6 %collective-permute-done.10 = bf16[2048,256]{1,0:T(8,128)(2,1)} collective-permute-done((bf16[2048,256]{1,0:T(8,128)(2,1)}, bf16[2048,256]{1,0:T(8,128)(2,1)}, u32[]{:S(2)}, u32[]{:S(2)}) %collective-permute-start.10) | collective-permute-done | bytes 1048608 | tf_op jit(solution)/shard_map/ppermute | solution.py:25
  123.5 3.7 constant_dynamic-slice_fusion.1
  129.4 3.8 collective-permute-start.18
  144.9 32.4 %all-to-all-done.3.cache = bf16[16,4,2,128,128]{4,3,2,1,0:T(8,128)(2,1)} async-done(((bf16[16,4,2,128,128]{4,3,2,1,0:T(8,128)(2,1)}), bf16[16,4,2,128,128]{4,3,2,1,0:T(8,128)(2,1)}, u32[]{:S(2)}, u32[]{:S(2)}) %all-to-all-start.3) | async-done | bytes 4194336 | tf_op jit(solution)/shard_map/all_to_all | solution.py:38
  180.5 4.1 all-to-all-start.4
  186.4 24.4 %all-to-all-done.4.parts = bf16[4,64,896]{2,1,0:T(8,128)(2,1)} async-done(((bf16[4,64,896]{2,1,0:T(8,128)(2,1)}), bf16[4,64,896]{2,1,0:T(8,128)(2,1)}, u32[]{:S(2)}, u32[]{:S(2)}) %all-to-all-start.4) | async-done | bytes 458784 | tf_op jit(solution)/shard_map/all_to_all | solution.py:44
  211.8 3.1 attend.4.first
  227.2 22.0 %all_to_all.80 = bf16[16,16,2048]{2,1,0:T(8,128)(2,1)S(1)} all-to-all(bf16[16,16,2048]{2,1,0:T(8,128)(2,1)S(1)} %output_terms.4), channel_id=1, replica_groups={{0,2,4,6,8,10,12,14,16,18,20,22,24,26,28,30},{1,3,5,7,9,11,13,15,17,19,..., dimensions={0} | all-to-all | bytes 2097152 | tf_op jit(solution)/shard_map/all_to_all | solution.py:38
  249.5 19.3 %all_to_all.81.rows = bf16[16,16,2048]{2,1,0:T(8,128)(2,1)S(1)} all-to-all(bf16[16,16,2048]{2,1,0:T(8,128)(2,1)S(1)} %broadcast_in_dim.81), channel_id=1, replica_groups={{0,2,4,6,8,10,12,14,16,18,20,22,24,26,28,30},{1,3,5,7,9,11,13,15,17,19,..., dimensions={0} | all-to-all | bytes 2097152 | tf_op jit(solution)/shard_map/all_to_all | solution.py:38
  271.5 10.1 %all_to_all.82.parts = bf16[4,64,896]{2,1,0:T(8,128)(2,1)S(1)} all-to-all(bf16[4,64,896]{2,1,0:T(8,128)(2,1)S(1)} %project.5), channel_id=1, replica_groups=mesh['section'=4,'tensor'=32] {'section'}, dimensions={0} | all-to-all | bytes 917504 | tf_op jit(solution)/shard_map/all_to_all | solution.py:44
  294.4 16.0 %all_to_all.83 = bf16[16,16,2048]{2,1,0:T(8,128)(2,1)S(1)} all-to-all(bf16[16,16,2048]{2,1,0:T(8,128)(2,1)S(1)} %output_terms.5), channel_id=1, replica_groups={{0,2,4,6,8,10,12,14,16,18,20,22,24,26,28,30},{1,3,5,7,9,11,13,15,17,19,..., dimensions={0} | all-to-all | bytes 2097152 | tf_op jit(solution)/shard_map/all_to_all | solution.py:38
  310.8 15.9 %all_to_all.84.rows = bf16[16,16,2048]{2,1,0:T(8,128)(2,1)S(1)} all-to-all(bf16[16,16,2048]{2,1,0:T(8,128)(2,1)S(1)} %broadcast_in_dim.82), channel_id=1, replica_groups={{0,2,4,6,8,10,12,14,16,18,20,22,24,26,28,30},{1,3,5,7,9,11,13,15,17,19,..., dimensions={0} | all-to-all | bytes 2097152 | tf_op jit(solution)/shard_map/all_to_all | solution.py:38
  329.4 11.1 %all_to_all.85.parts = bf16[4,64,896]{2,1,0:T(8,128)(2,1)S(1)} all-to-all(bf16[4,64,896]{2,1,0:T(8,128)(2,1)S(1)} %project.6), channel_id=1, replica_groups=mesh['section'=4,'tensor'=32] {'section'}, dimensions={0} | all-to-all | bytes 917504 | tf_op jit(solution)/shard_map/all_to_all | solution.py:44
  347.7 3.1 collective-permute-done.31.third
  353.2 19.6 %all_to_all.86 = bf16[16,16,2048]{2,1,0:T(8,128)(2,1)S(1)} all-to-all(bf16[16,16,2048]{2,1,0:T(8,128)(2,1)S(1)} %output_terms.6), channel_id=1, replica_groups={{0,2,4,6,8,10,12,14,16,18,20,22,24,26,28,30},{1,3,5,7,9,11,13,15,17,19,..., dimensions={0} | all-to-all | bytes 2097152 | tf_op jit(solution)/shard_map/all_to_all | solution.py:38
  373.1 15.6 %all_to_all.87.rows = bf16[16,16,2048]{2,1,0:T(8,128)(2,1)S(1)} all-to-all(bf16[16,16,2048]{2,1,0:T(8,128)(2,1)S(1)} %broadcast_in_dim.83), channel_id=1, replica_groups={{0,2,4,6,8,10,12,14,16,18,20,22,24,26,28,30},{1,3,5,7,9,11,13,15,17,19,..., dimensions={0} | all-to-all | bytes 2097152 | tf_op jit(solution)/shard_map/all_to_all | solution.py:38
  391.4 10.8 %all_to_all.88.parts = bf16[4,64,896]{2,1,0:T(8,128)(2,1)S(1)} all-to-all(bf16[4,64,896]{2,1,0:T(8,128)(2,1)S(1)} %project.7), channel_id=1, replica_groups=mesh['section'=4,'tensor'=32] {'section'}, dimensions={0} | all-to-all | bytes 917504 | tf_op jit(solution)/shard_map/all_to_all | solution.py:44
  415.0 15.9 %all_to_all.89 = bf16[16,16,2048]{2,1,0:T(8,128)(2,1)S(1)} all-to-all(bf16[16,16,2048]{2,1,0:T(8,128)(2,1)S(1)} %output_terms.7), channel_id=1, replica_groups={{0,2,4,6,8,10,12,14,16,18,20,22,24,26,28,30},{1,3,5,7,9,11,13,15,17,19,..., dimensions={0} | all-to-all | bytes 2097152 | tf_op jit(solution)/shard_map/all_to_all | solution.py:38
  431.2 8.4 %all_to_all.90 = f32[4,4,2048]{2,1,0:T(4,128)S(1)} all-to-all(f32[4,4,2048]{2,1,0:T(4,128)S(1)} %copy.43), channel_id=1, replica_groups=mesh['section'=4,'tensor'=32] {'section'}, dimensions={0} | all-to-all | bytes 262144 | tf_op jit(solution)/shard_map/all_to_all | solution.py:44
  (210 shorter events, 111.6 us)
Async XLA Ops:
  1.3 18.6 %collective-permute-start.2 = (bf16[64,2048]{1,0:T(8,128)(2,1)S(1)}, bf16[64,2048]{1,0:T(8,128)(2,1)S(1)}, u32[]{:S(2)}, u32[]{:S(2)}) collective-permute-start(bf16[64,2048]{1,0:T(8,128)(2,1)S(1)} %get-tuple-element.119), channel_id=1, source_target_pairs={{0,96},{32,0},{64,32},{96,64},{1,97},{33,1},{65,33},{97,65},{2,98}... | collective-permute-start | bytes 786440 | tf_op jit(solution)/shard_map/ppermute | solution.py:25
  4.5 15.5 %collective-permute-start = (bf16[64,2048]{1,0:T(8,128)(2,1)S(1)}, bf16[64,2048]{1,0:T(8,128)(2,1)S(1)}, u32[]{:S(2)}, u32[]{:S(2)}) collective-permute-start(bf16[64,2048]{1,0:T(8,128)(2,1)S(1)} %get-tuple-element.120), channel_id=1, source_target_pairs={{0,32},{32,64},{64,96},{96,0},{1,33},{33,65},{65,97},{97,1},{2,34}... | collective-permute-start | bytes 786440 | tf_op jit(solution)/shard_map/ppermute | solution.py:25
  4.5 15.5 %collective-permute-start.1 = (bf16[64,2048]{1,0:T(8,128)(2,1)S(1)}, bf16[64,2048]{1,0:T(8,128)(2,1)S(1)}, u32[]{:S(2)}, u32[]{:S(2)}) collective-permute-start(bf16[64,2048]{1,0:T(8,128)(2,1)S(1)} %get-tuple-element.122), channel_id=1, source_target_pairs={{0,64},{32,96},{64,0},{96,32},{1,65},{33,97},{65,1},{97,33},{2,66}... | collective-permute-start | bytes 786440 | tf_op jit(solution)/shard_map/ppermute | solution.py:25
  10.2 28.2 %collective-permute-start.4 = (bf16[2048,256]{1,0:T(8,128)(2,1)}, bf16[2048,256]{1,0:T(8,128)(2,1)}, u32[]{:S(2)}, u32[]{:S(2)}) collective-permute-start(bf16[2048,256]{1,0:T(8,128)(2,1)} %get-tuple-element.99), channel_id=1, source_target_pairs={{0,96},{32,0},{64,32},{96,64},{1,97},{33,1},{65,33},{97,65},{2,98}... | collective-permute-start | bytes 3145736 | tf_op jit(solution)/shard_map/ppermute | solution.py:25
  11.3 30.3 %collective-permute-start.3 = (bf16[2048,256]{1,0:T(8,128)(2,1)}, bf16[2048,256]{1,0:T(8,128)(2,1)}, u32[]{:S(2)}, u32[]{:S(2)}) collective-permute-start(bf16[2048,256]{1,0:T(8,128)(2,1)} %get-tuple-element.100), channel_id=1, source_target_pairs={{0,32},{32,64},{64,96},{96,0},{1,33},{33,65},{65,97},{97,1},{2,34}... | collective-permute-start | bytes 3145736 | tf_op jit(solution)/shard_map/ppermute | solution.py:25
  19.9 18.5 %all-to-all-start = ((bf16[32,24,256]{2,1,0:T(8,128)(2,1)}), bf16[32,24,256]{2,1,0:T(8,128)(2,1)S(1)}, u32[]{:S(2)}, u32[]{:S(2)}) async-start(bf16[32,24,256]{2,1,0:T(8,128)(2,1)} %pad_maximum_fusion.5), calls=%async_computation | async-start | bytes 786432 | tf_op jit(solution)/shard_map/all_to_all | solution.py:65
  42.4 17.0 %all-to-all-start.1 = ((bf16[32,24,256]{2,1,0:T(8,128)(2,1)}), bf16[32,24,256]{2,1,0:T(8,128)(2,1)S(1)}, u32[]{:S(2)}, u32[]{:S(2)}) async-start(bf16[32,24,256]{2,1,0:T(8,128)(2,1)} %fusion.17), calls=%async_computation.1 | async-start | bytes 786432 | tf_op jit(solution)/shard_map/all_to_all | solution.py:44
  48.5 28.9 %collective-permute-start.9 = (bf16[4,64,2048]{2,1,0:T(8,128)(2,1)}, bf16[4,64,2048]{2,1,0:T(8,128)(2,1)}, u32[]{:S(2)}, u32[]{:S(2)}) collective-permute-start(bf16[4,64,2048]{2,1,0:T(8,128)(2,1)} %pad_maximum_fusion.4), channel_id=1, source_target_pairs={{0,2},{1,3},{2,6},{3,7},{4,10},{5,11},{6,14},{7,15},{8,18},{9,19},... | collective-permute-start | bytes 3145736 | tf_op jit(solution)/shard_map/ppermute | solution.py:34
  50.0 27.4 %collective-permute-start.8 = (bf16[4,64,2048]{2,1,0:T(8,128)(2,1)}, bf16[4,64,2048]{2,1,0:T(8,128)(2,1)}, u32[]{:S(2)}, u32[]{:S(2)}) collective-permute-start(bf16[4,64,2048]{2,1,0:T(8,128)(2,1)} %pad_maximum_fusion.4), channel_id=1, source_target_pairs={{0,0},{1,1},{2,4},{3,5},{4,8},{5,9},{6,12},{7,13},{8,16},{9,17},{1... | collective-permute-start | bytes 3145736 | tf_op jit(solution)/shard_map/ppermute | solution.py:34
  61.4 33.4 %all-to-all-start.2 = ((bf16[16,16,2048]{2,1,0:T(8,128)(2,1)}), bf16[16,16,2048]{2,1,0:T(8,128)(2,1)S(1)}, u32[]{:S(2)}, u32[]{:S(2)}) async-start(bf16[16,16,2048]{2,1,0:T(8,128)(2,1)} %broadcast_in_dim.46), calls=%async_computation.2 | async-start | bytes 2097152 | tf_op jit(solution)/shard_map/all_to_all | solution.py:38
  68.4 15.5 %collective-permute-start.5 = (bf16[128,2048]{1,0:T(8,128)(2,1)}, bf16[128,2048]{1,0:T(8,128)(2,1)S(1)}, u32[]{:S(2)}, u32[]{:S(2)}) collective-permute-start(bf16[128,2048]{1,0:T(8,128)(2,1)} %get-tuple-element.43), channel_id=1, source_target_pairs={{0,32},{32,64},{64,96},{96,0},{1,33},{33,65},{65,97},{97,1},{2,34}... | collective-permute-start | bytes 1572872 | tf_op jit(solution)/shard_map/ppermute | solution.py:25
  70.5 24.3 %collective-permute-start.6 = (bf16[128,2048]{1,0:T(8,128)(2,1)}, bf16[128,2048]{1,0:T(8,128)(2,1)S(1)}, u32[]{:S(2)}, u32[]{:S(2)}) collective-permute-start(bf16[128,2048]{1,0:T(8,128)(2,1)} %get-tuple-element.44), channel_id=1, source_target_pairs={{0,64},{32,96},{64,0},{96,32},{1,65},{33,97},{65,1},{97,33},{2,66}... | collective-permute-start | bytes 1572872 | tf_op jit(solution)/shard_map/ppermute | solution.py:25
  73.2 21.7 %collective-permute-start.7 = (bf16[128,2048]{1,0:T(8,128)(2,1)}, bf16[128,2048]{1,0:T(8,128)(2,1)S(1)}, u32[]{:S(2)}, u32[]{:S(2)}) collective-permute-start(bf16[128,2048]{1,0:T(8,128)(2,1)} %get-tuple-element.45), channel_id=1, source_target_pairs={{0,96},{32,0},{64,32},{96,64},{1,97},{33,1},{65,33},{97,65},{2,98}... | collective-permute-start | bytes 1572872 | tf_op jit(solution)/shard_map/ppermute | solution.py:25
  97.5 25.5 %collective-permute-start.10 = (bf16[2048,256]{1,0:T(8,128)(2,1)}, bf16[2048,256]{1,0:T(8,128)(2,1)}, u32[]{:S(2)}, u32[]{:S(2)}) collective-permute-start(bf16[2048,256]{1,0:T(8,128)(2,1)} %constant_dynamic-slice_fusion.5), channel_id=1, source_target_pairs={{0,64},{32,96},{64,0},{96,32},{1,65},{33,97},{65,1},{97,33},{2,66}... | collective-permute-start | bytes 3145736 | tf_op jit(solution)/shard_map/ppermute | solution.py:25
  103.2 24.0 %collective-permute-start.16 = (bf16[4,64,2048]{2,1,0:T(8,128)(2,1)}, bf16[4,64,2048]{2,1,0:T(8,128)(2,1)}, u32[]{:S(2)}, u32[]{:S(2)}) collective-permute-start(bf16[4,64,2048]{2,1,0:T(8,128)(2,1)} %get-tuple-element.111), channel_id=1, source_target_pairs={{0,1},{1,0},{2,3},{3,2},{4,5},{5,4},{6,7},{7,6},{8,9},{9,8},{10,11... | collective-permute-start | bytes 3145736 | tf_op jit(solution)/shard_map/ppermute | solution.py:29
  105.8 71.5 %all-to-all-start.3 = ((bf16[16,4,2,128,128]{4,3,2,1,0:T(8,128)(2,1)}), bf16[16,4,2,128,128]{4,3,2,1,0:T(8,128)(2,1)}, u32[]{:S(2)}, u32[]{:S(2)}) async-start(bf16[16,4,2,128,128]{4,3,2,1,0:T(8,128)(2,1)} %copy-done), calls=%async_computation.3 | async-start | bytes 8388608 | tf_op jit(solution)/shard_map/all_to_all | solution.py:38
  113.0 16.4 %collective-permute-start.15 = (bf16[4,64,2048]{2,1,0:T(8,128)(2,1)S(1)}, bf16[4,64,2048]{2,1,0:T(8,128)(2,1)S(1)}, u32[]{:S(2)}, u32[]{:S(2)}) collective-permute-start(bf16[4,64,2048]{2,1,0:T(8,128)(2,1)S(1)} %copy-done.13), channel_id=1, source_target_pairs={{0,1},{1,0},{2,3},{3,2},{4,5},{5,4},{6,7},{7,6},{8,9},{9,8},{10,11... | collective-permute-start | bytes 3145736 | tf_op jit(solution)/shard_map/ppermute | solution.py:29
  123.0 14.9 %collective-permute-start.11 = (bf16[2048,256]{1,0:T(8,128)(2,1)S(1)}, bf16[2048,256]{1,0:T(8,128)(2,1)S(1)}, u32[]{:S(2)}, u32[]{:S(2)}) collective-permute-start(bf16[2048,256]{1,0:T(8,128)(2,1)S(1)} %copy-done.14), channel_id=1, source_target_pairs={{0,1},{1,0},{2,3},{3,2},{4,5},{5,4},{6,7},{7,6},{8,9},{9,8},{10,11... | collective-permute-start | bytes 3145736 | tf_op jit(solution)/shard_map/ppermute | solution.py:29
  123.0 14.9 %collective-permute-start.12 = (bf16[2048,256]{1,0:T(8,128)(2,1)}, bf16[2048,256]{1,0:T(8,128)(2,1)S(1)}, u32[]{:S(2)}, u32[]{:S(2)}) collective-permute-start(bf16[2048,256]{1,0:T(8,128)(2,1)} %collective-permute-done.3), channel_id=1, source_target_pairs={{0,1},{1,0},{2,3},{3,2},{4,5},{5,4},{6,7},{7,6},{8,9},{9,8},{10,11... | collective-permute-start | bytes 3145736 | tf_op jit(solution)/shard_map/ppermute | solution.py:29
  123.5 14.4 %collective-permute-start.13 = (bf16[2048,256]{1,0:T(8,128)(2,1)}, bf16[2048,256]{1,0:T(8,128)(2,1)S(1)}, u32[]{:S(2)}, u32[]{:S(2)}) collective-permute-start(bf16[2048,256]{1,0:T(8,128)(2,1)} %collective-permute-done.10), channel_id=1, source_target_pairs={{0,1},{1,0},{2,3},{3,2},{4,5},{5,4},{6,7},{7,6},{8,9},{9,8},{10,11... | collective-permute-start | bytes 3145736 | tf_op jit(solution)/shard_map/ppermute | solution.py:29
  127.2 10.8 %collective-permute-start.14 = (bf16[2048,256]{1,0:T(8,128)(2,1)}, bf16[2048,256]{1,0:T(8,128)(2,1)S(1)}, u32[]{:S(2)}, u32[]{:S(2)}) collective-permute-start(bf16[2048,256]{1,0:T(8,128)(2,1)} %collective-permute-done.4), channel_id=1, source_target_pairs={{0,1},{1,0},{2,3},{3,2},{4,5},{5,4},{6,7},{7,6},{8,9},{9,8},{10,11... | collective-permute-start | bytes 3145736 | tf_op jit(solution)/shard_map/ppermute | solution.py:29
  129.4 57.0 %collective-permute-start.18 = (bf16[256,2048]{1,0:T(8,128)(2,1)}, bf16[256,2048]{1,0:T(8,128)(2,1)}, u32[]{:S(2)}, u32[]{:S(2)}) collective-permute-start(bf16[256,2048]{1,0:T(8,128)(2,1)} %get-tuple-element.96), channel_id=1, source_target_pairs={{0,96},{32,0},{64,32},{96,64},{1,97},{33,1},{65,33},{97,65},{2,98}... | collective-permute-start | bytes 3145736 | tf_op jit(solution)/shard_map/ppermute | solution.py:25
  137.9 48.5 %collective-permute-start.17 = (bf16[256,2048]{1,0:T(8,128)(2,1)}, bf16[256,2048]{1,0:T(8,128)(2,1)}, u32[]{:S(2)}, u32[]{:S(2)}) collective-permute-start(bf16[256,2048]{1,0:T(8,128)(2,1)} %get-tuple-element.97), channel_id=1, source_target_pairs={{0,32},{32,64},{64,96},{96,0},{1,33},{33,65},{65,97},{97,1},{2,34}... | collective-permute-start | bytes 3145736 | tf_op jit(solution)/shard_map/ppermute | solution.py:25
  179.6 31.8 %collective-permute-start.22 = (bf16[256,2048]{1,0:T(8,128)(2,1)}, bf16[256,2048]{1,0:T(8,128)(2,1)}, u32[]{:S(2)}, u32[]{:S(2)}) collective-permute-start(bf16[256,2048]{1,0:T(8,128)(2,1)} %constant_dynamic-slice_fusion), channel_id=1, source_target_pairs={{0,64},{32,96},{64,0},{96,32},{1,65},{33,97},{65,1},{97,33},{2,66}... | collective-permute-start | bytes 3145736 | tf_op jit(solution)/shard_map/ppermute | solution.py:25
  180.5 30.4 %all-to-all-start.4 = ((bf16[4,64,896]{2,1,0:T(8,128)(2,1)}), bf16[4,64,896]{2,1,0:T(8,128)(2,1)}, u32[]{:S(2)}, u32[]{:S(2)}) async-start(bf16[4,64,896]{2,1,0:T(8,128)(2,1)} %copy-done.12), calls=%async_computation.4 | async-start | bytes 917504 | tf_op jit(solution)/shard_map/all_to_all | solution.py:44
  186.3 31.9 %collective-permute-start.23 = (bf16[256,2048]{1,0:T(8,128)(2,1)}, bf16[256,2048]{1,0:T(8,128)(2,1)}, u32[]{:S(2)}, u32[]{:S(2)}) collective-permute-start(bf16[256,2048]{1,0:T(8,128)(2,1)} %get-tuple-element.95), channel_id=1, source_target_pairs={{0,1},{1,0},{2,3},{3,2},{4,5},{5,4},{6,7},{7,6},{8,9},{9,8},{10,11... | collective-permute-start | bytes 3145736 | tf_op jit(solution)/shard_map/ppermute | solution.py:29
  210.8 8.7 %collective-permute-start.24 = (bf16[256,2048]{1,0:T(8,128)(2,1)}, bf16[256,2048]{1,0:T(8,128)(2,1)S(1)}, u32[]{:S(2)}, u32[]{:S(2)}) collective-permute-start(bf16[256,2048]{1,0:T(8,128)(2,1)} %collective-permute-done.17), channel_id=1, source_target_pairs={{0,1},{1,0},{2,3},{3,2},{4,5},{5,4},{6,7},{7,6},{8,9},{9,8},{10,11... | collective-permute-start | bytes 3145736 | tf_op jit(solution)/shard_map/ppermute | solution.py:29
  210.8 8.7 %collective-permute-start.26 = (bf16[256,2048]{1,0:T(8,128)(2,1)}, bf16[256,2048]{1,0:T(8,128)(2,1)S(1)}, u32[]{:S(2)}, u32[]{:S(2)}) collective-permute-start(bf16[256,2048]{1,0:T(8,128)(2,1)} %collective-permute-done.18), channel_id=1, source_target_pairs={{0,1},{1,0},{2,3},{3,2},{4,5},{5,4},{6,7},{7,6},{8,9},{9,8},{10,11... | collective-permute-start | bytes 3145736 | tf_op jit(solution)/shard_map/ppermute | solution.py:29
  211.4 8.1 %collective-permute-start.25 = (bf16[256,2048]{1,0:T(8,128)(2,1)}, bf16[256,2048]{1,0:T(8,128)(2,1)S(1)}, u32[]{:S(2)}, u32[]{:S(2)}) collective-permute-start(bf16[256,2048]{1,0:T(8,128)(2,1)} %collective-permute-done.22), channel_id=1, source_target_pairs={{0,1},{1,0},{2,3},{3,2},{4,5},{5,4},{6,7},{7,6},{8,9},{9,8},{10,11... | collective-permute-start | bytes 3145736 | tf_op jit(solution)/shard_map/ppermute | solution.py:29
  214.8 8.0 %collective-permute-start.21 = (bf16[64,512]{1,0:T(8,128)(2,1)S(1)}, bf16[64,512]{1,0:T(8,128)(2,1)S(1)}, u32[]{:S(2)}, u32[]{:S(2)}) collective-permute-start(bf16[64,512]{1,0:T(8,128)(2,1)S(1)} %attend.4.first), channel_id=1, source_target_pairs={{0,96},{32,0},{64,32},{96,64},{1,97},{33,1},{65,33},{97,65},{2,98}... | collective-permute-start | bytes 196616 | tf_op jit(solution)/shard_map/ppermute | solution.py:25
  218.2 6.2 %collective-permute-start.20 = (bf16[64,512]{1,0:T(8,128)(2,1)S(1)}, bf16[64,512]{1,0:T(8,128)(2,1)S(1)}, u32[]{:S(2)}, u32[]{:S(2)}) collective-permute-start(bf16[64,512]{1,0:T(8,128)(2,1)S(1)} %attend.4.first), channel_id=1, source_target_pairs={{0,64},{32,96},{64,0},{96,32},{1,65},{33,97},{65,1},{97,33},{2,66}... | collective-permute-start | bytes 196616 | tf_op jit(solution)/shard_map/ppermute | solution.py:25
  219.5 5.9 %collective-permute-start.19 = (bf16[64,512]{1,0:T(8,128)(2,1)S(1)}, bf16[64,512]{1,0:T(8,128)(2,1)S(1)}, u32[]{:S(2)}, u32[]{:S(2)}) collective-permute-start(bf16[64,512]{1,0:T(8,128)(2,1)S(1)} %attend.4.first), channel_id=1, source_target_pairs={{0,32},{32,64},{64,96},{96,0},{1,33},{33,65},{65,97},{97,1},{2,34}... | collective-permute-start | bytes 196616 | tf_op jit(solution)/shard_map/ppermute | solution.py:25
  (37 other events, 533.1 us)
